TPU v7x, 512 devices: a whole 4x4x16 slice. The times are simulated.
512 devices in a mesh: ctx: 16 (over z), ch: 32 (over x, y, core).
Axes of the slice: x: 4, y: 4, z: 16, core: 2. Of those that a mesh axis runs over, the one named last changes fastest.
Arguments:
- projected: bfloat16 [3, 8192, 4096], P(None, 'ctx', 'ch'), may hold values from -6 to 6
- conv_weight: float32 [3, 7, 4096], P(None, None, 'ch'), may hold values from -2 to 2
- residues: float32 [256, 16], P('ch'), may hold values from -0.26 to 0.26
- decay_rates: float32 [256, 16], P('ch'), may hold values from 5.6152344e-05 to 0.0333333333
- grad_out: bfloat16 [8192, 4096], P('ctx', 'ch'), may hold values from -0.9722718 to 0.9722718
Outputs:
- grad_projected: bfloat16 [3, 8192, 4096], P(None, 'ctx', 'ch')
- grad_conv: float32 [3, 7, 4096], P(None, None, 'ch')
- grad_residues: float32 [256, 16], P('ch')
- grad_log_rates: float32 [256, 16], P('ch')
All inputs are finite; a program needn't handle non-finite values.
Results may differ from a plain program's by a relative error of at most 0.0017.
Values may be sent and summed in bfloat16 or wider, within the bound.
No kernel may reach another device: no remote copies, remote signals or barrier semaphores. Data moves between devices by JAX's collectives and lax.ppermute only.
A program may use at most 64 MiB of HBM per device.

v0:
```python
import jax
import jax.numpy as jnp
from jax import lax
from jax.sharding import PartitionSpec as P

D = 4096
G = 256
MODES = 16
KW = 7


TOP_PRECISION = lax.Precision.HIGHEST


def from_behind(value, axis, steps):
    count = lax.axis_size(axis)
    initial, last = (max(0, -steps), min(count, count - steps))
    return lax.ppermute(value, axis, [(source, source + steps) for source in range(initial, last)])


def carried_in(value, axis, join, neutral, backward):
    count, mine = (lax.axis_size(axis), lax.axis_index(axis))
    pieces = jax.tree.map(lambda part: lax.all_gather(part, axis), value)
    if backward:
        pieces = jax.tree.map(lambda part: part[::-1], pieces)
        mine = count - 1 - mine
    subtotal = jax.tree.map(
        lambda part, zero: jnp.full_like(part, 0) + jnp.asarray(zero, part.dtype), value, neutral
    )

    def hop(position, subtotal):
        longer = join(subtotal, jax.tree.map(lambda part: part[position], pieces))
        return jax.tree.map(lambda new, old: jnp.where(position < mine, new, old), longer, subtotal)

    return lax.fori_loop(0, count - 1, hop, subtotal)


def toeplitz_rows(filter_kernel):
    side_length = filter_kernel.shape[0]
    extended = jnp.concatenate(
        [filter_kernel[::-1], jnp.zeros((side_length,), filter_kernel.dtype)]
    )
    flattened = jnp.tile(extended, side_length)[: side_length * (2 * side_length - 1)]
    return flattened.reshape(side_length, 2 * side_length - 1)[:, side_length - 1 :]


def diagonal_sums(matrix):
    side_length = matrix.shape[0]
    padded = jnp.concatenate([matrix[:, ::-1], jnp.zeros_like(matrix)], axis=1)
    flattened = padded.reshape(-1)[: side_length * (2 * side_length - 1)]
    return jnp.sum(
        flattened.reshape(side_length, 2 * side_length - 1)[:, side_length - 1 :], axis=0
    )


def forward_combine(first_part, second_part):
    decay_a, length_a, state_a, moment_a = first_part
    decay_b, length_b, state_b, moment_b = second_part
    return (
        decay_a * decay_b,
        length_a + length_b,
        decay_b[..., None] * state_a + state_b,
        decay_b[..., None] * (length_b * state_a + moment_a) + moment_b,
    )


def reverse_combine(first_part, second_part):
    return (
        first_part[0] * second_part[0],
        second_part[0][..., None] * first_part[1] + second_part[1],
    )


def shards(projected, conv_weight, residues, decay_rates, grad_out):
    row_count, channels = grad_out.shape
    groups, mode_count = residues.shape
    group_width = channels // groups
    tap_count = conv_weight.shape[1]
    margin = tap_count - 1
    block_rows = min(512, row_count)
    blocks = row_count // block_rows
    before = from_behind(projected[:, row_count - margin :, :], "ctx", 1)
    widened = jnp.concatenate([before, projected], axis=1).astype(jnp.float32)
    feature = conv_weight[:, 0, None, :] * widened[:, margin:, :]
    for offset in range(1, tap_count):
        feature = (
            feature
            + conv_weight[:, offset, None, :]
            * widened[:, margin - offset : margin - offset + row_count, :]
        )
    queries, keyed, valued = (feature[0], feature[1], feature[2])
    signal = grad_out.astype(jnp.float32)
    gated_input = keyed * valued
    grad_long = signal * queries
    gated_block_list = gated_input.reshape(blocks, block_rows, groups, group_width)
    long_block_list = grad_long.reshape(blocks, block_rows, groups, group_width)
    lag_offsets = jnp.arange(block_rows, dtype=jnp.float32)
    one_step = jnp.exp(-decay_rates)
    ascending_powers = jnp.exp(-decay_rates[:, :, None] * lag_offsets)
    descending_powers = ascending_powers[:, :, ::-1]
    lagged_signal = ascending_powers * one_step[:, :, None]
    step_decay = jnp.exp(-decay_rates * block_rows)
    final_state = jnp.einsum(
        "zot,ptzh->pzoh", descending_powers, gated_block_list, precision=TOP_PRECISION
    )
    end_moment = jnp.einsum(
        "zot,ptzh->pzoh",
        descending_powers * lag_offsets[::-1],
        gated_block_list,
        precision=TOP_PRECISION,
    )
    initial_state = jnp.einsum(
        "zot,ptzh->pzoh", ascending_powers, long_block_list, precision=TOP_PRECISION
    )
    weighted = jnp.einsum(
        "zot,ptzh->pzoh",
        lagged_signal * (lag_offsets + 1.0),
        long_block_list,
        precision=TOP_PRECISION,
    )
    zero_state = jnp.zeros((groups, mode_count, group_width), jnp.float32)
    carry_state = zero_state
    carry_moment = zero_state
    index_block = 0
    prefix_state = [carry_state]
    prefix_moment = [carry_moment]
    carry_moment = step_decay[..., None] * (block_rows * carry_state) + end_moment[index_block]
    carry_state = step_decay[..., None] * carry_state + final_state[index_block]
    suffix_state = [zero_state] * blocks
    carry_back = zero_state
    for index_block in reversed(range(blocks)):
        suffix_state[index_block] = carry_back
        carry_back = step_decay[..., None] * carry_back + initial_state[index_block]
    device_decay = jnp.exp(-decay_rates * row_count)
    span_rows = jnp.full((), row_count, jnp.float32)
    unit_decay = jnp.ones_like(device_decay)
    scanned = carried_in(
        (device_decay, span_rows, carry_state, carry_moment),
        "ctx",
        forward_combine,
        (unit_decay, jnp.zeros((), jnp.float32), zero_state, zero_state),
        False,
    )
    incoming = scanned[2]
    incoming_moment = scanned[3]
    reversed_scan = carried_in(
        (device_decay, carry_back), "ctx", reverse_combine, (unit_decay, zero_state), True
    )
    incoming_back = reversed_scan[1]
    starts = jnp.arange(blocks, dtype=jnp.float32) * block_rows
    lead_decay = jnp.exp(-decay_rates[None] * starts[:, None, None])
    state_in = lead_decay[..., None] * incoming[None] + jnp.stack(prefix_state)
    moment_in = lead_decay[..., None] * (
        starts[:, None, None, None] * incoming[None] + incoming_moment[None]
    ) + jnp.stack(prefix_moment)
    back_in = lead_decay[::-1][..., None] * incoming_back[None] + jnp.stack(suffix_state)
    filter_kernel = jnp.einsum("lt,ltj->lj", residues, ascending_powers, precision=TOP_PRECISION)
    toeplitz = lax.map(toeplitz_rows, filter_kernel)
    long_out = jnp.einsum(
        "gts,nsgc->ntgc", toeplitz, gated_block_list, precision=TOP_PRECISION
    ) + jnp.einsum(
        "gmt,ngmc->ntgc", residues[:, :, None] * lagged_signal, state_in, precision=TOP_PRECISION
    )
    tail_weight = residues[:, :, None] * descending_powers * one_step[:, :, None]
    grad_gated = jnp.einsum(
        "gts,ntgc->nsgc", toeplitz, long_block_list, precision=TOP_PRECISION
    ) + jnp.einsum("gms,ngmc->nsgc", tail_weight, back_in, precision=TOP_PRECISION)
    grad_query = signal * long_out.reshape(row_count, channels)
    grad_gated = grad_gated.reshape(row_count, channels)
    grad_feature = jnp.stack([grad_query, grad_gated * valued, grad_gated * keyed])
    products = jnp.einsum(
        "ntgc,nsgc->gts", long_block_list, gated_block_list, precision=TOP_PRECISION
    )
    lag_grad = lax.map(diagonal_sums, products)
    leading = initial_state * one_step[None, :, :, None]
    residue_part = jnp.einsum(
        "gk,gmk->gm", lag_grad, ascending_powers, precision=TOP_PRECISION
    ) + jnp.sum(leading * state_in, axis=(0, 3))
    moment_part = jnp.einsum(
        "gk,gmk->gm", lag_grad, ascending_powers * lag_offsets, precision=TOP_PRECISION
    ) + jnp.sum(weighted * state_in + leading * moment_in, axis=(0, 3))
    rate_part = -decay_rates * residues * moment_part
    conv_part = jnp.stack(
        [
            jnp.sum(
                grad_feature * widened[:, margin - offset : margin - offset + row_count, :], axis=1
            )
            for offset in range(tap_count)
        ],
        axis=1,
    )
    after_rows = from_behind(grad_feature[:, :margin, :], "ctx", -1)
    trailing = jnp.concatenate([grad_feature, after_rows], axis=1)
    grad_inputs = conv_weight[:, 0, None, :] * trailing[:, :row_count, :]
    for offset in range(1, tap_count):
        grad_inputs = (
            grad_inputs
            + conv_weight[:, offset, None, :] * trailing[:, offset : offset + row_count, :]
        )
    grad_projected = grad_inputs.astype(jnp.bfloat16)
    entry_count = 3 * KW * D + 2 * G * MODES
    conv_total, residue_total, rate_total = lax.psum((conv_part, residue_part, rate_part), "ctx")
    squares = (
        jnp.sum(conv_total * conv_total)
        + jnp.sum(residue_total * residue_total)
        + jnp.sum(rate_total * rate_total)
    )
    total_squares = lax.psum(squares, "ch")
    factor = jnp.minimum(1.0, lax.rsqrt(total_squares / entry_count + 1e-06))
    return (grad_projected, conv_total * factor, residue_total * factor, rate_total * factor)


def solution(mesh):
    in_specs = (
        P(None, "ctx", "ch"),
        P(None, None, "ch"),
        P("ch", None),
        P("ch", None),
        P("ctx", "ch"),
    )
    out_specs = (P(None, "ctx", "ch"), P(None, None, "ch"), P("ch", None), P("ch", None))
    return jax.shard_map(shards, mesh=mesh, in_specs=in_specs, out_specs=out_specs, check_vma=False)
```

profile of v0, /device:TPU:1, one launch (start us, length us, event | category | flops | bytes accessed | tf_op | source)
XLA Modules:
  0.0 549.7 jit_solution(7592030483017279546)
XLA Ops:
  1.5 4.4 collective-permute-start
  11.6 50.6 %while.50 = (s32[]{:T(128)}, f32[8,512,512]{2,1,0:T(8,128)}, f32[8,512]{1,0:T(8,128)S(1)}, s32[]{:T(128)}, f32[]{:T(128)}) while((s32[]{:T(128)}, f32[8,512,512]{2,1,0:T(8,128)}, f32[8,512]{1,0:T(8,128)S(1)}, s32[]{:T(128)}, f32[]{:T(128)}) %tuple.136), condition=%wide.region_1.2_spmd, body=%wide.region_0.1_spmd.sunk | while | flops 2 | bytes 12597329 | solution.py:158
  12.4 2.8 reshape.110
  18.7 2.8 reshape.110
  25.1 2.8 reshape.110
  31.4 2.8 reshape.110
  37.7 2.8 reshape.110
  44.0 2.8 reshape.110
  50.4 2.8 reshape.110
  56.7 2.8 reshape.110
  62.7 26.9 %all-gather = f32[128,16]{1,0:T(8,128)S(1)} all-gather(f32[8,16]{1,0:T(8,128)S(1)} %get-tuple-element.425), channel_id=2, replica_groups=mesh['ctx'=16,'ch'=32] {'ctx'}, dimensions={0}, use_global_device_ids=true | all-gather | bytes 8704 | tf_op jit(solution)/shard_map/all_gather | solution.py:23
  92.3 21.3 %all-reduce.2 = f32[16]{0:T(128)} all-reduce(f32[16]{0:T(128)S(1)} %dynamic-update-slice), channel_id=1, replica_groups=mesh['ctx'=16,'ch'=32] {'ctx'}, use_global_device_ids=true, to_apply=%add.2 | all-reduce | flops 16 | bytes 128
  117.3 4.1 fusion.54
  121.5 27.9 %all_gather.28 = f32[16,8,16,16]{3,2,1,0:T(8,128)S(1)} all-gather(f32[1,8,16,16]{3,2,1,0:T(8,128)S(1)} %copy.57), channel_id=1, replica_groups=mesh['ctx'=16,'ch'=32] {'ctx'}, dimensions={0}, use_global_device_ids=true | all-gather | bytes 139264 | tf_op jit(solution)/shard_map/all_gather | solution.py:23
  150.6 14.6 %while.53 = (s32[]{:T(128)}, f32[8,16,16]{2,1,0:T(8,128)S(1)}, s32[]{:T(128)}, f32[16,8,16]{2,1,0:T(8,128)S(1)}, f32[16,8,16,16]{3,2,1,0:T(8,128)}, /*index=5*/s32[]{:T(128)}, s32[]{:T(128)}) while((s32[]{:T(128)}, f32[8,16,16]{2,1,0:T(8,128)S(1)}, s32[]{:T(128)}, f32[16,8,16]{2,1,0:T(8,128)S(1)}, f32[16,8,16,16]{3,2,1,0:T(8,128)}, ...), condition=%wide.region_5.6_spmd.clone, body=%wide.region_4.5_spmd.clone.sunk | while | flops 8196 | bytes 26225 | solution.py:35
  167.7 9.9 %fusion.53 = f32[8,16,512]{2,1,0:T(8,128)} fusion(f32[512,8,16]{0,2,1:T(8,128)S(1)} %bitcast.182, f32[8,512,512]{2,1,0:T(8,128)} %get-tuple-element.272), kind=kOutput, calls=%fused_computation.122 | convolution fusion | flops 402653184 | bytes 8912896 | tf_op jit(solution)/shard_map/gts,nsgc->ntgc/dot_general | solution.py:159
  178.6 8.9 %fusion.55 = f32[8,512,512]{2,1,0:T(8,128)} fusion(f32[512,8,16]{0,2,1:T(8,128)S(1)} %bitcast.188, f32[512,8,16]{0,2,1:T(8,128)S(1)} %bitcast.184), kind=kOutput, calls=%fused_computation.124 | convolution fusion | flops 402653184 | bytes 8912896 | tf_op jit(solution)/shard_map/ntgc,nsgc->gts/dot_general | solution.py:171
  187.6 75.0 %while.51 = (s32[]{:T(128)}, f32[8,512]{1,0:T(8,128)}, f32[8,512,512]{2,1,0:T(8,128)}, s32[]{:T(128)}, s32[]{:T(128)}) while((s32[]{:T(128)}, f32[8,512]{1,0:T(8,128)}, f32[8,512,512]{2,1,0:T(8,128)}, s32[]{:T(128)}, s32[]{:T(128)}) %tuple.132), condition=%wide.region_17.18_spmd, body=%wide.region_15.17_spmd.sunk | while | flops 261634 | bytes 16779340 | solution.py:174
  191.1 2.8 reshape.111
  200.5 2.8 reshape.111
  209.9 2.8 reshape.111
  219.2 2.8 reshape.111
  228.6 2.8 reshape.111
  238.0 2.8 reshape.111
  247.4 2.8 reshape.111
  256.8 2.8 reshape.111
  267.1 24.6 %all_gather.25 = f32[16,8,16,16]{3,2,1,0:T(8,128)S(1)} all-gather(f32[1,8,16,16]{3,2,1,0:T(8,128)S(1)} %copy.54), channel_id=1, replica_groups=mesh['ctx'=16,'ch'=32] {'ctx'}, dimensions={0}, use_global_device_ids=true | all-gather | bytes 139264 | tf_op jit(solution)/shard_map/all_gather | solution.py:23
  293.2 30.3 %all_gather.27 = f32[16,8,16,16]{3,2,1,0:T(8,128)} all-gather(f32[1,8,16,16]{3,2,1,0:T(8,128)S(1)} %copy.55), channel_id=1, replica_groups=mesh['ctx'=16,'ch'=32] {'ctx'}, dimensions={0}, use_global_device_ids=true | all-gather | bytes 139264 | tf_op jit(solution)/shard_map/all_gather | solution.py:23
  323.5 52.8 %while.52 = (s32[]{:T(128)}, f32[8,16,16]{2,1,0:T(8,128)S(1)}, f32[8,16,16]{2,1,0:T(8,128)S(1)}, s32[]{:T(128)}, f32[16,8,16]{2,1,0:T(8,128)}, /*index=5*/f32[16...) while((s32[]{:T(128)}, f32[8,16,16]{2,1,0:T(8,128)S(1)}, ...), condition=%wide.region_3.4_spmd.clone, body=%wide.region_2.3_spmd.clone.sunk | while | flops 20484 | bytes 50841 | solution.py:35
  382.4 38.8 %all-reduce.3 = (f32[3,7,128]{2,0,1:T(4,128)S(1)}, f32[8,16]{1,0:T(8,128)S(1)}, f32[8,16]{1,0:T(8,128)S(1)}) all-reduce(f32[3,7,128]{2,0,1:T(4,128)S(1)} %constant_dynamic-update-slice_fusion, f32[8,16]{1,0:T(8,128)S(1)} %add.223, f32[8,16]{1,0:T(8,128)S(1)} %add_multiply_fusion), channel_id=1, replica_groups=mesh['ctx'=16,'ch'=32] {'ctx'}, use_global_device_ids=true, to_apply=%region_13.14 | all-reduce | flops 2944 | bytes 23552 | tf_op jit(solution)/shard_map/psum | solution.py:202
  424.9 111.9 %psum.31 = f32[]{:T(128)} all-reduce(f32[]{:T(128)S(6)} %add.230), channel_id=1, replica_groups=mesh['ctx'=16,'ch'=32] {'ch'}, use_global_device_ids=true, to_apply=%region_24.25 | all-reduce | flops 1 | bytes 8 | tf_op jit(solution)/shard_map/psum | solution.py:208
  540.6 5.5 collective-permute-done.1
  (286 shorter events, 184.8 us)
Async XLA Ops:
  1.5 112.1 %collective-permute-start = (bf16[3,6,128]{1,2,0:T(8,128)(2,1)S(1)}, bf16[3,6,128]{1,2,0:T(8,128)(2,1)S(1)}, u32[]{:S(2)}, u32[]{:S(2)}) collective-permute-start(bf16[3,6,128]{1,2,0:T(8,128)(2,1)S(1)} %copy.52), channel_id=1, source_target_pairs={{0,32},{32,64},{64,96},{96,128},{128,160},{160,192},{192,224},{224... | collective-permute-start | bytes 13832 | tf_op jit(solution)/shard_map/ppermute | solution.py:18
  8.7 107.0 %copy-start.7 = (bf16[512,128]{0,1:T(8,128)(2,1)}, bf16[512,128]{0,1:T(8,128)(2,1)S(1)}, u32[]{:S(2)}) copy-start(bf16[512,128]{0,1:T(8,128)(2,1)S(1)} %copy.51) | copy-start | bytes 393220
  9.7 104.2 %copy-start.11 = (f32[3,1,128]{2,0,1:T(4,128)}, f32[3,1,128]{2,0,1:T(4,128)S(1)}, u32[]{:S(2)}) copy-start(f32[3,1,128]{2,0,1:T(4,128)S(1)} %copy.90) | copy-start | bytes 4612
  62.6 115.1 %copy-start.5 = (f32[8,16,512]{2,1,0:T(8,128)}, f32[8,16,512]{2,1,0:T(8,128)S(1)}, u32[]{:S(2)}) copy-start(f32[8,16,512]{2,1,0:T(8,128)S(1)} %rev.18) | copy-start | bytes 786436
  62.6 58.8 %copy-start.12 = (f32[3,128]{1,0:T(4,128)}, f32[3,128]{1,0:T(4,128)S(1)}, u32[]{:S(2)}) copy-start(f32[3,128]{1,0:T(4,128)S(1)} %get-tuple-element.429) | copy-start | bytes 4612
  62.6 58.8 %copy-start.13 = (f32[3,128]{1,0:T(4,128)}, f32[3,128]{1,0:T(4,128)S(1)}, u32[]{:S(2)}) copy-start(f32[3,128]{1,0:T(4,128)S(1)} %get-tuple-element.430) | copy-start | bytes 4612
  62.6 58.8 %copy-start.14 = (f32[3,128]{1,0:T(4,128)}, f32[3,128]{1,0:T(4,128)S(1)}, u32[]{:S(2)}) copy-start(f32[3,128]{1,0:T(4,128)S(1)} %get-tuple-element.431) | copy-start | bytes 4612
  62.6 58.8 %copy-start.15 = (f32[3,128]{1,0:T(4,128)}, f32[3,128]{1,0:T(4,128)S(1)}, u32[]{:S(2)}) copy-start(f32[3,128]{1,0:T(4,128)S(1)} %get-tuple-element.432) | copy-start | bytes 4612
  62.7 58.8 %copy-start.16 = (f32[3,128]{1,0:T(4,128)}, f32[3,128]{1,0:T(4,128)S(1)}, u32[]{:S(2)}) copy-start(f32[3,128]{1,0:T(4,128)S(1)} %get-tuple-element.433) | copy-start | bytes 4612
  62.7 58.8 %copy-start.17 = (f32[3,128]{1,0:T(4,128)}, f32[3,128]{1,0:T(4,128)S(1)}, u32[]{:S(2)}) copy-start(f32[3,128]{1,0:T(4,128)S(1)} %get-tuple-element.434) | copy-start | bytes 4612
  89.6 31.8 %copy-start.8 = (f32[128,16]{1,0:T(8,128)}, f32[128,16]{1,0:T(8,128)S(1)}, u32[]{:S(2)}) copy-start(f32[128,16]{1,0:T(8,128)S(1)} %all-gather) | copy-start | bytes 24580
  113.6 3.7 copy-start
  115.7 0.9 copy-start.6
  116.6 48.8 %copy-start.9 = (f32[8,16]{1,0:T(8,128)S(1)}, f32[8,16]{1,0:T(8,128)}, u32[]{:S(2)}) copy-start(f32[8,16]{1,0:T(8,128)} %param.15) | copy-start | bytes 1540
  116.6 62.0 %copy-start.3 = (f32[512,128]{0,1:T(8,128)}, f32[512,128]{0,1:T(8,128)S(1)}, u32[]{:S(2)}) copy-start(f32[512,128]{0,1:T(8,128)S(1)} %convert_multiply_fusion) | copy-start | bytes 786436
  262.6 119.1 %copy-start.4 = (f32[512,128]{0,1:T(8,128)S(1)}, f32[512,128]{0,1:T(8,128)}, u32[]{:S(2)}) copy-start(f32[512,128]{0,1:T(8,128)} %copy-done.3) | copy-start | bytes 786436
  262.6 283.5 %copy-start.1 = (f32[1,512,128]{1,2,0:T(8,128)S(1)}, f32[1,512,128]{1,2,0:T(8,128)}, u32[]{:S(2)}) copy-start(f32[1,512,128]{1,2,0:T(8,128)} %get-tuple-element.413) | copy-start | bytes 786436
  262.6 283.5 %copy-start.2 = (f32[1,512,128]{1,2,0:T(8,128)S(1)}, f32[1,512,128]{1,2,0:T(8,128)}, u32[]{:S(2)}) copy-start(f32[1,512,128]{1,2,0:T(8,128)} %get-tuple-element.414) | copy-start | bytes 786436
  293.1 88.6 %copy-start.20 = (f32[8,1,16]{2,1,0:T(1,128)S(1)}, f32[8,1,16]{2,1,0:T(1,128)}, u32[]{:S(2)}) copy-start(f32[8,1,16]{2,1,0:T(1,128)} %fusion.27) | copy-start | bytes 1540
  293.1 88.7 %copy-start.21 = (f32[512]{0:T(512)S(1)}, f32[512]{0:T(512)}, u32[]{:S(2)}) copy-start(f32[512]{0:T(512)} %iota_add_fusion) | copy-start | bytes 6148
  293.1 89.2 %copy-start.10 = (f32[8,16]{1,0:T(8,128)S(1)}, f32[8,16]{1,0:T(8,128)}, u32[]{:S(2)}) copy-start(f32[8,16]{1,0:T(8,128)} %param.15) | copy-start | bytes 1540
  293.1 89.2 %copy-start.18 = (f32[8,16]{1,0:T(8,128)S(1)}, f32[8,16]{1,0:T(8,128)}, u32[]{:S(2)}) copy-start(f32[8,16]{1,0:T(8,128)} %param.16) | copy-start | bytes 1540
  293.1 89.2 %copy-start.19 = (f32[8,1,16]{2,1,0:T(1,128)S(1)}, f32[8,1,16]{2,1,0:T(1,128)}, u32[]{:S(2)}) copy-start(f32[8,1,16]{2,1,0:T(1,128)} %fusion.20) | copy-start | bytes 1540
  538.1 8.0 %collective-permute-start.1 = (f32[3,6,128]{1,2,0:T(8,128)S(1)}, f32[3,6,128]{1,2,0:T(8,128)S(1)}, u32[]{:S(2)}, u32[]{:S(2)}) collective-permute-start(f32[3,6,128]{1,2,0:T(8,128)S(1)} %slice.140), channel_id=1, source_target_pairs={{32,0},{64,32},{96,64},{128,96},{160,128},{192,160},{224,192},{256... | collective-permute-start | bytes 27656 | tf_op jit(solution)/shard_map/ppermute | solution.py:18
where the time goes:
time: 554 us; the launch traced here: 550 us
  blocking collectives  282 us (51%)
  local copies, waits for them, and re-layouts  153 us (28%)
  other arithmetic  65.7 us (12%)
  matrix products  32.8 us (6%)
  starting transfers between devices  5.67 us (1%)
    psum x1, blocking collectives, shards(): total_squares = lax.psum(squares, 'ch')  112 us
    all_gather x4, blocking collectives, carried_in(): pieces = jax.tree.map(lambda part: lax.all_gather(part, axis), value)  110 us
    psum x1, blocking collectives, shards(): lax.psum((conv_part, residue_part, rate_part), 'ctx')  38.8 us
    select_n x30, other arithmetic, hop(): jnp.where(position < mine, new, old)  37.5 us
    reshape x8, local copies, waits for them, and re-layouts, toeplitz_rows(): flattened.reshape(side_length, 2 * side_length - 1)[:, side_length - 1:]  22.7 us
    reshape x8, local copies, waits for them, and re-layouts, diagonal_sums(): flattened.reshape(side_length, 2 * side_length - 1)[:, side_length - 1:]  22.7 us
    unnamed x1, blocking collectives  21.3 us
    dynamic_update_slice x8, local copies, waits for them, and re-layouts, shards(): toeplitz = lax.map(toeplitz_rows, filter_kernel)  21.2 us
  transfers between devices with their start and end apart: 2, of which 1 were waited for; matrix products, arithmetic and copies ran while one was open for 11% of the time, Pallas kernels for 0%

commit v1 on v0

v1 whole, which is shorter than its diff:
```python
import jax
import jax.numpy as jnp
from jax import lax
from jax.experimental import pallas as pl
from jax.experimental.pallas import tpu as pltpu
from jax.sharding import PartitionSpec as P

D = 4096
G = 256
MODES = 16
KW = 7

ROWS = 512
CHANNELS = 128
GROUPS = 8
WIDTH = 16
CHUNK = 128
CHUNKS = ROWS // CHUNK
LEAD = 16
MARGIN = KW - 1
STATS = 24

F32 = jnp.float32
BF16 = jnp.bfloat16
EXACT = lax.Precision.HIGHEST
MM = (((1,), (0,)), ((), ()))
NT = (((1,), (1,)), ((), ()))


def split(value):
    high = value.astype(BF16)
    low = (value - high.astype(F32)).astype(BF16)
    return high, low


def dot3(left, right, dims=MM):
    lh, ll = left
    rh, rl = right

    def product(a, b):
        return lax.dot_general(a, b, dims, preferred_element_type=F32)

    return product(lh, rh) + (product(lh, rl) + product(ll, rh))


def iota(shape, axis):
    return lax.broadcasted_iota(jnp.int32, shape, axis)


def lane_group(rows):
    return (iota((rows, CHANNELS), 1) // WIDTH == iota((rows, CHANNELS), 0)).astype(F32)


def mode_row(table):
    pick = (iota((MODES, CHANNELS), 1) % MODES == iota((MODES, CHANNELS), 0)).astype(F32)
    spread = lax.dot_general(table, pick, MM, precision=EXACT, preferred_element_type=F32)
    return jnp.sum(spread * lane_group(GROUPS), axis=0, keepdims=True)


def mode_column(row):
    eye = iota((CHANNELS, CHANNELS), 0) == iota((CHANNELS, CHANNELS), 1)
    return jnp.sum(jnp.where(eye, row, 0.0), axis=1, keepdims=True)


def mode_compact(table):
    return lax.dot_general(
        table, lane_group(GROUPS), (((0,), (0,)), ((), ())), precision=EXACT, preferred_element_type=F32
    )


def compact(full):
    lanes = full.shape[1]
    total = None
    for g in range(GROUPS):
        own = (iota((MODES, lanes), 1) % CHANNELS) // WIDTH == g
        part = jnp.where(own, full[g * MODES : (g + 1) * MODES, :], 0.0)
        total = part if total is None else total + part
    return total


def expand(small):
    lanes = small.shape[1]
    own = (iota((CHANNELS, lanes), 0) // MODES == (iota((CHANNELS, lanes), 1) % CHANNELS) // WIDTH).astype(F32)
    return split(jnp.concatenate([small] * GROUPS, axis=0) * own)


def side_by_side(value):
    return jnp.concatenate([value[q * CHUNK : (q + 1) * CHUNK, :] for q in range(CHUNKS)], axis=1)


def chunk_lanes(value, q):
    return value[:, q * CHANNELS : (q + 1) * CHANNELS]


def first_kernel(me_ref, proj_ref, before_ref, weight_ref, rate_ref, out_grad_ref,
                 ext_ref, kv_ref, gi_ref, gl_ref, states_ref, send_ref):
    me = me_ref[0]
    for i in range(3):
        ext_ref[i, 0:LEAD, :] = before_ref[i].astype(F32)
        ext_ref[i, LEAD:, :] = proj_ref[i].astype(F32)
    for q in range(CHUNKS):
        feature = []
        for i in range(3):
            total = None
            for j in range(KW):
                term = weight_ref[i, j : j + 1, :] * ext_ref[i, pl.ds(LEAD - j + q * CHUNK, CHUNK), :]
                total = term if total is None else total + term
            feature.append(total)
        rows = pl.ds(q * CHUNK, CHUNK)
        kv_ref[0, rows, :] = feature[1]
        kv_ref[1, rows, :] = feature[2]
        gi_ref[:, q * CHANNELS : (q + 1) * CHANNELS] = feature[1] * feature[2]
        gl_ref[:, q * CHANNELS : (q + 1) * CHANNELS] = out_grad_ref[rows, :].astype(F32) * feature[0]
    rates = rate_ref[...]
    column = mode_column(mode_row(rates))
    lag = iota((CHANNELS, CHUNK), 1).astype(F32)
    ascending = jnp.exp(-column * lag)
    descending = jnp.exp(-column * (CHUNK - 1 - lag))
    small_rates = mode_compact(rates)
    one_step = jnp.exp(-small_rates)
    chunk_decay = jnp.exp(-small_rates * CHUNK)
    ends = compact(dot3(split(descending), split(gi_ref[...])))
    leads = compact(dot3(split(ascending), split(gl_ref[...])))
    state = jnp.zeros((MODES, CHANNELS), F32)
    for q in range(CHUNKS):
        part = chunk_lanes(ends, q)
        states_ref[0, :, q * CHANNELS : (q + 1) * CHANNELS] = part
        state = chunk_decay * state + part
    back = jnp.zeros((MODES, CHANNELS), F32)
    for q in reversed(range(CHUNKS)):
        part = one_step * chunk_lanes(leads, q)
        states_ref[1, :, q * CHANNELS : (q + 1) * CHANNELS] = part
        back = chunk_decay * back + part
    for d in range(send_ref.shape[0]):
        send_ref[d] = jnp.where(d > me, state, back)


def middle_kernel(rate_ref, residue_ref, gi_ref, gl_ref, states_ref,
                  long_ref, gated_ref, local_ref, small_ref, lag_ref):
    rates = rate_ref[...]
    row = mode_row(rates)
    column = mode_column(row)
    lag = iota((CHANNELS, CHUNK), 1)
    back_lag = lax.rem(CHUNK - lag, CHUNK)
    ascending = jnp.exp(-column * lag.astype(F32))
    descending = jnp.exp(-column * (CHUNK - 1 - lag).astype(F32))
    turned = jnp.exp(-column * back_lag.astype(F32))
    residue_row = mode_row(residue_ref[...]) * lane_group(GROUPS)
    filters = lax.dot_general(residue_row, ascending, MM, precision=EXACT, preferred_element_type=F32)
    turned_filters = lax.dot_general(residue_row, turned, MM, precision=EXACT, preferred_element_type=F32)
    gi = split(gi_ref[...])
    gl = split(gl_ref[...])
    down = iota((CHUNK, CHUNK), 0)
    across = iota((CHUNK, CHUNK), 1)
    mirror = (down + across == CHUNK - 1).astype(F32).astype(BF16)
    mirrored = [
        lax.dot_general(mirror, part, MM, preferred_element_type=F32).astype(BF16) for part in gl
    ]
    wide_group = (iota((1, ROWS), 1) % CHANNELS) // WIDTH
    lane_of = iota((CHUNK, CHANNELS), 1) // WIDTH
    for g in range(GROUPS):
        straight = jnp.broadcast_to(turned_filters[g : g + 1, :], (CHUNK, CHUNK))
        straight = pltpu.roll(straight, 0, 1, stride=1, stride_axis=0)
        straight = split(jnp.where(across <= down, straight, 0.0))
        flipped = jnp.broadcast_to(filters[g : g + 1, :], (CHUNK, CHUNK))
        flipped = pltpu.roll(flipped, 0, 1, stride=1, stride_axis=0)
        flipped = split(jnp.where(across >= down, flipped, 0.0))
        forward = dot3(straight, gi)
        backward = dot3(flipped, gl)
        for q in range(CHUNKS):
            rows = pl.ds(q * CHUNK, CHUNK)
            if g == 0:
                long_ref[rows, :] = chunk_lanes(forward, q)
                gated_ref[rows, :] = chunk_lanes(backward, q)
            else:
                long_ref[rows, :] = jnp.where(lane_of == g, chunk_lanes(forward, q), long_ref[rows, :])
                gated_ref[rows, :] = jnp.where(lane_of == g, chunk_lanes(backward, q), gated_ref[rows, :])
        own = (wide_group == g).astype(F32).astype(BF16)
        products = dot3((mirrored[0] * own, mirrored[1] * own), gi, NT)
        products = jnp.where(across + down <= CHUNK - 1, products, 0.0)
        sheared = pltpu.roll(products, 1, 1, stride=1, stride_axis=0)
        lag_ref[g : g + 1, :] = jnp.sum(sheared, axis=0, keepdims=True)
    lag_grad = lag_ref[...]
    down_lag = lax.rem(CHUNK - down, CHUNK).astype(F32)
    powers = jnp.exp(-row * down_lag)
    residue_sums = lax.dot_general(lag_grad, powers, MM, precision=EXACT, preferred_element_type=F32)
    moment_sums = lax.dot_general(lag_grad, powers * down_lag, MM, precision=EXACT, preferred_element_type=F32)
    own_group = lane_group(GROUPS)
    local_ref[...] = jnp.zeros(local_ref.shape, F32)
    local_ref[0:1, :] = jnp.sum(residue_sums * own_group, axis=0, keepdims=True)
    local_ref[1:2, :] = jnp.sum(moment_sums * own_group, axis=0, keepdims=True)
    small_rates = mode_compact(rates)
    chunk_decay = jnp.exp(-small_rates * CHUNK)
    lag_value = lag.astype(F32)
    end_moments = compact(dot3(split(descending * (CHUNK - 1 - lag_value)), gi))
    lead_moments = compact(dot3(split(ascending * (jnp.exp(-column) * (lag_value + 1.0))), gl))
    zero = jnp.zeros((MODES, CHANNELS), F32)
    state, moment = zero, zero
    residue_part, moment_part, lead_moment = zero, zero, zero
    offset_decay = jnp.ones((MODES, CHANNELS), F32)
    for q in range(CHUNKS):
        lead = chunk_lanes(states_ref[1], q)
        end = chunk_lanes(states_ref[0], q)
        lead_here = chunk_lanes(lead_moments, q)
        small_ref[0, :, q * CHANNELS : (q + 1) * CHANNELS] = state
        residue_part = residue_part + lead * state
        moment_part = moment_part + lead_here * state + lead * moment
        lead_moment = lead_moment + offset_decay * (lead_here + float(q * CHUNK) * lead)
        offset_decay = offset_decay * chunk_decay
        moment = chunk_decay * (moment + float(CHUNK) * state) + chunk_lanes(end_moments, q)
        state = chunk_decay * state + end
    back = zero
    for q in reversed(range(CHUNKS)):
        small_ref[1, :, q * CHANNELS : (q + 1) * CHANNELS] = back
        back = chunk_decay * back + chunk_lanes(states_ref[1], q)
    for at, value in enumerate((residue_part, moment_part, lead_moment, moment)):
        small_ref[2, :, at * CHANNELS : (at + 1) * CHANNELS] = value
    small_ref[3, :, 0:CHANNELS] = back


def finish_kernel(me_ref, arrived_ref, rate_ref, residue_ref, small_ref, local_ref, long_ref, gated_ref,
                  kv_ref, out_grad_ref, ext_ref, feature_ref, stats_ref):
    me = me_ref[0]
    rates = rate_ref[...]
    residues = residue_ref[...]
    row = mode_row(rates)
    small_rates = mode_compact(rates)
    small_residues = mode_compact(residues)
    chunk_decay = jnp.exp(-small_rates * CHUNK)
    zero = jnp.zeros((MODES, CHANNELS), F32)
    state_in, late_in, back_in = zero, zero, zero
    for d in range(arrived_ref.shape[0]):
        away = (jnp.abs(me - d) - 1).astype(F32) * float(ROWS)
        term = jnp.exp(-small_rates * away) * arrived_ref[d]
        state_in = state_in + jnp.where(d < me, term, 0.0)
        late_in = late_in + jnp.where(d < me, term * away, 0.0)
        back_in = back_in + jnp.where(d > me, term, 0.0)
    states, backs = [], []
    carried = state_in
    for q in range(CHUNKS):
        states.append(small_residues * (chunk_lanes(small_ref[0], q) + carried))
        carried = carried * chunk_decay
    carried = back_in
    for q in reversed(range(CHUNKS)):
        backs.insert(0, small_residues * (chunk_lanes(small_ref[1], q) + carried))
        carried = carried * chunk_decay
    down = iota((CHUNK, CHANNELS), 0).astype(F32)
    long_far = dot3(split(jnp.exp(-row * (down + 1.0))), expand(jnp.concatenate(states, axis=1)))
    gated_far = dot3(split(jnp.exp(-row * (CHUNK - 1 - down))), expand(jnp.concatenate(backs, axis=1)))
    sums = [jnp.zeros((8, CHANNELS), F32) for _ in range(3 * KW)]
    for q in range(CHUNKS):
        rows = pl.ds(q * CHUNK, CHUNK)
        signal = out_grad_ref[rows, :].astype(F32)
        grad_gated = gated_ref[rows, :] + chunk_lanes(gated_far, q)
        parts = (
            signal * (long_ref[rows, :] + chunk_lanes(long_far, q)),
            grad_gated * kv_ref[1, rows, :],
            grad_gated * kv_ref[0, rows, :],
        )
        for i in range(3):
            feature_ref[i, rows, :] = parts[i]
            for j in range(KW):
                product = parts[i] * ext_ref[i, pl.ds(LEAD - j + q * CHUNK, CHUNK), :]
                sums[i * KW + j] = sums[i * KW + j] + jnp.sum(
                    product.reshape(CHUNK // 8, 8, CHANNELS), axis=0
                )
    residue_part, moment_part, lead_moment, end_moment = (
        chunk_lanes(small_ref[2], at) for at in range(4)
    )
    lead = small_ref[3, :, 0:CHANNELS]
    residue_part = residue_part + lead * state_in
    moment_part = moment_part + lead_moment * state_in + lead * late_in + end_moment * back_in
    same = (iota((CHANNELS, CHANNELS), 0) // WIDTH == iota((CHANNELS, CHANNELS), 1) // MODES).astype(F32)
    pick = (iota((MODES, CHANNELS), 1) % MODES == iota((MODES, CHANNELS), 0)).astype(F32)

    def by_mode(part):
        spread = lax.dot_general(part, same, MM, precision=EXACT, preferred_element_type=F32)
        return jnp.sum(spread * pick, axis=0, keepdims=True)

    residue_row = local_ref[0:1, :] + by_mode(residue_part)
    moment_row = local_ref[1:2, :] + by_mode(moment_part)
    rate_row = -row * mode_row(residues) * moment_row
    lines = [jnp.sum(part, axis=0, keepdims=True) for part in sums]
    stats = jnp.concatenate(lines + [residue_row, rate_row, jnp.zeros((1, CHANNELS), F32)], axis=0)
    for d in range(stats_ref.shape[0]):
        stats_ref[d] = stats


def inputs_kernel(feature_ref, after_ref, weight_ref, out_ref, ext_ref):
    for i in range(3):
        ext_ref[0:ROWS, :] = feature_ref[i]
        ext_ref[ROWS:, :] = after_ref[i]
        for q in range(CHUNKS):
            total = None
            for j in range(KW):
                term = weight_ref[i, j : j + 1, :] * ext_ref[pl.ds(j + q * CHUNK, CHUNK), :]
                total = term if total is None else total + term
            out_ref[i, pl.ds(q * CHUNK, CHUNK), :] = total.astype(BF16)


def total_kernel(stats_ref, total_ref, square_ref):
    total = jnp.sum(stats_ref[...], axis=0)
    total_ref[...] = total
    square = jnp.sum(total * total, axis=0, keepdims=True)
    for d in range(square_ref.shape[0]):
        square_ref[d] = jnp.broadcast_to(square, square_ref.shape[1:])


def scale_kernel(square_ref, total_ref, conv_ref, residue_ref, rate_ref):
    squares = jnp.sum(jnp.sum(square_ref[:, 0, :], axis=0, keepdims=True), axis=1, keepdims=True)
    factor = jnp.minimum(1.0, lax.rsqrt(squares / (3 * KW * D + 2 * G * MODES) + 1e-6))
    total = total_ref[...] * factor
    for i in range(3):
        conv_ref[i] = total[i * KW : (i + 1) * KW, :]
    pick = (iota((MODES, CHANNELS), 1) % MODES == iota((MODES, CHANNELS), 0)).astype(F32)
    own = lane_group(GROUPS)
    at = 3 * KW
    residue_ref[...] = lax.dot_general(
        total[at : at + 1, :] * own, pick, NT, precision=EXACT, preferred_element_type=F32
    )
    rate_ref[...] = lax.dot_general(
        total[at + 1 : at + 2, :] * own, pick, NT, precision=EXACT, preferred_element_type=F32
    )


def shape(*dims, dtype=F32):
    return jax.ShapeDtypeStruct(dims, dtype)


VMEM = pl.BlockSpec(memory_space=pltpu.VMEM)
SMEM = pl.BlockSpec(memory_space=pltpu.SMEM)


def call(kernel, name, out_shape, scalars, inputs, cost_us, scratch=()):
    return pl.pallas_call(
        kernel,
        out_shape=out_shape,
        in_specs=[SMEM] * scalars + [VMEM] * (inputs - scalars),
        out_specs=jax.tree.map(lambda _: VMEM, out_shape),
        scratch_shapes=list(scratch),
        compiler_params=pltpu.CompilerParams(vmem_limit_bytes=24 * 2**20),
        cost_estimate=pl.CostEstimate(
            flops=int(cost_us * 1e9), bytes_accessed=int(cost_us * 3e6), transcendentals=0
        ),
        name=name,
    )


def shards(projected, conv_weight, residues, decay_rates, grad_out):
    ctx = lax.axis_size("ctx")
    planes = lax.axis_size("ch")
    me = lax.axis_index("ctx").astype(jnp.int32).reshape(1)
    before = lax.ppermute(
        projected[:, ROWS - LEAD :, :], "ctx", [(source, source + 1) for source in range(ctx - 1)]
    )
    rows = shape(ROWS, CHANNELS)
    wide = shape(CHUNK, CHUNKS * CHANNELS)
    ext, kv, gi, gl, states, send = call(
        first_kernel, "features",
        (shape(3, LEAD + ROWS, CHANNELS), shape(2, ROWS, CHANNELS), wide, wide,
         shape(2, MODES, CHUNKS * CHANNELS), shape(ctx, MODES, CHANNELS)),
        1, 6, 3,
    )(me, projected, before, conv_weight, decay_rates, grad_out)
    arrived = lax.all_to_all(send, "ctx", 0, 0)
    long_near, gated_near, local, small = call(
        middle_kernel, "within",
        (rows, rows, shape(8, CHANNELS), shape(4, MODES, CHUNKS * CHANNELS)),
        0, 5, 8,
        scratch=[pltpu.VMEM((GROUPS, CHANNELS), F32)],
    )(decay_rates, residues, gi, gl, states)
    grad_feature, stats = call(
        finish_kernel, "across",
        (shape(3, ROWS, CHANNELS), shape(ctx, STATS, CHANNELS)),
        1, 11, 4,
    )(me, arrived, decay_rates, residues, small, local, long_near, gated_near, kv, grad_out, ext)
    after = lax.ppermute(
        grad_feature[:, :8, :], "ctx", [(source + 1, source) for source in range(ctx - 1)]
    )
    gathered = lax.all_to_all(stats, "ctx", 0, 0)
    grad_projected = call(
        inputs_kernel, "inputs", shape(3, ROWS, CHANNELS, dtype=BF16), 0, 3, 2,
        scratch=[pltpu.VMEM((ROWS + 8, CHANNELS), F32)],
    )(grad_feature, after, conv_weight)
    total, square = call(
        total_kernel, "total", (shape(STATS, CHANNELS), shape(planes, 8, CHANNELS)), 0, 1, 1,
    )(gathered)
    squares = lax.all_to_all(square, "ch", 0, 0)
    grad_conv, grad_residues, grad_log_rates = call(
        scale_kernel, "scale",
        (shape(3, KW, CHANNELS), shape(GROUPS, MODES), shape(GROUPS, MODES)), 0, 2, 1,
    )(squares, total)
    return grad_projected, grad_conv, grad_residues, grad_log_rates


def solution(mesh):
    in_specs = (
        P(None, "ctx", "ch"),
        P(None, None, "ch"),
        P("ch", None),
        P("ch", None),
        P("ctx", "ch"),
    )
    out_specs = (P(None, "ctx", "ch"), P(None, None, "ch"), P("ch", None), P("ch", None))
    return jax.shard_map(shards, mesh=mesh, in_specs=in_specs, out_specs=out_specs, check_vma=False)
```

time: 554 us -> 79.8 us (0.14)
  blocking collectives: 282 us -> 0 us
  local copies, waits for them, and re-layouts: 153 us -> 3.33 us
  other arithmetic: 65.7 us -> 0 us
  starting transfers between devices: 5.67 us -> 39.4 us
  matrix products: 32.8 us -> 0 us
  waiting for transfers between devices: 5.5 us -> 25.7 us
  Pallas kernels: 0 us -> 10.2 us
    psum x2 -> x0, blocking collectives: 151 us -> none  [the longest x1 112 us: shards(): total_squares = lax.psum(squares, 'ch')]
    all_gather x4 -> x0, blocking collectives: 110 us -> none  [carried_in(): pieces = jax.tree.map(lambda part: lax.all_gather(part, axis), value)]
    reshape x16 -> x0, local copies, waits for them, and re-layouts: 45.4 us -> none  [the longest x8 22.7 us: toeplitz_rows(): flattened.reshape(side_length, 2 * side_length - 1)[:, side_length - 1:]]
    select_n x30 -> x0, other arithmetic: 37.5 us -> none  [hop(): jnp.where(position < mine, new, old)]
    all_to_all x0 -> x3, starting transfers between devices: none -> 33.8 us  [the longest x1 16.2 us: shards(): arrived = lax.all_to_all(send, 'ctx', 0, 0)]
    dot_general x12 -> x0, matrix products: 32.8 us -> none  [the longest x1 9.9 us: shards(): jnp.einsum('gts,nsgc->ntgc', toeplitz, gated_block_list, precision=TOP_PR...]
    dynamic_update_slice x16 -> x0, local copies, waits for them, and re-layouts: 31.9 us -> none  [the longest x8 21.2 us: shards(): toeplitz = lax.map(toeplitz_rows, filter_kernel)]
    all_to_all x0 -> x3, waiting for transfers between devices: none -> 24.9 us  [the longest x1 11 us: shards(): gathered = lax.all_to_all(stats, 'ctx', 0, 0)]
  transfers between devices with their start and end apart: 2 -> 5, of which waited for: 1 -> 4; matrix products, arithmetic and copies ran while one was open for 11% -> 0% of each run, Pallas kernels for 0% -> 7%
where the time goes in v1:
time: 79.8 us; the launch traced here: 79.3 us
  starting transfers between devices  39.4 us (49%)
  waiting for transfers between devices  25.7 us (32%)
  Pallas kernels  10.2 us (13%)
  local copies, waits for them, and re-layouts  3.33 us (4%)
    all_to_all x1, starting transfers between devices, shards(): arrived = lax.all_to_all(send, 'ctx', 0, 0)  16.2 us
    all_to_all x1, starting transfers between devices, shards(): squares = lax.all_to_all(square, 'ch', 0, 0)  12.6 us
    all_to_all x1, waiting for transfers between devices, shards(): gathered = lax.all_to_all(stats, 'ctx', 0, 0)  11 us
    all_to_all x1, waiting for transfers between devices, shards(): arrived = lax.all_to_all(send, 'ctx', 0, 0)  7.34 us
    all_to_all x1, waiting for transfers between devices, shards(): squares = lax.all_to_all(square, 'ch', 0, 0)  6.49 us
    all_to_all x1, starting transfers between devices, shards(): gathered = lax.all_to_all(stats, 'ctx', 0, 0)  5 us
    ppermute x1, starting transfers between devices, shards(): lax.ppermute(projected[:, ROWS - LEAD:, :], 'ctx', [(source, source + 1)...  4.36 us
    pallas_call x1, Pallas kernels, shards(): call(middle_kernel, 'within', (rows, rows, shape(8, CHANNELS), shape(4, M...  3.94 us
  transfers between devices with their start and end apart: 5, of which 4 were waited for; matrix products, arithmetic and copies ran while one was open for 0% of the time, Pallas kernels for 7%

profile of v1, /device:TPU:1, one launch (start us, length us, event | category | flops | bytes accessed | tf_op | source)
XLA Modules:
  0.0 79.3 jit_solution(17551988954426837172)
XLA Ops:
  0.6 0.0 copy-start.3
  0.6 0.7 slice.6
  1.4 4.4 %collective-permute-start = (bf16[3,16,128]{2,1,0:T(8,128)(2,1)S(1)}, bf16[3,16,128]{2,1,0:T(8,128)(2,1)S(1)}, u32[]{:S(2)}, u32[]{:S(2)}) collective-permute-start(bf16[3,16,128]{2,1,0:T(8,128)(2,1)S(1)} %slice.6), channel_id=1, source_target_pairs={{0,32},{32,64},{64,96},{96,128},{128,160},{160,192},{192,224},{224... | collective-permute-start | bytes 36872 | tf_op jit(solution)/shard_map/ppermute | solution.py:353
  5.7 0.0 copy-start.4
  5.8 0.8 %collective-permute-done.before_ref = bf16[3,16,128]{2,1,0:T(8,128)(2,1)S(1)} collective-permute-done((bf16[3,16,128]{2,1,0:T(8,128)(2,1)S(1)}, bf16[3,16,128]{2,1,0:T(8,128)(2,1)S(1)}, u32[]{:S(2)}, u32[]{:S(2)}) %collective-permute-start) | collective-permute-done | bytes 12320 | tf_op jit(solution)/shard_map/ppermute | solution.py:353
  6.6 0.0 copy-done.3
  6.6 0.0 copy-done.4
  6.6 0.0 copy-start
  6.6 1.0 %copy-done = bf16[3,512,128]{2,1,0:T(8,128)(2,1)S(1)} copy-done((bf16[3,512,128]{2,1,0:T(8,128)(2,1)S(1)}, bf16[3,512,128]{2,1,0:T(8,128)(2,1)}, u32[]{:S(2)}) %copy-start) | copy-done | bytes 393240
  7.6 0.0 copy-start.1
  7.6 0.9 %copy-done.1 = bf16[512,128]{1,0:T(8,128)(2,1)S(1)} copy-done((bf16[512,128]{1,0:T(8,128)(2,1)S(1)}, bf16[512,128]{1,0:T(8,128)(2,1)}, u32[]{:S(2)}) %copy-start.1) | copy-done | bytes 131096
  8.5 1.6 %features.1 = (f32[3,528,128]{2,1,0:T(8,128)S(1)}, f32[2,512,128]{2,1,0:T(8,128)S(1)}, f32[128,512]{1,0:T(8,128)S(1)}, f32[128,512]{1,0:T(8,128)S(1)}, f32[2,16,...) custom-call(s32[1]{0:T(128)} %bitcast.me_ref, bf16[3,512,128]{2,1,0:T(8,128)(2,1)S(1)} %copy-done, ...), custom_call_target="tpu_custom_call" | custom-call | flops 3000000000 | bytes 9000000 | tf_op jit(solution)/shard_map/features/pallas_call | solution.py:358
  10.1 16.2 %all-to-all-start = ((f32[16,16,128]{2,1,0:T(8,128)}), f32[16,16,128]{2,1,0:T(8,128)S(1)}, u32[]{:S(2)}, u32[]{:S(2)}) async-start(f32[16,16,128]{2,1,0:T(8,128)} %get-tuple-element.21), calls=%async_computation | async-start | bytes 262144 | tf_op jit(solution)/shard_map/all_to_all | solution.py:364
  26.3 0.0 copy-start.5
  26.3 0.7 copy-done.5
  27.0 0.0 copy-start.2
  27.0 3.9 %within.1 = (f32[512,128]{1,0:T(8,128)S(1)}, f32[512,128]{1,0:T(8,128)S(1)}, f32[8,128]{1,0:T(8,128)S(1)}, f32[4,16,512]{2,1,0:T(8,128)S(1)}) custom-call(f32[8,16]{1,0:T(8,128)S(1)} %copy-done.4, f32[8,16]{1,0:T(8,128)S(1)} %copy-done.5, f32[128,512]{1,0:T(8,128)S(1)} %get-tuple-element.22.gi_ref, f32[128,512]{1,0:T(8,128)S(1)} %get-tuple-element.23.gl_ref, ...), custom_call_target="tpu_custom_call" | custom-call | flops 8000000000 | bytes 24000000 | tf_op jit(solution)/shard_map/within/pallas_call | solution.py:365
  30.9 7.3 %all-to-all-done.arrived_ref = f32[16,16,128]{2,1,0:T(8,128)S(1)} async-done(((f32[16,16,128]{2,1,0:T(8,128)}), f32[16,16,128]{2,1,0:T(8,128)S(1)}, u32[]{:S(2)}, u32[]{:S(2)}) %all-to-all-start) | async-done | bytes 131104 | tf_op jit(solution)/shard_map/all_to_all | solution.py:364
  38.3 0.0 copy-done.2
  38.3 1.9 %across.1 = (f32[3,512,128]{2,1,0:T(8,128)S(1)}, f32[16,24,128]{2,1,0:T(8,128)}) custom-call(s32[1]{0:T(128)} %bitcast.me_ref, f32[16,16,128]{2,1,0:T(8,128)S(1)} %all-to-all-done.arrived_ref, f32[8,16]{1,0:T(8,128)S(1)} %copy-done.4, f32[8,16]{1,0:T(8,128)S(1)} %copy-done.5, f32[4,16,512]{2,1,0:T(8,128)S(1)} %get-tuple-element.25.small_ref, ...), custom_call_target="tpu_custom_call" | custom-call | flops 4000000000 | bytes 12000000 | tf_op jit(solution)/shard_map/across/pallas_call | solution.py:371
  40.2 5.0 %all-to-all-start.1 = ((f32[16,24,128]{2,1,0:T(8,128)}), f32[16,24,128]{2,1,0:T(8,128)S(1)}, u32[]{:S(2)}, u32[]{:S(2)}) async-start(f32[16,24,128]{2,1,0:T(8,128)} %get-tuple-element.32), calls=%async_computation.1 | async-start | bytes 393216 | tf_op jit(solution)/shard_map/all_to_all | solution.py:379
  45.2 1.3 %collective-permute-start.1 = (f32[3,8,128]{2,1,0:T(8,128)S(1)}, f32[3,8,128]{2,1,0:T(8,128)S(1)}, u32[]{:S(2)}, u32[]{:S(2)}) collective-permute-start(f32[3,8,128]{2,1,0:T(8,128)S(1)} %slice.7), channel_id=1, source_target_pairs={{32,0},{64,32},{96,64},{128,96},{160,128},{192,160},{224,192},{256... | collective-permute-start | bytes 36872 | tf_op jit(solution)/shard_map/ppermute | solution.py:376
  46.5 11.0 %all-to-all-done.1.stats_ref = f32[16,24,128]{2,1,0:T(8,128)S(1)} async-done(((f32[16,24,128]{2,1,0:T(8,128)}), f32[16,24,128]{2,1,0:T(8,128)S(1)}, u32[]{:S(2)}, u32[]{:S(2)}) %all-to-all-start.1) | async-done | bytes 196640 | tf_op jit(solution)/shard_map/all_to_all | solution.py:379
  57.5 0.7 total.1
  58.2 12.6 %all-to-all-start.2 = ((f32[32,8,128]{2,1,0:T(8,128)}), f32[32,8,128]{2,1,0:T(8,128)S(1)}, u32[]{:S(2)}, u32[]{:S(2)}) async-start(f32[32,8,128]{2,1,0:T(8,128)} %get-tuple-element.33), calls=%async_computation.2 | async-start | bytes 262144 | tf_op jit(solution)/shard_map/all_to_all | solution.py:387
  70.8 0.0 collective-permute-done.1.after_ref
  70.8 1.2 %inputs.1 = bf16[3,512,128]{2,1,0:T(8,128)(2,1)} custom-call(f32[3,512,128]{2,1,0:T(8,128)S(1)} %get-tuple-element.31.feature_ref, f32[3,8,128]{2,1,0:T(8,128)S(1)} %collective-permute-done.1.after_ref, f32[3,7,128]{2,1,0:T(8,128)S(1)} %copy-done.3), custom_call_target="tpu_custom_call" | custom-call | flops 2000000000 | bytes 6000000 | tf_op jit(solution)/shard_map/inputs/pallas_call | solution.py:380
  72.0 6.5 %all-to-all-done.2.square_ref = f32[32,8,128]{2,1,0:T(8,128)S(1)} async-done(((f32[32,8,128]{2,1,0:T(8,128)}), f32[32,8,128]{2,1,0:T(8,128)S(1)}, u32[]{:S(2)}, u32[]{:S(2)}) %all-to-all-start.2) | async-done | bytes 131104 | tf_op jit(solution)/shard_map/all_to_all | solution.py:387
  78.5 0.8 %scale.1 = (f32[3,7,128]{2,1,0:T(8,128)}, f32[8,16]{1,0:T(8,128)}, f32[8,16]{1,0:T(8,128)}) custom-call(f32[32,8,128]{2,1,0:T(8,128)S(1)} %all-to-all-done.2.square_ref, f32[24,128]{1,0:T(8,128)S(1)} %get-tuple-element.34.total_ref), custom_call_target="tpu_custom_call" | custom-call | flops 1000000000 | bytes 3000000 | tf_op jit(solution)/shard_map/scale/pallas_call | solution.py:388
  (1 shorter events, 0.0 us)
Async XLA Ops:
  0.6 5.9 %copy-start.3 = (f32[3,7,128]{2,1,0:T(8,128)S(1)}, f32[3,7,128]{2,1,0:T(8,128)}, u32[]{:S(2)}) copy-start(f32[3,7,128]{2,1,0:T(8,128)} %weight_ref.3) | copy-start | bytes 32260
  1.4 5.2 %collective-permute-start = (bf16[3,16,128]{2,1,0:T(8,128)(2,1)S(1)}, bf16[3,16,128]{2,1,0:T(8,128)(2,1)S(1)}, u32[]{:S(2)}, u32[]{:S(2)}) collective-permute-start(bf16[3,16,128]{2,1,0:T(8,128)(2,1)S(1)} %slice.6), channel_id=1, source_target_pairs={{0,32},{32,64},{64,96},{96,128},{128,160},{160,192},{192,224},{224... | collective-permute-start | bytes 36872 | tf_op jit(solution)/shard_map/ppermute | solution.py:353
  5.7 0.8 %copy-start.4 = (f32[8,16]{1,0:T(8,128)S(1)}, f32[8,16]{1,0:T(8,128)}, u32[]{:S(2)}) copy-start(f32[8,16]{1,0:T(8,128)} %rate_ref.5) | copy-start | bytes 1540
  6.6 1.0 %copy-start = (bf16[3,512,128]{2,1,0:T(8,128)(2,1)S(1)}, bf16[3,512,128]{2,1,0:T(8,128)(2,1)}, u32[]{:S(2)}) copy-start(bf16[3,512,128]{2,1,0:T(8,128)(2,1)} %proj_ref.1) | copy-start | bytes 1179652
  7.6 0.9 %copy-start.1 = (bf16[512,128]{1,0:T(8,128)(2,1)S(1)}, bf16[512,128]{1,0:T(8,128)(2,1)}, u32[]{:S(2)}) copy-start(bf16[512,128]{1,0:T(8,128)(2,1)} %out_grad_ref.3) | copy-start | bytes 393220
  10.1 28.2 %all-to-all-start = ((f32[16,16,128]{2,1,0:T(8,128)}), f32[16,16,128]{2,1,0:T(8,128)S(1)}, u32[]{:S(2)}, u32[]{:S(2)}) async-start(f32[16,16,128]{2,1,0:T(8,128)} %get-tuple-element.21), calls=%async_computation | async-start | bytes 262144 | tf_op jit(solution)/shard_map/all_to_all | solution.py:364
  26.3 0.7 copy-start.5
  27.0 11.3 %copy-start.2 = (bf16[512,128]{1,0:T(8,128)(2,1)S(1)}, bf16[512,128]{1,0:T(8,128)(2,1)}, u32[]{:S(2)}) copy-start(bf16[512,128]{1,0:T(8,128)(2,1)} %out_grad_ref.3) | copy-start | bytes 393220
  40.2 17.4 %all-to-all-start.1 = ((f32[16,24,128]{2,1,0:T(8,128)}), f32[16,24,128]{2,1,0:T(8,128)S(1)}, u32[]{:S(2)}, u32[]{:S(2)}) async-start(f32[16,24,128]{2,1,0:T(8,128)} %get-tuple-element.32), calls=%async_computation.1 | async-start | bytes 393216 | tf_op jit(solution)/shard_map/all_to_all | solution.py:379
  45.2 25.6 %collective-permute-start.1 = (f32[3,8,128]{2,1,0:T(8,128)S(1)}, f32[3,8,128]{2,1,0:T(8,128)S(1)}, u32[]{:S(2)}, u32[]{:S(2)}) collective-permute-start(f32[3,8,128]{2,1,0:T(8,128)S(1)} %slice.7), channel_id=1, source_target_pairs={{32,0},{64,32},{96,64},{128,96},{160,128},{192,160},{224,192},{256... | collective-permute-start | bytes 36872 | tf_op jit(solution)/shard_map/ppermute | solution.py:376
  58.2 20.3 %all-to-all-start.2 = ((f32[32,8,128]{2,1,0:T(8,128)}), f32[32,8,128]{2,1,0:T(8,128)S(1)}, u32[]{:S(2)}, u32[]{:S(2)}) async-start(f32[32,8,128]{2,1,0:T(8,128)} %get-tuple-element.33), calls=%async_computation.2 | async-start | bytes 262144 | tf_op jit(solution)/shard_map/all_to_all | solution.py:387

commit v2 on v1

--- a/solution.py
+++ b/solution.py
@@ -17,8 +17,9 @@
 CHUNK = 128
 CHUNKS = ROWS // CHUNK
 LEAD = 16
-MARGIN = KW - 1
+HEAD = 8
 STATS = 24
+LOCAL = (2 * CHUNKS + 5) * MODES
 
 F32 = jnp.float32
 BF16 = jnp.bfloat16
@@ -84,20 +85,50 @@
     return split(jnp.concatenate([small] * GROUPS, axis=0) * own)
 
 
-def side_by_side(value):
-    return jnp.concatenate([value[q * CHUNK : (q + 1) * CHUNK, :] for q in range(CHUNKS)], axis=1)
+def near_parts(near_ref):
+    return near_ref.at[0:ROWS, :], near_ref.at[ROWS : 2 * ROWS, :], near_ref.at[2 * ROWS :, :]
+
+
+def piece(at):
+    return slice(at * MODES, (at + 1) * MODES)
 
 
 def chunk_lanes(value, q):
     return value[:, q * CHANNELS : (q + 1) * CHANNELS]
 
 
-def first_kernel(me_ref, proj_ref, before_ref, weight_ref, rate_ref, out_grad_ref,
-                 ext_ref, kv_ref, gi_ref, gl_ref, states_ref, send_ref):
-    me = me_ref[0]
+def prepare_kernel(weight_ref, rate_ref, residue_ref, proj_ref, out_grad_ref,
+                   kv_ref, pair_ref, states_ref, ends_ref, head_ref, power_ref, table_ref,
+                   raw_ref, signal_ref, ext_ref, sem_ref):
+    gi_ref, gl_ref = pair_ref.at[0], pair_ref.at[1]
+    copies = [
+        pltpu.make_async_copy(proj_ref, raw_ref, sem_ref.at[0]),
+        pltpu.make_async_copy(out_grad_ref, signal_ref, sem_ref.at[1]),
+    ]
+    for copy in copies:
+        copy.start()
+    rates = rate_ref[...]
+    table_ref[0] = rates
+    table_ref[1] = residue_ref[...]
+    column = mode_column(mode_row(rates))
+    lag = iota((CHANNELS, CHUNK), 1).astype(F32)
+    ascending = split(jnp.exp(-column * lag))
+    descending = split(jnp.exp(-column * (CHUNK - 1 - lag)))
+    small_rates = mode_compact(rates)
+    one_step = jnp.exp(-small_rates)
+    chunk_decay = jnp.exp(-small_rates * CHUNK)
+    for r in range(HEAD):
+        power_ref[0, r] = jnp.exp(-small_rates * float(CHUNK - 1 - r))
+        power_ref[1, r] = jnp.exp(-small_rates * float(r + 1))
+    power_ref[2, 0] = jnp.exp(-small_rates * float(ROWS - CHUNK))
+    for r in range(1, HEAD):
+        power_ref[2, r] = jnp.zeros((MODES, CHANNELS), F32)
+    for copy in copies:
+        copy.wait()
     for i in range(3):
-        ext_ref[i, 0:LEAD, :] = before_ref[i].astype(F32)
-        ext_ref[i, LEAD:, :] = proj_ref[i].astype(F32)
+        ext_ref[i, 0:LEAD, :] = jnp.zeros((LEAD, CHANNELS), F32)
+        ext_ref[i, LEAD:, :] = raw_ref[i].astype(F32)
+    blank = jnp.zeros((HEAD, CHANNELS), F32)
     for q in range(CHUNKS):
         feature = []
         for i in range(3):
@@ -107,20 +138,20 @@
                 total = term if total is None else total + term
             feature.append(total)
         rows = pl.ds(q * CHUNK, CHUNK)
+        lanes = slice(q * CHANNELS, (q + 1) * CHANNELS)
+        signal = signal_ref[rows, :].astype(F32)
         kv_ref[0, rows, :] = feature[1]
         kv_ref[1, rows, :] = feature[2]
-        gi_ref[:, q * CHANNELS : (q + 1) * CHANNELS] = feature[1] * feature[2]
-        gl_ref[:, q * CHANNELS : (q + 1) * CHANNELS] = out_grad_ref[rows, :].astype(F32) * feature[0]
-    rates = rate_ref[...]
-    column = mode_column(mode_row(rates))
-    lag = iota((CHANNELS, CHUNK), 1).astype(F32)
-    ascending = jnp.exp(-column * lag)
-    descending = jnp.exp(-column * (CHUNK - 1 - lag))
-    small_rates = mode_compact(rates)
-    one_step = jnp.exp(-small_rates)
-    chunk_decay = jnp.exp(-small_rates * CHUNK)
-    ends = compact(dot3(split(descending), split(gi_ref[...])))
-    leads = compact(dot3(split(ascending), split(gl_ref[...])))
+        gi_ref[:, lanes] = feature[1] * feature[2]
+        gl_ref[:, lanes] = signal * feature[0]
+        if q == 0:
+            for i in range(3):
+                head_ref[i] = feature[i][0:HEAD, :]
+            head_ref[3] = signal[0:HEAD, :]
+            gi_ref[0:HEAD, lanes] = blank
+            gl_ref[0:HEAD, lanes] = blank
+    ends = compact(dot3(descending, split(gi_ref[...])))
+    leads = compact(dot3(ascending, split(gl_ref[...])))
     state = jnp.zeros((MODES, CHANNELS), F32)
     for q in range(CHUNKS):
         part = chunk_lanes(ends, q)
@@ -131,13 +162,49 @@
         part = one_step * chunk_lanes(leads, q)
         states_ref[1, :, q * CHANNELS : (q + 1) * CHANNELS] = part
         back = chunk_decay * back + part
+    ends_ref[0] = state
+    ends_ref[1] = back
+
+
+def patch_kernel(me_ref, before_ref, weight_ref, head_ref, power_ref, ends_ref,
+                 patch_ref, delta_ref, send_ref, ext_ref):
+    me = me_ref[0]
+    feature = []
+    for i in range(3):
+        ext_ref[0:LEAD, :] = before_ref[i].astype(F32)
+        ext_ref[LEAD:, :] = jnp.zeros((HEAD, CHANNELS), F32)
+        total = head_ref[i]
+        for j in range(1, KW):
+            total = total + weight_ref[i, j : j + 1, :] * ext_ref[pl.ds(LEAD - j, HEAD), :]
+        feature.append(total)
+    gi = feature[1] * feature[2]
+    gl = head_ref[3] * feature[0]
+    for at, value in enumerate((feature[1], feature[2], gi, gl)):
+        patch_ref[at] = value
+    state_part, back_part = None, None
+    for r in range(HEAD):
+        ahead = power_ref[0, r] * gi[r : r + 1, :]
+        behind = power_ref[1, r] * gl[r : r + 1, :]
+        state_part = ahead if r == 0 else state_part + ahead
+        back_part = behind if r == 0 else back_part + behind
+    delta_ref[0] = state_part
+    delta_ref[1] = back_part
+    state = ends_ref[0] + power_ref[2, 0] * state_part
+    back = ends_ref[1] + back_part
     for d in range(send_ref.shape[0]):
-        send_ref[d] = jnp.where(d > me, state, back)
-
-
-def middle_kernel(rate_ref, residue_ref, gi_ref, gl_ref, states_ref,
-                  long_ref, gated_ref, local_ref, small_ref, lag_ref):
-    rates = rate_ref[...]
+        send_ref[d] = jnp.where(d > me, state, back).astype(send_ref.dtype)
+
+
+def spliced(wide_ref, patch):
+    top = jnp.concatenate([patch, wide_ref[0:HEAD, CHANNELS:]], axis=1)
+    return jnp.concatenate([top, wide_ref[HEAD:, :]], axis=0)
+
+
+def middle_kernel(table_ref, pair_ref, states_ref, patch_ref, delta_ref,
+                  near_ref, lag_ref):
+    long_ref, gated_ref, small_ref = near_parts(near_ref)
+    gi_ref, gl_ref = pair_ref.at[0], pair_ref.at[1]
+    rates = table_ref[0]
     row = mode_row(rates)
     column = mode_column(row)
     lag = iota((CHANNELS, CHUNK), 1)
@@ -145,11 +212,11 @@
     ascending = jnp.exp(-column * lag.astype(F32))
     descending = jnp.exp(-column * (CHUNK - 1 - lag).astype(F32))
     turned = jnp.exp(-column * back_lag.astype(F32))
-    residue_row = mode_row(residue_ref[...]) * lane_group(GROUPS)
+    residue_row = mode_row(table_ref[1]) * lane_group(GROUPS)
     filters = lax.dot_general(residue_row, ascending, MM, precision=EXACT, preferred_element_type=F32)
     turned_filters = lax.dot_general(residue_row, turned, MM, precision=EXACT, preferred_element_type=F32)
-    gi = split(gi_ref[...])
-    gl = split(gl_ref[...])
+    gi = split(spliced(gi_ref, patch_ref[2]))
+    gl = split(spliced(gl_ref, patch_ref[3]))
     down = iota((CHUNK, CHUNK), 0)
     across = iota((CHUNK, CHUNK), 1)
     mirror = (down + across == CHUNK - 1).astype(F32).astype(BF16)
@@ -186,23 +253,26 @@
     residue_sums = lax.dot_general(lag_grad, powers, MM, precision=EXACT, preferred_element_type=F32)
     moment_sums = lax.dot_general(lag_grad, powers * down_lag, MM, precision=EXACT, preferred_element_type=F32)
     own_group = lane_group(GROUPS)
-    local_ref[...] = jnp.zeros(local_ref.shape, F32)
-    local_ref[0:1, :] = jnp.sum(residue_sums * own_group, axis=0, keepdims=True)
-    local_ref[1:2, :] = jnp.sum(moment_sums * own_group, axis=0, keepdims=True)
+    small_ref[LOCAL : LOCAL + 1, :] = jnp.sum(residue_sums * own_group, axis=0, keepdims=True)
+    small_ref[LOCAL + 1 : LOCAL + 2, :] = jnp.sum(moment_sums * own_group, axis=0, keepdims=True)
     small_rates = mode_compact(rates)
     chunk_decay = jnp.exp(-small_rates * CHUNK)
     lag_value = lag.astype(F32)
     end_moments = compact(dot3(split(descending * (CHUNK - 1 - lag_value)), gi))
     lead_moments = compact(dot3(split(ascending * (jnp.exp(-column) * (lag_value + 1.0))), gl))
     zero = jnp.zeros((MODES, CHANNELS), F32)
+    leads = []
     state, moment = zero, zero
     residue_part, moment_part, lead_moment = zero, zero, zero
     offset_decay = jnp.ones((MODES, CHANNELS), F32)
     for q in range(CHUNKS):
         lead = chunk_lanes(states_ref[1], q)
         end = chunk_lanes(states_ref[0], q)
+        if q == 0:
+            end, lead = end + delta_ref[0], lead + delta_ref[1]
+        leads.append(lead)
         lead_here = chunk_lanes(lead_moments, q)
-        small_ref[0, :, q * CHANNELS : (q + 1) * CHANNELS] = state
+        small_ref[piece(q), :] = state
         residue_part = residue_part + lead * state
         moment_part = moment_part + lead_here * state + lead * moment
         lead_moment = lead_moment + offset_decay * (lead_here + float(q * CHUNK) * lead)
@@ -211,18 +281,20 @@
         state = chunk_decay * state + end
     back = zero
     for q in reversed(range(CHUNKS)):
-        small_ref[1, :, q * CHANNELS : (q + 1) * CHANNELS] = back
-        back = chunk_decay * back + chunk_lanes(states_ref[1], q)
-    for at, value in enumerate((residue_part, moment_part, lead_moment, moment)):
-        small_ref[2, :, at * CHANNELS : (at + 1) * CHANNELS] = value
-    small_ref[3, :, 0:CHANNELS] = back
-
-
-def finish_kernel(me_ref, arrived_ref, rate_ref, residue_ref, small_ref, local_ref, long_ref, gated_ref,
-                  kv_ref, out_grad_ref, ext_ref, feature_ref, stats_ref):
+        small_ref[piece(CHUNKS + q), :] = back
+        back = chunk_decay * back + leads[q]
+    for at, value in enumerate((residue_part, moment_part, lead_moment, moment, back)):
+        small_ref[piece(2 * CHUNKS + at), :] = value
+
+
+def finish_kernel(me_ref, arrived_ref, table_ref, near_ref,
+                  kv_ref, patch_ref, out_grad_ref, proj_ref, before_ref, feature_ref, stats_ref, ext_ref):
+    for i in range(3):
+        ext_ref[i, 0:LEAD, :] = before_ref[i].astype(F32)
+        ext_ref[i, LEAD:, :] = proj_ref[i].astype(F32)
+    long_ref, gated_ref, small_ref = near_parts(near_ref)
     me = me_ref[0]
-    rates = rate_ref[...]
-    residues = residue_ref[...]
+    rates, residues = table_ref[0], table_ref[1]
     row = mode_row(rates)
     small_rates = mode_compact(rates)
     small_residues = mode_compact(residues)
@@ -231,18 +303,18 @@
     state_in, late_in, back_in = zero, zero, zero
     for d in range(arrived_ref.shape[0]):
         away = (jnp.abs(me - d) - 1).astype(F32) * float(ROWS)
-        term = jnp.exp(-small_rates * away) * arrived_ref[d]
+        term = jnp.exp(-small_rates * away) * arrived_ref[d].astype(F32)
         state_in = state_in + jnp.where(d < me, term, 0.0)
         late_in = late_in + jnp.where(d < me, term * away, 0.0)
         back_in = back_in + jnp.where(d > me, term, 0.0)
     states, backs = [], []
     carried = state_in
     for q in range(CHUNKS):
-        states.append(small_residues * (chunk_lanes(small_ref[0], q) + carried))
+        states.append(small_residues * (small_ref[piece(q), :] + carried))
         carried = carried * chunk_decay
     carried = back_in
     for q in reversed(range(CHUNKS)):
-        backs.insert(0, small_residues * (chunk_lanes(small_ref[1], q) + carried))
+        backs.insert(0, small_residues * (small_ref[piece(CHUNKS + q), :] + carried))
         carried = carried * chunk_decay
     down = iota((CHUNK, CHANNELS), 0).astype(F32)
     long_far = dot3(split(jnp.exp(-row * (down + 1.0))), expand(jnp.concatenate(states, axis=1)))
@@ -252,10 +324,14 @@
         rows = pl.ds(q * CHUNK, CHUNK)
         signal = out_grad_ref[rows, :].astype(F32)
         grad_gated = gated_ref[rows, :] + chunk_lanes(gated_far, q)
+        keyed, valued = kv_ref[0, rows, :], kv_ref[1, rows, :]
+        if q == 0:
+            keyed = jnp.concatenate([patch_ref[0], keyed[HEAD:, :]], axis=0)
+            valued = jnp.concatenate([patch_ref[1], valued[HEAD:, :]], axis=0)
         parts = (
             signal * (long_ref[rows, :] + chunk_lanes(long_far, q)),
-            grad_gated * kv_ref[1, rows, :],
-            grad_gated * kv_ref[0, rows, :],
+            grad_gated * valued,
+            grad_gated * keyed,
         )
         for i in range(3):
             feature_ref[i, rows, :] = parts[i]
@@ -264,10 +340,9 @@
                 sums[i * KW + j] = sums[i * KW + j] + jnp.sum(
                     product.reshape(CHUNK // 8, 8, CHANNELS), axis=0
                 )
-    residue_part, moment_part, lead_moment, end_moment = (
-        chunk_lanes(small_ref[2], at) for at in range(4)
-    )
-    lead = small_ref[3, :, 0:CHANNELS]
+    residue_part, moment_part, lead_moment, end_moment, lead = (
+        small_ref[piece(2 * CHUNKS + at), :] for at in range(5)
+    )
     residue_part = residue_part + lead * state_in
     moment_part = moment_part + lead_moment * state_in + lead * late_in + end_moment * back_in
     same = (iota((CHANNELS, CHANNELS), 0) // WIDTH == iota((CHANNELS, CHANNELS), 1) // MODES).astype(F32)
@@ -277,8 +352,8 @@
         spread = lax.dot_general(part, same, MM, precision=EXACT, preferred_element_type=F32)
         return jnp.sum(spread * pick, axis=0, keepdims=True)
 
-    residue_row = local_ref[0:1, :] + by_mode(residue_part)
-    moment_row = local_ref[1:2, :] + by_mode(moment_part)
+    residue_row = small_ref[LOCAL : LOCAL + 1, :] + by_mode(residue_part)
+    moment_row = small_ref[LOCAL + 1 : LOCAL + 2, :] + by_mode(moment_part)
     rate_row = -row * mode_row(residues) * moment_row
     lines = [jnp.sum(part, axis=0, keepdims=True) for part in sums]
     stats = jnp.concatenate(lines + [residue_row, rate_row, jnp.zeros((1, CHANNELS), F32)], axis=0)
@@ -331,14 +406,17 @@
 SMEM = pl.BlockSpec(memory_space=pltpu.SMEM)
 
 
-def call(kernel, name, out_shape, scalars, inputs, cost_us, scratch=()):
+HBM = pl.BlockSpec(memory_space=pltpu.HBM)
+
+
+def call(kernel, name, out_shape, specs, cost_us, scratch=()):
     return pl.pallas_call(
         kernel,
         out_shape=out_shape,
-        in_specs=[SMEM] * scalars + [VMEM] * (inputs - scalars),
+        in_specs=specs,
         out_specs=jax.tree.map(lambda _: VMEM, out_shape),
         scratch_shapes=list(scratch),
-        compiler_params=pltpu.CompilerParams(vmem_limit_bytes=24 * 2**20),
+        compiler_params=pltpu.CompilerParams(vmem_limit_bytes=12 * 2**20),
         cost_estimate=pl.CostEstimate(
             flops=int(cost_us * 1e9), bytes_accessed=int(cost_us * 3e6), transcendentals=0
         ),
@@ -353,41 +431,50 @@
     before = lax.ppermute(
         projected[:, ROWS - LEAD :, :], "ctx", [(source, source + 1) for source in range(ctx - 1)]
     )
-    rows = shape(ROWS, CHANNELS)
-    wide = shape(CHUNK, CHUNKS * CHANNELS)
-    ext, kv, gi, gl, states, send = call(
-        first_kernel, "features",
-        (shape(3, LEAD + ROWS, CHANNELS), shape(2, ROWS, CHANNELS), wide, wide,
-         shape(2, MODES, CHUNKS * CHANNELS), shape(ctx, MODES, CHANNELS)),
-        1, 6, 3,
-    )(me, projected, before, conv_weight, decay_rates, grad_out)
+    kv, pair, states, ends, head, powers, table = call(
+        prepare_kernel, "prepare",
+        (shape(2, ROWS, CHANNELS), shape(2, CHUNK, CHUNKS * CHANNELS), shape(2, MODES, CHUNKS * CHANNELS),
+         shape(2, MODES, CHANNELS), shape(4, HEAD, CHANNELS), shape(3, HEAD, MODES, CHANNELS),
+         shape(2, GROUPS, MODES)),
+        [VMEM] * 3 + [HBM] * 2, 3,
+        scratch=[pltpu.VMEM((3, ROWS, CHANNELS), BF16), pltpu.VMEM((ROWS, CHANNELS), BF16),
+                 pltpu.VMEM((3, LEAD + ROWS, CHANNELS), F32), pltpu.SemaphoreType.DMA((2,))],
+    )(conv_weight, decay_rates, residues,
+      *(pltpu.with_memory_space_constraint(part, pltpu.HBM) for part in (projected, grad_out)))
+    patch, delta, send = call(
+        patch_kernel, "patch",
+        (shape(4, HEAD, CHANNELS), shape(2, MODES, CHANNELS), shape(ctx, MODES, CHANNELS)),
+        [SMEM] + [VMEM] * 5, 1,
+        scratch=[pltpu.VMEM((LEAD + HEAD, CHANNELS), F32)],
+    )(me, before, conv_weight, head, powers, ends)
     arrived = lax.all_to_all(send, "ctx", 0, 0)
-    long_near, gated_near, local, small = call(
+    near = call(
         middle_kernel, "within",
-        (rows, rows, shape(8, CHANNELS), shape(4, MODES, CHUNKS * CHANNELS)),
-        0, 5, 8,
+        shape(2 * ROWS + LOCAL + 8, CHANNELS),
+        [VMEM] * 5, 8,
         scratch=[pltpu.VMEM((GROUPS, CHANNELS), F32)],
-    )(decay_rates, residues, gi, gl, states)
+    )(table, pair, states, patch, delta)
     grad_feature, stats = call(
         finish_kernel, "across",
         (shape(3, ROWS, CHANNELS), shape(ctx, STATS, CHANNELS)),
-        1, 11, 4,
-    )(me, arrived, decay_rates, residues, small, local, long_near, gated_near, kv, grad_out, ext)
+        [SMEM] + [VMEM] * 8, 4,
+        scratch=[pltpu.VMEM((3, LEAD + ROWS, CHANNELS), F32)],
+    )(me, arrived, table, near, kv, patch, grad_out, projected, before)
     after = lax.ppermute(
         grad_feature[:, :8, :], "ctx", [(source + 1, source) for source in range(ctx - 1)]
     )
     gathered = lax.all_to_all(stats, "ctx", 0, 0)
     grad_projected = call(
-        inputs_kernel, "inputs", shape(3, ROWS, CHANNELS, dtype=BF16), 0, 3, 2,
+        inputs_kernel, "inputs", shape(3, ROWS, CHANNELS, dtype=BF16), [VMEM] * 3, 2,
         scratch=[pltpu.VMEM((ROWS + 8, CHANNELS), F32)],
     )(grad_feature, after, conv_weight)
     total, square = call(
-        total_kernel, "total", (shape(STATS, CHANNELS), shape(planes, 8, CHANNELS)), 0, 1, 1,
+        total_kernel, "total", (shape(STATS, CHANNELS), shape(planes, 1, CHANNELS)), [VMEM], 1,
     )(gathered)
     squares = lax.all_to_all(square, "ch", 0, 0)
     grad_conv, grad_residues, grad_log_rates = call(
         scale_kernel, "scale",
-        (shape(3, KW, CHANNELS), shape(GROUPS, MODES), shape(GROUPS, MODES)), 0, 2, 1,
+        (shape(3, KW, CHANNELS), shape(GROUPS, MODES), shape(GROUPS, MODES)), [VMEM] * 2, 1,
     )(squares, total)
     return grad_projected, grad_conv, grad_residues, grad_log_rates
 

time: 79.8 us -> 76.2 us (0.955)
  local copies, waits for them, and re-layouts: 3.33 us -> 0.76 us
  starting transfers between devices: 39.4 us -> 38.4 us
  waiting for transfers between devices: 25.7 us -> 24.8 us
  Pallas kernels: 10.2 us -> 11 us
    unnamed x12 -> x10, local copies, waits for them, and re-layouts: 2.6 us -> 0.03 us
    all_to_all x1, starting transfers between devices: 16.2 us -> 15.2 us  [shards(): arrived = lax.all_to_all(send, 'ctx', 0, 0)]
    pallas_call x4 -> x5, Pallas kernels: 7.45 us -> 8.27 us  [the longest x1 3.93 us: shards(): call(middle_kernel, 'within', shape(2 * ROWS + LOCAL + 8, CHANNELS), [VME...]
  transfers between devices with their start and end apart: 5 -> 5, of which waited for: 4 -> 3; matrix products, arithmetic and copies ran while one was open for 0% -> 0% of each run, Pallas kernels for 7% -> 10%
where the time goes in v2:
time: 76.2 us; the launch traced here: 75.7 us
  starting transfers between devices  38.4 us (50%)
  waiting for transfers between devices  24.8 us (33%)
  Pallas kernels  11 us (14%)
  between operations  0.78 us (1%)
    all_to_all x1, starting transfers between devices, shards(): arrived = lax.all_to_all(send, 'ctx', 0, 0)  15.2 us
    all_to_all x1, starting transfers between devices, shards(): squares = lax.all_to_all(square, 'ch', 0, 0)  12.6 us
    all_to_all x1, waiting for transfers between devices, shards(): gathered = lax.all_to_all(stats, 'ctx', 0, 0)  11 us
    all_to_all x1, waiting for transfers between devices, shards(): arrived = lax.all_to_all(send, 'ctx', 0, 0)  8.02 us
    all_to_all x1, waiting for transfers between devices, shards(): squares = lax.all_to_all(square, 'ch', 0, 0)  5.72 us
    all_to_all x1, starting transfers between devices, shards(): gathered = lax.all_to_all(stats, 'ctx', 0, 0)  4.99 us
    ppermute x1, starting transfers between devices, shards(): lax.ppermute(projected[:, ROWS - LEAD:, :], 'ctx', [(source, source + 1)...  4.36 us
    pallas_call x1, Pallas kernels, shards(): call(middle_kernel, 'within', shape(2 * ROWS + LOCAL + 8, CHANNELS), [VME...  3.93 us
  transfers between devices with their start and end apart: 5, of which 3 were waited for; matrix products, arithmetic and copies ran while one was open for 0% of the time, Pallas kernels for 10%

profile of v2, /device:TPU:1, one launch (start us, length us, event | category | flops | bytes accessed | tf_op | source)
XLA Modules:
  0.0 75.7 jit_solution(11073737899240026680)
XLA Ops:
  0.6 0.0 copy-start.2
  0.6 0.0 copy-start.3
  0.7 0.0 copy-start.4
  0.7 0.7 slice.6
  1.4 4.4 %collective-permute-start = (bf16[3,16,128]{2,1,0:T(8,128)(2,1)S(1)}, bf16[3,16,128]{2,1,0:T(8,128)(2,1)S(1)}, u32[]{:S(2)}, u32[]{:S(2)}) collective-permute-start(bf16[3,16,128]{2,1,0:T(8,128)(2,1)S(1)} %slice.6), channel_id=1, source_target_pairs={{0,32},{32,64},{64,96},{96,128},{128,160},{160,192},{192,224},{224... | collective-permute-start | bytes 36872 | tf_op jit(solution)/shard_map/ppermute | solution.py:431
  5.8 0.0 copy-done.2
  5.8 0.0 copy-done.3
  5.8 0.0 copy-done.4
  5.8 1.8 %prepare.1 = (f32[2,512,128]{2,1,0:T(8,128)S(1)}, f32[2,128,512]{2,1,0:T(8,128)S(1)}, f32[2,16,512]{2,1,0:T(8,128)S(1)}, f32[2,16,128]{2,1,0:T(8,128)S(1)}, f32[...) custom-call(f32[3,7,128]{2,1,0:T(8,128)S(1)} %copy-done.2, f32[8,16]{1,0:T(8,128)S(1)} %copy-done.3, ...), custom_call_target="tpu_custom_call" | custom-call | flops 3000000000 | bytes 9000000 | tf_op jit(solution)/shard_map/prepare/pallas_call | solution.py:434
  7.6 0.0 collective-permute-done.before_ref
  7.6 0.7 patch.1
  8.3 15.2 %all-to-all-start = ((f32[16,16,128]{2,1,0:T(8,128)}), f32[16,16,128]{2,1,0:T(8,128)S(1)}, u32[]{:S(2)}, u32[]{:S(2)}) async-start(f32[16,16,128]{2,1,0:T(8,128)} %get-tuple-element.24), calls=%async_computation | async-start | bytes 262144 | tf_op jit(solution)/shard_map/all_to_all | solution.py:450
  23.5 0.0 copy-start
  23.5 0.0 copy-start.1
  23.5 3.9 %within.1.near_ref = f32[1240,128]{1,0:T(8,128)S(1)} custom-call(f32[2,8,16]{2,1,0:T(8,128)S(1)} %get-tuple-element.25.table_ref, f32[2,128,512]{2,1,0:T(8,128)S(1)} %get-tuple-element.26.pair_ref, f32[2,16,512]{2,1,0:T(8,128)S(1)} %get-tuple-element.27.states_ref, f32[4,8,128]{2,1,0:T(8,128)S(1)} %get-tuple-element.28.patch_ref, ...), custom_call_target="tpu_custom_call" | custom-call | flops 8000000000 | bytes 24000000 | tf_op jit(solution)/shard_map/within/pallas_call | solution.py:451
  27.5 8.0 %all-to-all-done.arrived_ref = f32[16,16,128]{2,1,0:T(8,128)S(1)} async-done(((f32[16,16,128]{2,1,0:T(8,128)}), f32[16,16,128]{2,1,0:T(8,128)S(1)}, u32[]{:S(2)}, u32[]{:S(2)}) %all-to-all-start) | async-done | bytes 131104 | tf_op jit(solution)/shard_map/all_to_all | solution.py:450
  35.5 0.0 copy-done
  35.5 0.0 copy-done.1
  35.5 1.9 %across.1 = (f32[3,512,128]{2,1,0:T(8,128)S(1)}, f32[16,24,128]{2,1,0:T(8,128)}) custom-call(s32[1]{0:T(128)} %bitcast.me_ref, f32[16,16,128]{2,1,0:T(8,128)S(1)} %all-to-all-done.arrived_ref, f32[2,8,16]{2,1,0:T(8,128)S(1)} %get-tuple-element.25.table_ref, f32[1240,128]{1,0:T(8,128)S(1)} %within.1.near_ref, f32[2,512,128]{2,1,0:T(8,128)S(1)} %get-tuple-element.30.kv_ref, ...), custom_call_target="tpu_custom_call" | custom-call | flops 4000000000 | bytes 12000000 | tf_op jit(solution)/shard_map/across/pallas_call | solution.py:457
  37.4 5.0 %all-to-all-start.1 = ((f32[16,24,128]{2,1,0:T(8,128)}), f32[16,24,128]{2,1,0:T(8,128)S(1)}, u32[]{:S(2)}, u32[]{:S(2)}) async-start(f32[16,24,128]{2,1,0:T(8,128)} %get-tuple-element.32), calls=%async_computation.1 | async-start | bytes 393216 | tf_op jit(solution)/shard_map/all_to_all | solution.py:466
  42.4 1.3 %collective-permute-start.1 = (f32[3,8,128]{2,1,0:T(8,128)S(1)}, f32[3,8,128]{2,1,0:T(8,128)S(1)}, u32[]{:S(2)}, u32[]{:S(2)}) collective-permute-start(f32[3,8,128]{2,1,0:T(8,128)S(1)} %slice.7), channel_id=1, source_target_pairs={{32,0},{64,32},{96,64},{128,96},{160,128},{192,160},{224,192},{256... | collective-permute-start | bytes 36872 | tf_op jit(solution)/shard_map/ppermute | solution.py:463
  43.7 11.0 %all-to-all-done.1.stats_ref = f32[16,24,128]{2,1,0:T(8,128)S(1)} async-done(((f32[16,24,128]{2,1,0:T(8,128)}), f32[16,24,128]{2,1,0:T(8,128)S(1)}, u32[]{:S(2)}, u32[]{:S(2)}) %all-to-all-start.1) | async-done | bytes 196640 | tf_op jit(solution)/shard_map/all_to_all | solution.py:466
  54.7 0.6 total.1
  55.4 12.6 %all-to-all-start.2 = ((f32[32,1,128]{2,1,0:T(1,128)}), f32[32,1,128]{2,1,0:T(1,128)S(1)}, u32[]{:S(2)}, u32[]{:S(2)}) async-start(f32[32,1,128]{2,1,0:T(1,128)} %get-tuple-element.33), calls=%async_computation.2 | async-start | bytes 32768 | tf_op jit(solution)/shard_map/all_to_all | solution.py:474
  68.0 0.0 collective-permute-done.1.after_ref
  68.0 1.2 %inputs.1 = bf16[3,512,128]{2,1,0:T(8,128)(2,1)} custom-call(f32[3,512,128]{2,1,0:T(8,128)S(1)} %get-tuple-element.31.feature_ref, f32[3,8,128]{2,1,0:T(8,128)S(1)} %collective-permute-done.1.after_ref, f32[3,7,128]{2,1,0:T(8,128)S(1)} %copy-done.2), custom_call_target="tpu_custom_call" | custom-call | flops 2000000000 | bytes 6000000 | tf_op jit(solution)/shard_map/inputs/pallas_call | solution.py:467
  69.2 5.7 %all-to-all-done.2.square_ref = f32[32,1,128]{2,1,0:T(1,128)S(1)} async-done(((f32[32,1,128]{2,1,0:T(1,128)}), f32[32,1,128]{2,1,0:T(1,128)S(1)}, u32[]{:S(2)}, u32[]{:S(2)}) %all-to-all-start.2) | async-done | bytes 16416 | tf_op jit(solution)/shard_map/all_to_all | solution.py:474
  74.9 0.8 %scale.1 = (f32[3,7,128]{2,1,0:T(8,128)}, f32[8,16]{1,0:T(8,128)}, f32[8,16]{1,0:T(8,128)}) custom-call(f32[32,1,128]{2,1,0:T(1,128)S(1)} %all-to-all-done.2.square_ref, f32[24,128]{1,0:T(8,128)S(1)} %get-tuple-element.34.total_ref), custom_call_target="tpu_custom_call" | custom-call | flops 1000000000 | bytes 3000000 | tf_op jit(solution)/shard_map/scale/pallas_call | solution.py:475
  (1 shorter events, 0.0 us)
Async XLA Ops:
  0.6 5.1 %copy-start.2 = (f32[3,7,128]{2,1,0:T(8,128)S(1)}, f32[3,7,128]{2,1,0:T(8,128)}, u32[]{:S(2)}) copy-start(f32[3,7,128]{2,1,0:T(8,128)} %weight_ref.5) | copy-start | bytes 32260
  0.6 5.1 %copy-start.3 = (f32[8,16]{1,0:T(8,128)S(1)}, f32[8,16]{1,0:T(8,128)}, u32[]{:S(2)}) copy-start(f32[8,16]{1,0:T(8,128)} %rate_ref.1) | copy-start | bytes 1540
  0.7 5.1 %copy-start.4 = (f32[8,16]{1,0:T(8,128)S(1)}, f32[8,16]{1,0:T(8,128)}, u32[]{:S(2)}) copy-start(f32[8,16]{1,0:T(8,128)} %residue_ref.1) | copy-start | bytes 1540
  1.4 6.2 %collective-permute-start = (bf16[3,16,128]{2,1,0:T(8,128)(2,1)S(1)}, bf16[3,16,128]{2,1,0:T(8,128)(2,1)S(1)}, u32[]{:S(2)}, u32[]{:S(2)}) collective-permute-start(bf16[3,16,128]{2,1,0:T(8,128)(2,1)S(1)} %slice.6), channel_id=1, source_target_pairs={{0,32},{32,64},{64,96},{96,128},{128,160},{160,192},{192,224},{224... | collective-permute-start | bytes 36872 | tf_op jit(solution)/shard_map/ppermute | solution.py:431
  8.3 27.2 %all-to-all-start = ((f32[16,16,128]{2,1,0:T(8,128)}), f32[16,16,128]{2,1,0:T(8,128)S(1)}, u32[]{:S(2)}, u32[]{:S(2)}) async-start(f32[16,16,128]{2,1,0:T(8,128)} %get-tuple-element.24), calls=%async_computation | async-start | bytes 262144 | tf_op jit(solution)/shard_map/all_to_all | solution.py:450
  23.5 12.0 %copy-start = (bf16[3,512,128]{2,1,0:T(8,128)(2,1)S(1)}, bf16[3,512,128]{2,1,0:T(8,128)(2,1)}, u32[]{:S(2)}) copy-start(bf16[3,512,128]{2,1,0:T(8,128)(2,1)} %proj_ref.3) | copy-start | bytes 1179652
  23.5 12.0 %copy-start.1 = (bf16[512,128]{1,0:T(8,128)(2,1)S(1)}, bf16[512,128]{1,0:T(8,128)(2,1)}, u32[]{:S(2)}) copy-start(bf16[512,128]{1,0:T(8,128)(2,1)} %out_grad_ref.3) | copy-start | bytes 393220
  37.4 17.4 %all-to-all-start.1 = ((f32[16,24,128]{2,1,0:T(8,128)}), f32[16,24,128]{2,1,0:T(8,128)S(1)}, u32[]{:S(2)}, u32[]{:S(2)}) async-start(f32[16,24,128]{2,1,0:T(8,128)} %get-tuple-element.32), calls=%async_computation.1 | async-start | bytes 393216 | tf_op jit(solution)/shard_map/all_to_all | solution.py:466
  42.4 25.6 %collective-permute-start.1 = (f32[3,8,128]{2,1,0:T(8,128)S(1)}, f32[3,8,128]{2,1,0:T(8,128)S(1)}, u32[]{:S(2)}, u32[]{:S(2)}) collective-permute-start(f32[3,8,128]{2,1,0:T(8,128)S(1)} %slice.7), channel_id=1, source_target_pairs={{32,0},{64,32},{96,64},{128,96},{160,128},{192,160},{224,192},{256... | collective-permute-start | bytes 36872 | tf_op jit(solution)/shard_map/ppermute | solution.py:463
  55.4 19.5 %all-to-all-start.2 = ((f32[32,1,128]{2,1,0:T(1,128)}), f32[32,1,128]{2,1,0:T(1,128)S(1)}, u32[]{:S(2)}, u32[]{:S(2)}) async-start(f32[32,1,128]{2,1,0:T(1,128)} %get-tuple-element.33), calls=%async_computation.2 | async-start | bytes 32768 | tf_op jit(solution)/shard_map/all_to_all | solution.py:474

commit v3 on v2

--- a/solution.py
+++ b/solution.py
@@ -23,6 +23,7 @@
 
 F32 = jnp.float32
 BF16 = jnp.bfloat16
+F16 = jnp.float16
 EXACT = lax.Precision.HIGHEST
 MM = (((1,), (0,)), ((), ()))
 NT = (((1,), (1,)), ((), ()))
@@ -357,8 +358,10 @@
     rate_row = -row * mode_row(residues) * moment_row
     lines = [jnp.sum(part, axis=0, keepdims=True) for part in sums]
     stats = jnp.concatenate(lines + [residue_row, rate_row, jnp.zeros((1, CHANNELS), F32)], axis=0)
-    for d in range(stats_ref.shape[0]):
-        stats_ref[d] = stats
+    largest = jnp.max(jnp.abs(stats), axis=0, keepdims=True)
+    exponent = jnp.ceil(jnp.log2(jnp.maximum(largest, 1e-30))) - 15.0
+    last = iota((STATS, CHANNELS), 0) == STATS - 1
+    stats_ref[...] = jnp.where(last, exponent, stats * jnp.exp2(-exponent))
 
 
 def inputs_kernel(feature_ref, after_ref, weight_ref, out_ref, ext_ref):
@@ -374,7 +377,10 @@
 
 
 def total_kernel(stats_ref, total_ref, square_ref):
-    total = jnp.sum(stats_ref[...], axis=0)
+    total = jnp.zeros((STATS, CHANNELS), F32)
+    for d in range(stats_ref.shape[0]):
+        total = total + stats_ref[d] * jnp.exp2(stats_ref[d, STATS - 1 :, :])
+    total = jnp.where(iota((STATS, CHANNELS), 0) == STATS - 1, 0.0, total)
     total_ref[...] = total
     square = jnp.sum(total * total, axis=0, keepdims=True)
     for d in range(square_ref.shape[0]):
@@ -456,14 +462,15 @@
     )(table, pair, states, patch, delta)
     grad_feature, stats = call(
         finish_kernel, "across",
-        (shape(3, ROWS, CHANNELS), shape(ctx, STATS, CHANNELS)),
+        (shape(3, ROWS, CHANNELS), shape(STATS, CHANNELS)),
         [SMEM] + [VMEM] * 8, 4,
         scratch=[pltpu.VMEM((3, LEAD + ROWS, CHANNELS), F32)],
     )(me, arrived, table, near, kv, patch, grad_out, projected, before)
     after = lax.ppermute(
         grad_feature[:, :8, :], "ctx", [(source + 1, source) for source in range(ctx - 1)]
     )
-    gathered = lax.all_to_all(stats, "ctx", 0, 0)
+    stats = jnp.broadcast_to(stats.astype(F16), (ctx, STATS, CHANNELS))
+    gathered = lax.all_to_all(stats, "ctx", 0, 0).astype(F32)
     grad_projected = call(
         inputs_kernel, "inputs", shape(3, ROWS, CHANNELS, dtype=BF16), [VMEM] * 3, 2,
         scratch=[pltpu.VMEM((ROWS + 8, CHANNELS), F32)],

time: 76.2 us -> 74 us (0.971)
  starting transfers between devices: 38.4 us -> 36.8 us
    all_to_all x1, starting transfers between devices: 12.6 us -> 10.9 us  [shards(): squares = lax.all_to_all(square, 'ch', 0, 0)]
where the time goes in v3:
time: 74 us; the launch traced here: 73.6 us
  starting transfers between devices  36.8 us (50%)
  waiting for transfers between devices  24.3 us (33%)
  Pallas kernels  10.3 us (14%)
  local copies, waits for them, and re-layouts  1.43 us (2%)
  between operations  0.79 us (1%)
    all_to_all x1, starting transfers between devices, shards(): arrived = lax.all_to_all(send, 'ctx', 0, 0)  15.2 us
    all_to_all x1, starting transfers between devices, shards(): squares = lax.all_to_all(square, 'ch', 0, 0)  10.9 us
    all_to_all x1, waiting for transfers between devices, shards(): gathered = lax.all_to_all(stats, 'ctx', 0, 0).astype(F32)  10.5 us
    all_to_all x1, waiting for transfers between devices, shards(): arrived = lax.all_to_all(send, 'ctx', 0, 0)  8.02 us
    all_to_all x1, waiting for transfers between devices, shards(): squares = lax.all_to_all(square, 'ch', 0, 0)  5.72 us
    all_to_all x1, starting transfers between devices, shards(): gathered = lax.all_to_all(stats, 'ctx', 0, 0).astype(F32)  4.99 us
    ppermute x1, starting transfers between devices, shards(): lax.ppermute(projected[:, ROWS - LEAD:, :], 'ctx', [(source, source + 1)...  4.36 us
    pallas_call x1, Pallas kernels, shards(): call(middle_kernel, 'within', shape(2 * ROWS + LOCAL + 8, CHANNELS), [VME...  3.93 us
  transfers between devices with their start and end apart: 5, of which 3 were waited for; matrix products, arithmetic and copies ran while one was open for 0% of the time, Pallas kernels for 10%

profile of v3, /device:TPU:1, one launch (start us, length us, event | category | flops | bytes accessed | tf_op | source)
XLA Modules:
  0.0 73.6 jit_solution(14274559305857982544)
XLA Ops:
  0.6 0.0 copy-start.2
  0.6 0.0 copy-start.3
  0.7 0.0 copy-start.4
  0.7 0.7 slice.6
  1.4 4.4 %collective-permute-start = (bf16[3,16,128]{2,1,0:T(8,128)(2,1)S(1)}, bf16[3,16,128]{2,1,0:T(8,128)(2,1)S(1)}, u32[]{:S(2)}, u32[]{:S(2)}) collective-permute-start(bf16[3,16,128]{2,1,0:T(8,128)(2,1)S(1)} %slice.6), channel_id=1, source_target_pairs={{0,32},{32,64},{64,96},{96,128},{128,160},{160,192},{192,224},{224... | collective-permute-start | bytes 36872 | tf_op jit(solution)/shard_map/ppermute | solution.py:437
  5.8 0.0 copy-done.2
  5.8 0.0 copy-done.3
  5.8 0.0 copy-done.4
  5.8 1.8 %prepare.1 = (f32[2,512,128]{2,1,0:T(8,128)S(1)}, f32[2,128,512]{2,1,0:T(8,128)S(1)}, f32[2,16,512]{2,1,0:T(8,128)S(1)}, f32[2,16,128]{2,1,0:T(8,128)S(1)}, f32[...) custom-call(f32[3,7,128]{2,1,0:T(8,128)S(1)} %copy-done.2, f32[8,16]{1,0:T(8,128)S(1)} %copy-done.3, ...), custom_call_target="tpu_custom_call" | custom-call | flops 3000000000 | bytes 9000000 | tf_op jit(solution)/shard_map/prepare/pallas_call | solution.py:440
  7.6 0.0 collective-permute-done.before_ref
  7.6 0.7 patch.1
  8.3 15.2 %all-to-all-start = ((f32[16,16,128]{2,1,0:T(8,128)}), f32[16,16,128]{2,1,0:T(8,128)S(1)}, u32[]{:S(2)}, u32[]{:S(2)}) async-start(f32[16,16,128]{2,1,0:T(8,128)} %get-tuple-element.24), calls=%async_computation | async-start | bytes 262144 | tf_op jit(solution)/shard_map/all_to_all | solution.py:456
  23.5 0.0 copy-start
  23.5 0.0 copy-start.1
  23.5 3.9 %within.1.near_ref = f32[1240,128]{1,0:T(8,128)S(1)} custom-call(f32[2,8,16]{2,1,0:T(8,128)S(1)} %get-tuple-element.25.table_ref, f32[2,128,512]{2,1,0:T(8,128)S(1)} %get-tuple-element.26.pair_ref, f32[2,16,512]{2,1,0:T(8,128)S(1)} %get-tuple-element.27.states_ref, f32[4,8,128]{2,1,0:T(8,128)S(1)} %get-tuple-element.28.patch_ref, ...), custom_call_target="tpu_custom_call" | custom-call | flops 8000000000 | bytes 24000000 | tf_op jit(solution)/shard_map/within/pallas_call | solution.py:457
  27.5 8.0 %all-to-all-done.arrived_ref = f32[16,16,128]{2,1,0:T(8,128)S(1)} async-done(((f32[16,16,128]{2,1,0:T(8,128)}), f32[16,16,128]{2,1,0:T(8,128)S(1)}, u32[]{:S(2)}, u32[]{:S(2)}) %all-to-all-start) | async-done | bytes 131104 | tf_op jit(solution)/shard_map/all_to_all | solution.py:456
  35.5 0.0 copy-done
  35.5 0.0 copy-done.1
  35.5 1.2 %across.1 = (f32[3,512,128]{2,1,0:T(8,128)S(1)}, f32[24,128]{1,0:T(8,128)S(1)}) custom-call(s32[1]{0:T(128)} %bitcast.me_ref, f32[16,16,128]{2,1,0:T(8,128)S(1)} %all-to-all-done.arrived_ref, f32[2,8,16]{2,1,0:T(8,128)S(1)} %get-tuple-element.25.table_ref, f32[1240,128]{1,0:T(8,128)S(1)} %within.1.near_ref, f32[2,512,128]{2,1,0:T(8,128)S(1)} %get-tuple-element.30.kv_ref, ...), custom_call_target="tpu_custom_call" | custom-call | flops 4000000000 | bytes 12000000 | tf_op jit(solution)/shard_map/across/pallas_call | solution.py:463
  36.7 0.7 broadcast_in_dim.3
  37.4 5.0 %all-to-all-start.1 = ((f16[16,24,128]{2,1,0:T(8,128)(2,1)}), f16[16,24,128]{2,1,0:T(8,128)(2,1)S(1)}, u32[]{:S(2)}, u32[]{:S(2)}) async-start(f16[16,24,128]{2,1,0:T(8,128)(2,1)} %broadcast_in_dim.3), calls=%async_computation.1 | async-start | bytes 196608 | tf_op jit(solution)/shard_map/all_to_all | solution.py:473
  42.4 1.3 %collective-permute-start.1 = (f32[3,8,128]{2,1,0:T(8,128)S(1)}, f32[3,8,128]{2,1,0:T(8,128)S(1)}, u32[]{:S(2)}, u32[]{:S(2)}) collective-permute-start(f32[3,8,128]{2,1,0:T(8,128)S(1)} %slice.7), channel_id=1, source_target_pairs={{32,0},{64,32},{96,64},{128,96},{160,128},{192,160},{224,192},{256... | collective-permute-start | bytes 36872 | tf_op jit(solution)/shard_map/ppermute | solution.py:469
  43.7 10.5 %all-to-all-done.1 = f16[16,24,128]{2,1,0:T(8,128)(2,1)S(1)} async-done(((f16[16,24,128]{2,1,0:T(8,128)(2,1)}), f16[16,24,128]{2,1,0:T(8,128)(2,1)S(1)}, u32[]{:S(2)}, u32[]{:S(2)}) %all-to-all-start.1) | async-done | bytes 98336 | tf_op jit(solution)/shard_map/all_to_all | solution.py:473
  54.2 0.6 total.1
  54.9 10.9 %all-to-all-start.2 = ((f32[32,1,128]{2,1,0:T(1,128)}), f32[32,1,128]{2,1,0:T(1,128)S(1)}, u32[]{:S(2)}, u32[]{:S(2)}) async-start(f32[32,1,128]{2,1,0:T(1,128)} %get-tuple-element.33), calls=%async_computation.2 | async-start | bytes 32768 | tf_op jit(solution)/shard_map/all_to_all | solution.py:481
  65.8 0.0 collective-permute-done.1.after_ref
  65.8 1.2 %inputs.1 = bf16[3,512,128]{2,1,0:T(8,128)(2,1)} custom-call(f32[3,512,128]{2,1,0:T(8,128)S(1)} %get-tuple-element.31.feature_ref, f32[3,8,128]{2,1,0:T(8,128)S(1)} %collective-permute-done.1.after_ref, f32[3,7,128]{2,1,0:T(8,128)S(1)} %copy-done.2), custom_call_target="tpu_custom_call" | custom-call | flops 2000000000 | bytes 6000000 | tf_op jit(solution)/shard_map/inputs/pallas_call | solution.py:474
  67.0 5.7 %all-to-all-done.2.square_ref = f32[32,1,128]{2,1,0:T(1,128)S(1)} async-done(((f32[32,1,128]{2,1,0:T(1,128)}), f32[32,1,128]{2,1,0:T(1,128)S(1)}, u32[]{:S(2)}, u32[]{:S(2)}) %all-to-all-start.2) | async-done | bytes 16416 | tf_op jit(solution)/shard_map/all_to_all | solution.py:481
  72.8 0.8 %scale.1 = (f32[3,7,128]{2,1,0:T(8,128)}, f32[8,16]{1,0:T(8,128)}, f32[8,16]{1,0:T(8,128)}) custom-call(f32[32,1,128]{2,1,0:T(1,128)S(1)} %all-to-all-done.2.square_ref, f32[24,128]{1,0:T(8,128)S(1)} %get-tuple-element.34.total_ref), custom_call_target="tpu_custom_call" | custom-call | flops 1000000000 | bytes 3000000 | tf_op jit(solution)/shard_map/scale/pallas_call | solution.py:482
  (3 shorter events, 0.0 us)
Async XLA Ops:
  0.6 5.1 %copy-start.2 = (f32[3,7,128]{2,1,0:T(8,128)S(1)}, f32[3,7,128]{2,1,0:T(8,128)}, u32[]{:S(2)}) copy-start(f32[3,7,128]{2,1,0:T(8,128)} %weight_ref.5) | copy-start | bytes 32260
  0.6 5.1 %copy-start.3 = (f32[8,16]{1,0:T(8,128)S(1)}, f32[8,16]{1,0:T(8,128)}, u32[]{:S(2)}) copy-start(f32[8,16]{1,0:T(8,128)} %rate_ref.1) | copy-start | bytes 1540
  0.7 5.1 %copy-start.4 = (f32[8,16]{1,0:T(8,128)S(1)}, f32[8,16]{1,0:T(8,128)}, u32[]{:S(2)}) copy-start(f32[8,16]{1,0:T(8,128)} %residue_ref.1) | copy-start | bytes 1540
  1.4 6.2 %collective-permute-start = (bf16[3,16,128]{2,1,0:T(8,128)(2,1)S(1)}, bf16[3,16,128]{2,1,0:T(8,128)(2,1)S(1)}, u32[]{:S(2)}, u32[]{:S(2)}) collective-permute-start(bf16[3,16,128]{2,1,0:T(8,128)(2,1)S(1)} %slice.6), channel_id=1, source_target_pairs={{0,32},{32,64},{64,96},{96,128},{128,160},{160,192},{192,224},{224... | collective-permute-start | bytes 36872 | tf_op jit(solution)/shard_map/ppermute | solution.py:437
  8.3 27.2 %all-to-all-start = ((f32[16,16,128]{2,1,0:T(8,128)}), f32[16,16,128]{2,1,0:T(8,128)S(1)}, u32[]{:S(2)}, u32[]{:S(2)}) async-start(f32[16,16,128]{2,1,0:T(8,128)} %get-tuple-element.24), calls=%async_computation | async-start | bytes 262144 | tf_op jit(solution)/shard_map/all_to_all | solution.py:456
  23.5 12.0 %copy-start = (bf16[3,512,128]{2,1,0:T(8,128)(2,1)S(1)}, bf16[3,512,128]{2,1,0:T(8,128)(2,1)}, u32[]{:S(2)}) copy-start(bf16[3,512,128]{2,1,0:T(8,128)(2,1)} %proj_ref.3) | copy-start | bytes 1179652
  23.5 12.0 %copy-start.1 = (bf16[512,128]{1,0:T(8,128)(2,1)S(1)}, bf16[512,128]{1,0:T(8,128)(2,1)}, u32[]{:S(2)}) copy-start(bf16[512,128]{1,0:T(8,128)(2,1)} %out_grad_ref.3) | copy-start | bytes 393220
  37.4 16.8 %all-to-all-start.1 = ((f16[16,24,128]{2,1,0:T(8,128)(2,1)}), f16[16,24,128]{2,1,0:T(8,128)(2,1)S(1)}, u32[]{:S(2)}, u32[]{:S(2)}) async-start(f16[16,24,128]{2,1,0:T(8,128)(2,1)} %broadcast_in_dim.3), calls=%async_computation.1 | async-start | bytes 196608 | tf_op jit(solution)/shard_map/all_to_all | solution.py:473
  42.4 23.5 %collective-permute-start.1 = (f32[3,8,128]{2,1,0:T(8,128)S(1)}, f32[3,8,128]{2,1,0:T(8,128)S(1)}, u32[]{:S(2)}, u32[]{:S(2)}) collective-permute-start(f32[3,8,128]{2,1,0:T(8,128)S(1)} %slice.7), channel_id=1, source_target_pairs={{32,0},{64,32},{96,64},{128,96},{160,128},{192,160},{224,192},{256... | collective-permute-start | bytes 36872 | tf_op jit(solution)/shard_map/ppermute | solution.py:469
  54.9 17.9 %all-to-all-start.2 = ((f32[32,1,128]{2,1,0:T(1,128)}), f32[32,1,128]{2,1,0:T(1,128)S(1)}, u32[]{:S(2)}, u32[]{:S(2)}) async-start(f32[32,1,128]{2,1,0:T(1,128)} %get-tuple-element.33), calls=%async_computation.2 | async-start | bytes 32768 | tf_op jit(solution)/shard_map/all_to_all | solution.py:481

commit v4 on v3

--- a/solution.py
+++ b/solution.py
@@ -167,9 +167,14 @@
     ends_ref[1] = back
 
 
-def patch_kernel(me_ref, before_ref, weight_ref, head_ref, power_ref, ends_ref,
+def scaled_columns(value):
+    largest = jnp.max(jnp.abs(value), axis=0, keepdims=True)
+    exponent = jnp.ceil(jnp.log2(jnp.maximum(largest, 1e-30))) - 15.0
+    return value * jnp.exp2(-exponent), exponent
+
+
+def patch_kernel(before_ref, weight_ref, head_ref, power_ref, ends_ref,
                  patch_ref, delta_ref, send_ref, ext_ref):
-    me = me_ref[0]
     feature = []
     for i in range(3):
         ext_ref[0:LEAD, :] = before_ref[i].astype(F32)
@@ -192,8 +197,10 @@
     delta_ref[1] = back_part
     state = ends_ref[0] + power_ref[2, 0] * state_part
     back = ends_ref[1] + back_part
-    for d in range(send_ref.shape[0]):
-        send_ref[d] = jnp.where(d > me, state, back).astype(send_ref.dtype)
+    for at, value in enumerate((back, state)):
+        scaled, exponent = scaled_columns(value)
+        send_ref[at, 0:MODES, :] = scaled
+        send_ref[at, MODES:, :] = jnp.broadcast_to(exponent, (8, CHANNELS))
 
 
 def spliced(wide_ref, patch):
@@ -304,7 +311,8 @@
     state_in, late_in, back_in = zero, zero, zero
     for d in range(arrived_ref.shape[0]):
         away = (jnp.abs(me - d) - 1).astype(F32) * float(ROWS)
-        term = jnp.exp(-small_rates * away) * arrived_ref[d].astype(F32)
+        scale = jnp.exp2(arrived_ref[d, MODES : MODES + 1, :])
+        term = jnp.exp(-small_rates * away) * (arrived_ref[d, 0:MODES, :] * scale)
         state_in = state_in + jnp.where(d < me, term, 0.0)
         late_in = late_in + jnp.where(d < me, term * away, 0.0)
         back_in = back_in + jnp.where(d > me, term, 0.0)
@@ -358,10 +366,9 @@
     rate_row = -row * mode_row(residues) * moment_row
     lines = [jnp.sum(part, axis=0, keepdims=True) for part in sums]
     stats = jnp.concatenate(lines + [residue_row, rate_row, jnp.zeros((1, CHANNELS), F32)], axis=0)
-    largest = jnp.max(jnp.abs(stats), axis=0, keepdims=True)
-    exponent = jnp.ceil(jnp.log2(jnp.maximum(largest, 1e-30))) - 15.0
+    scaled, exponent = scaled_columns(stats)
     last = iota((STATS, CHANNELS), 0) == STATS - 1
-    stats_ref[...] = jnp.where(last, exponent, stats * jnp.exp2(-exponent))
+    stats_ref[...] = jnp.where(last, exponent, scaled)
 
 
 def inputs_kernel(feature_ref, after_ref, weight_ref, out_ref, ext_ref):
@@ -449,11 +456,13 @@
       *(pltpu.with_memory_space_constraint(part, pltpu.HBM) for part in (projected, grad_out)))
     patch, delta, send = call(
         patch_kernel, "patch",
-        (shape(4, HEAD, CHANNELS), shape(2, MODES, CHANNELS), shape(ctx, MODES, CHANNELS)),
-        [SMEM] + [VMEM] * 5, 1,
+        (shape(4, HEAD, CHANNELS), shape(2, MODES, CHANNELS), shape(2, MODES + 8, CHANNELS)),
+        [VMEM] * 5, 1,
         scratch=[pltpu.VMEM((LEAD + HEAD, CHANNELS), F32)],
-    )(me, before, conv_weight, head, powers, ends)
-    arrived = lax.all_to_all(send, "ctx", 0, 0)
+    )(before, conv_weight, head, powers, ends)
+    later = lax.broadcasted_iota(jnp.int32, (ctx, 1, 1), 0) > me.reshape(1, 1, 1)
+    send = jnp.where(later, send[1], send[0]).astype(F16)
+    arrived = lax.all_to_all(send, "ctx", 0, 0).astype(F32)
     near = call(
         middle_kernel, "within",
         shape(2 * ROWS + LOCAL + 8, CHANNELS),

time: 74 us -> 73.7 us (level)
  other arithmetic: 0.02 us -> 0.78 us
    convert_element_type x0 -> x2, other arithmetic: none -> 0.75 us  [the longest x1 0.74 us: shards(): send = jnp.where(later, send[1], send[0]).astype(F16)]
where the time goes in v4:
time: 73.7 us; the launch traced here: 73.3 us
  starting transfers between devices  36.3 us (49%)
  waiting for transfers between devices  24.2 us (33%)
  Pallas kernels  9.67 us (13%)
  local copies, waits for them, and re-layouts  1.43 us (2%)
  between operations  0.82 us (1%)
  other arithmetic  0.78 us (1%)
    all_to_all x1, starting transfers between devices, shards(): arrived = lax.all_to_all(send, 'ctx', 0, 0).astype(F32)  15.2 us
    all_to_all x1, starting transfers between devices, shards(): squares = lax.all_to_all(square, 'ch', 0, 0)  11 us
    all_to_all x1, waiting for transfers between devices, shards(): gathered = lax.all_to_all(stats, 'ctx', 0, 0).astype(F32)  10.6 us
    all_to_all x1, waiting for transfers between devices, shards(): arrived = lax.all_to_all(send, 'ctx', 0, 0).astype(F32)  7.88 us
    all_to_all x1, waiting for transfers between devices, shards(): squares = lax.all_to_all(square, 'ch', 0, 0)  5.73 us
    ppermute x1, starting transfers between devices, shards(): lax.ppermute(projected[:, ROWS - LEAD:, :], 'ctx', [(source, source + 1)...  4.49 us
    all_to_all x1, starting transfers between devices, shards(): gathered = lax.all_to_all(stats, 'ctx', 0, 0).astype(F32)  4.42 us
    pallas_call x1, Pallas kernels, shards(): call(middle_kernel, 'within', shape(2 * ROWS + LOCAL + 8, CHANNELS), [VME...  3.93 us
  transfers between devices with their start and end apart: 5, of which 3 were waited for; matrix products, arithmetic and copies ran while one was open for 0% of the time, Pallas kernels for 10%

profile of v4, /device:TPU:1, one launch (start us, length us, event | category | flops | bytes accessed | tf_op | source)
XLA Modules:
  0.0 73.3 jit_solution(3858731032037749212)
XLA Ops:
  0.6 0.0 copy-start.2
  0.6 0.0 copy-start.4
  0.7 0.7 slice.12
  1.4 0.0 copy-start.3
  1.4 4.5 %collective-permute-start = (bf16[3,16,128]{2,1,0:T(8,128)(2,1)S(1)}, bf16[3,16,128]{2,1,0:T(8,128)(2,1)S(1)}, u32[]{:S(2)}, u32[]{:S(2)}) collective-permute-start(bf16[3,16,128]{2,1,0:T(8,128)(2,1)S(1)} %slice.12), channel_id=1, source_target_pairs={{0,32},{32,64},{64,96},{96,128},{128,160},{160,192},{192,224},{224... | collective-permute-start | bytes 36872 | tf_op jit(solution)/shard_map/ppermute | solution.py:444
  5.9 0.0 copy-done.2
  5.9 0.0 copy-done.4
  5.9 0.0 copy-done.3
  5.9 1.8 %prepare.1 = (f32[2,512,128]{2,1,0:T(8,128)S(1)}, f32[2,128,512]{2,1,0:T(8,128)S(1)}, f32[2,16,512]{2,1,0:T(8,128)S(1)}, f32[2,16,128]{2,1,0:T(8,128)S(1)}, f32[...) custom-call(f32[3,7,128]{2,1,0:T(8,128)S(1)} %copy-done.2, f32[8,16]{1,0:T(8,128)S(1)} %copy-done.3, ...), custom_call_target="tpu_custom_call" | custom-call | flops 3000000000 | bytes 9000000 | tf_op jit(solution)/shard_map/prepare/pallas_call | solution.py:447
  7.7 0.0 collective-permute-done.before_ref
  7.7 0.1 patch.1
  7.8 0.7 %select_convert_fusion = f16[16,24,128]{2,1,0:T(8,128)(2,1)} fusion(f32[24,128]{1,0:T(8,128)S(1)} %get-tuple-element.39, f32[24,128]{1,0:T(8,128)S(1)} %get-tuple-element.38, pred[16]{0:T(512)(128)(4,1)S(1)} %iota_compare_fusion), kind=kLoop, calls=%fused_computation | loop fusion | flops 98304 | bytes 122896 | tf_op jit(solution)/shard_map/convert_element_type | solution.py:464
  8.6 15.2 %all-to-all-start = ((f16[16,24,128]{2,1,0:T(8,128)(2,1)}), f16[16,24,128]{2,1,0:T(8,128)(2,1)S(1)}, u32[]{:S(2)}, u32[]{:S(2)}) async-start(f16[16,24,128]{2,1,0:T(8,128)(2,1)} %select_convert_fusion), calls=%async_computation | async-start | bytes 196608 | tf_op jit(solution)/shard_map/all_to_all | solution.py:465
  23.7 0.0 copy-start
  23.7 3.9 %within.1.near_ref = f32[1240,128]{1,0:T(8,128)S(1)} custom-call(f32[2,8,16]{2,1,0:T(8,128)S(1)} %get-tuple-element.25.table_ref, f32[2,128,512]{2,1,0:T(8,128)S(1)} %get-tuple-element.26.pair_ref, f32[2,16,512]{2,1,0:T(8,128)S(1)} %get-tuple-element.27.states_ref, f32[4,8,128]{2,1,0:T(8,128)S(1)} %get-tuple-element.28.patch_ref, ...), custom_call_target="tpu_custom_call" | custom-call | flops 8000000000 | bytes 24000000 | tf_op jit(solution)/shard_map/within/pallas_call | solution.py:466
  27.7 0.0 copy-start.1
  27.7 7.9 %all-to-all-done = f16[16,24,128]{2,1,0:T(8,128)(2,1)S(1)} async-done(((f16[16,24,128]{2,1,0:T(8,128)(2,1)}), f16[16,24,128]{2,1,0:T(8,128)(2,1)S(1)}, u32[]{:S(2)}, u32[]{:S(2)}) %all-to-all-start) | async-done | bytes 98336 | tf_op jit(solution)/shard_map/all_to_all | solution.py:465
  35.6 0.0 copy-done
  35.6 0.0 copy-done.1
  35.6 1.2 %across.1 = (f32[3,512,128]{2,1,0:T(8,128)S(1)}, f32[24,128]{1,0:T(8,128)S(1)}) custom-call(s32[1]{0:T(128)} %bitcast.me_ref, f32[16,24,128]{2,1,0:T(8,128)S(1)} %convert_element_type.13.arrived_ref, f32[2,8,16]{2,1,0:T(8,128)S(1)} %get-tuple-element.25.table_ref, f32[1240,128]{1,0:T(8,128)S(1)} %within.1.near_ref, ...), custom_call_target="tpu_custom_call" | custom-call | flops 4000000000 | bytes 12000000 | tf_op jit(solution)/shard_map/across/pallas_call | solution.py:472
  36.8 0.7 broadcast_in_dim.22
  37.5 4.4 %all-to-all-start.1 = ((f16[16,24,128]{2,1,0:T(8,128)(2,1)}), f16[16,24,128]{2,1,0:T(8,128)(2,1)S(1)}, u32[]{:S(2)}, u32[]{:S(2)}) async-start(f16[16,24,128]{2,1,0:T(8,128)(2,1)} %broadcast_in_dim.22), calls=%async_computation.1 | async-start | bytes 196608 | tf_op jit(solution)/shard_map/all_to_all | solution.py:482
  41.9 1.3 %collective-permute-start.1 = (f32[3,8,128]{2,1,0:T(8,128)S(1)}, f32[3,8,128]{2,1,0:T(8,128)S(1)}, u32[]{:S(2)}, u32[]{:S(2)}) collective-permute-start(f32[3,8,128]{2,1,0:T(8,128)S(1)} %slice.15), channel_id=1, source_target_pairs={{32,0},{64,32},{96,64},{128,96},{160,128},{192,160},{224,192},{256... | collective-permute-start | bytes 36872 | tf_op jit(solution)/shard_map/ppermute | solution.py:478
  43.2 10.6 %all-to-all-done.1 = f16[16,24,128]{2,1,0:T(8,128)(2,1)S(1)} async-done(((f16[16,24,128]{2,1,0:T(8,128)(2,1)}), f16[16,24,128]{2,1,0:T(8,128)(2,1)S(1)}, u32[]{:S(2)}, u32[]{:S(2)}) %all-to-all-start.1) | async-done | bytes 98336 | tf_op jit(solution)/shard_map/all_to_all | solution.py:482
  53.9 0.6 total.1
  54.5 11.0 %all-to-all-start.2 = ((f32[32,1,128]{2,1,0:T(1,128)}), f32[32,1,128]{2,1,0:T(1,128)S(1)}, u32[]{:S(2)}, u32[]{:S(2)}) async-start(f32[32,1,128]{2,1,0:T(1,128)} %get-tuple-element.33), calls=%async_computation.2 | async-start | bytes 32768 | tf_op jit(solution)/shard_map/all_to_all | solution.py:490
  65.5 0.0 collective-permute-done.1.after_ref
  65.5 1.2 %inputs.1 = bf16[3,512,128]{2,1,0:T(8,128)(2,1)} custom-call(f32[3,512,128]{2,1,0:T(8,128)S(1)} %get-tuple-element.31.feature_ref, f32[3,8,128]{2,1,0:T(8,128)S(1)} %collective-permute-done.1.after_ref, f32[3,7,128]{2,1,0:T(8,128)S(1)} %copy-done.2), custom_call_target="tpu_custom_call" | custom-call | flops 2000000000 | bytes 6000000 | tf_op jit(solution)/shard_map/inputs/pallas_call | solution.py:483
  66.7 5.7 %all-to-all-done.2.square_ref = f32[32,1,128]{2,1,0:T(1,128)S(1)} async-done(((f32[32,1,128]{2,1,0:T(1,128)}), f32[32,1,128]{2,1,0:T(1,128)S(1)}, u32[]{:S(2)}, u32[]{:S(2)}) %all-to-all-start.2) | async-done | bytes 16416 | tf_op jit(solution)/shard_map/all_to_all | solution.py:490
  72.4 0.8 %scale.1 = (f32[3,7,128]{2,1,0:T(8,128)}, f32[8,16]{1,0:T(8,128)}, f32[8,16]{1,0:T(8,128)}) custom-call(f32[32,1,128]{2,1,0:T(1,128)S(1)} %all-to-all-done.2.square_ref, f32[24,128]{1,0:T(8,128)S(1)} %get-tuple-element.34.total_ref), custom_call_target="tpu_custom_call" | custom-call | flops 1000000000 | bytes 3000000 | tf_op jit(solution)/shard_map/scale/pallas_call | solution.py:491
  (6 shorter events, 0.1 us)
Async XLA Ops:
  0.6 5.3 %copy-start.2 = (f32[3,7,128]{2,1,0:T(8,128)S(1)}, f32[3,7,128]{2,1,0:T(8,128)}, u32[]{:S(2)}) copy-start(f32[3,7,128]{2,1,0:T(8,128)} %weight_ref.5) | copy-start | bytes 32260
  0.6 5.3 %copy-start.4 = (f32[8,16]{1,0:T(8,128)S(1)}, f32[8,16]{1,0:T(8,128)}, u32[]{:S(2)}) copy-start(f32[8,16]{1,0:T(8,128)} %residue_ref.1) | copy-start | bytes 1540
  1.4 4.5 %copy-start.3 = (f32[8,16]{1,0:T(8,128)S(1)}, f32[8,16]{1,0:T(8,128)}, u32[]{:S(2)}) copy-start(f32[8,16]{1,0:T(8,128)} %rate_ref.1) | copy-start | bytes 1540
  1.4 6.3 %collective-permute-start = (bf16[3,16,128]{2,1,0:T(8,128)(2,1)S(1)}, bf16[3,16,128]{2,1,0:T(8,128)(2,1)S(1)}, u32[]{:S(2)}, u32[]{:S(2)}) collective-permute-start(bf16[3,16,128]{2,1,0:T(8,128)(2,1)S(1)} %slice.12), channel_id=1, source_target_pairs={{0,32},{32,64},{64,96},{96,128},{128,160},{160,192},{192,224},{224... | collective-permute-start | bytes 36872 | tf_op jit(solution)/shard_map/ppermute | solution.py:444
  8.6 27.0 %all-to-all-start = ((f16[16,24,128]{2,1,0:T(8,128)(2,1)}), f16[16,24,128]{2,1,0:T(8,128)(2,1)S(1)}, u32[]{:S(2)}, u32[]{:S(2)}) async-start(f16[16,24,128]{2,1,0:T(8,128)(2,1)} %select_convert_fusion), calls=%async_computation | async-start | bytes 196608 | tf_op jit(solution)/shard_map/all_to_all | solution.py:465
  23.7 11.9 %copy-start = (bf16[3,512,128]{2,1,0:T(8,128)(2,1)S(1)}, bf16[3,512,128]{2,1,0:T(8,128)(2,1)}, u32[]{:S(2)}) copy-start(bf16[3,512,128]{2,1,0:T(8,128)(2,1)} %proj_ref.3) | copy-start | bytes 1179652
  27.7 7.9 %copy-start.1 = (bf16[512,128]{1,0:T(8,128)(2,1)S(1)}, bf16[512,128]{1,0:T(8,128)(2,1)}, u32[]{:S(2)}) copy-start(bf16[512,128]{1,0:T(8,128)(2,1)} %out_grad_ref.3) | copy-start | bytes 393220
  37.5 16.4 %all-to-all-start.1 = ((f16[16,24,128]{2,1,0:T(8,128)(2,1)}), f16[16,24,128]{2,1,0:T(8,128)(2,1)S(1)}, u32[]{:S(2)}, u32[]{:S(2)}) async-start(f16[16,24,128]{2,1,0:T(8,128)(2,1)} %broadcast_in_dim.22), calls=%async_computation.1 | async-start | bytes 196608 | tf_op jit(solution)/shard_map/all_to_all | solution.py:482
  41.9 23.6 %collective-permute-start.1 = (f32[3,8,128]{2,1,0:T(8,128)S(1)}, f32[3,8,128]{2,1,0:T(8,128)S(1)}, u32[]{:S(2)}, u32[]{:S(2)}) collective-permute-start(f32[3,8,128]{2,1,0:T(8,128)S(1)} %slice.15), channel_id=1, source_target_pairs={{32,0},{64,32},{96,64},{128,96},{160,128},{192,160},{224,192},{256... | collective-permute-start | bytes 36872 | tf_op jit(solution)/shard_map/ppermute | solution.py:478
  54.5 17.9 %all-to-all-start.2 = ((f32[32,1,128]{2,1,0:T(1,128)}), f32[32,1,128]{2,1,0:T(1,128)S(1)}, u32[]{:S(2)}, u32[]{:S(2)}) async-start(f32[32,1,128]{2,1,0:T(1,128)} %get-tuple-element.33), calls=%async_computation.2 | async-start | bytes 32768 | tf_op jit(solution)/shard_map/all_to_all | solution.py:490

commit v5 on v4

--- a/solution.py
+++ b/solution.py
@@ -88,6 +88,10 @@
 
 def near_parts(near_ref):
     return near_ref.at[0:ROWS, :], near_ref.at[ROWS : 2 * ROWS, :], near_ref.at[2 * ROWS :, :]
+
+
+def member(position, count):
+    return (position + count // 2) % count
 
 
 def piece(at):
@@ -309,10 +313,11 @@
     chunk_decay = jnp.exp(-small_rates * CHUNK)
     zero = jnp.zeros((MODES, CHANNELS), F32)
     state_in, late_in, back_in = zero, zero, zero
-    for d in range(arrived_ref.shape[0]):
+    for at in range(arrived_ref.shape[0]):
+        d = member(at, arrived_ref.shape[0])
         away = (jnp.abs(me - d) - 1).astype(F32) * float(ROWS)
-        scale = jnp.exp2(arrived_ref[d, MODES : MODES + 1, :])
-        term = jnp.exp(-small_rates * away) * (arrived_ref[d, 0:MODES, :] * scale)
+        scale = jnp.exp2(arrived_ref[at, MODES : MODES + 1, :])
+        term = jnp.exp(-small_rates * away) * (arrived_ref[at, 0:MODES, :] * scale)
         state_in = state_in + jnp.where(d < me, term, 0.0)
         late_in = late_in + jnp.where(d < me, term * away, 0.0)
         back_in = back_in + jnp.where(d > me, term, 0.0)
@@ -437,6 +442,11 @@
     )
 
 
+def exchange(blocks):
+    count = blocks.shape[0]
+    return lax.all_to_all(blocks, "ctx", 0, 0, axis_index_groups=[[member(p, count) for p in range(count)]])
+
+
 def shards(projected, conv_weight, residues, decay_rates, grad_out):
     ctx = lax.axis_size("ctx")
     planes = lax.axis_size("ch")
@@ -460,9 +470,9 @@
         [VMEM] * 5, 1,
         scratch=[pltpu.VMEM((LEAD + HEAD, CHANNELS), F32)],
     )(before, conv_weight, head, powers, ends)
-    later = lax.broadcasted_iota(jnp.int32, (ctx, 1, 1), 0) > me.reshape(1, 1, 1)
+    later = member(lax.broadcasted_iota(jnp.int32, (ctx, 1, 1), 0), ctx) > me.reshape(1, 1, 1)
     send = jnp.where(later, send[1], send[0]).astype(F16)
-    arrived = lax.all_to_all(send, "ctx", 0, 0).astype(F32)
+    arrived = exchange(send).astype(F32)
     near = call(
         middle_kernel, "within",
         shape(2 * ROWS + LOCAL + 8, CHANNELS),
@@ -479,7 +489,7 @@
         grad_feature[:, :8, :], "ctx", [(source + 1, source) for source in range(ctx - 1)]
     )
     stats = jnp.broadcast_to(stats.astype(F16), (ctx, STATS, CHANNELS))
-    gathered = lax.all_to_all(stats, "ctx", 0, 0).astype(F32)
+    gathered = exchange(stats).astype(F32)
     grad_projected = call(
         inputs_kernel, "inputs", shape(3, ROWS, CHANNELS, dtype=BF16), [VMEM] * 3, 2,
         scratch=[pltpu.VMEM((ROWS + 8, CHANNELS), F32)],

time: 73.7 us -> 67.4 us (0.915)
  waiting for transfers between devices: 24.2 us -> 8.27 us
  starting transfers between devices: 36.3 us -> 45.2 us
  local copies, waits for them, and re-layouts: 1.43 us -> 2.28 us
    all_to_all x2, waiting for transfers between devices: 18.5 us -> 2.53 us  [exchange(): lax.all_to_all(blocks, 'ctx', 0, 0, axis_index_groups=[[member(p, count)...]
    all_to_all x2, starting transfers between devices: 19.6 us -> 28.8 us  [exchange(): lax.all_to_all(blocks, 'ctx', 0, 0, axis_index_groups=[[member(p, count)...]
    unnamed x10, local copies, waits for them, and re-layouts: 0.02 us -> 0.87 us
  transfers between devices with their start and end apart: 5 -> 5, of which waited for: 3 -> 2; matrix products, arithmetic and copies ran while one was open for 0% -> 0% of each run, Pallas kernels for 10% -> 11%
where the time goes in v5:
time: 67.4 us; the launch traced here: 67 us
  starting transfers between devices  45.2 us (67%)
  Pallas kernels  9.67 us (14%)
  waiting for transfers between devices  8.27 us (12%)
  local copies, waits for them, and re-layouts  2.28 us (3%)
  between operations  0.8 us (1%)
  other arithmetic  0.79 us (1%)
    all_to_all x2, starting transfers between devices, exchange(): lax.all_to_all(blocks, 'ctx', 0, 0, axis_index_groups=[[member(p, count)...  28.8 us
    all_to_all x1, starting transfers between devices, shards(): squares = lax.all_to_all(square, 'ch', 0, 0)  10.6 us
    all_to_all x1, waiting for transfers between devices, shards(): squares = lax.all_to_all(square, 'ch', 0, 0)  5.73 us
    ppermute x1, starting transfers between devices, shards(): lax.ppermute(projected[:, ROWS - LEAD:, :], 'ctx', [(source, source + 1)...  4.49 us
    pallas_call x1, Pallas kernels, shards(): call(middle_kernel, 'within', shape(2 * ROWS + LOCAL + 8, CHANNELS), [VME...  3.93 us
    all_to_all x2, waiting for transfers between devices, exchange(): lax.all_to_all(blocks, 'ctx', 0, 0, axis_index_groups=[[member(p, count)...  2.53 us
    pallas_call x1, Pallas kernels, shards(): call(prepare_kernel, 'prepare', (shape(2, ROWS, CHANNELS), shape(2, CHUNK...  1.79 us
  transfers between devices with their start and end apart: 5, of which 2 were waited for; matrix products, arithmetic and copies ran while one was open for 0% of the time, Pallas kernels for 11%

profile of v5, /device:TPU:1, one launch (start us, length us, event | category | flops | bytes accessed | tf_op | source)
XLA Modules:
  0.0 67.0 jit_solution(4623153250233978081)
XLA Ops:
  0.6 0.0 copy-start.2
  0.6 0.0 copy-start.4
  0.7 0.7 %slice.12 = bf16[3,16,128]{2,1,0:T(8,128)(2,1)S(1)} slice(bf16[3,512,128]{2,1,0:T(8,128)(2,1)} %proj_ref.3), slice={[0:3], [496:512], [0:128]} | slice | bytes 24576 | tf_op jit(solution)/shard_map/slice | solution.py:455
  1.4 0.0 copy-start.3
  1.4 4.5 %collective-permute-start = (bf16[3,16,128]{2,1,0:T(8,128)(2,1)S(1)}, bf16[3,16,128]{2,1,0:T(8,128)(2,1)S(1)}, u32[]{:S(2)}, u32[]{:S(2)}) collective-permute-start(bf16[3,16,128]{2,1,0:T(8,128)(2,1)S(1)} %slice.12), channel_id=1, source_target_pairs={{0,32},{32,64},{64,96},{96,128},{128,160},{160,192},{192,224},{224... | collective-permute-start | bytes 36872 | tf_op jit(solution)/shard_map/ppermute | solution.py:454
  5.9 0.0 copy-done.2
  5.9 0.0 copy-done.4
  5.9 0.0 copy-done.3
  5.9 1.8 %prepare.1 = (f32[2,512,128]{2,1,0:T(8,128)S(1)}, f32[2,128,512]{2,1,0:T(8,128)S(1)}, f32[2,16,512]{2,1,0:T(8,128)S(1)}, f32[2,16,128]{2,1,0:T(8,128)S(1)}, f32[...) custom-call(f32[3,7,128]{2,1,0:T(8,128)S(1)} %copy-done.2, f32[8,16]{1,0:T(8,128)S(1)} %copy-done.3, ...), custom_call_target="tpu_custom_call" | custom-call | flops 3000000000 | bytes 9000000 | tf_op jit(solution)/shard_map/prepare/pallas_call | solution.py:457
  7.7 0.0 collective-permute-done.before_ref
  7.7 0.1 patch.1
  7.8 0.7 %select_convert_fusion = f16[16,24,128]{2,1,0:T(8,128)(2,1)} fusion(f32[24,128]{1,0:T(8,128)S(1)} %get-tuple-element.39, f32[24,128]{1,0:T(8,128)S(1)} %get-tuple-element.38, pred[16]{0:T(512)(128)(4,1)S(1)} %fusion), kind=kLoop, calls=%fused_computation | loop fusion | flops 98304 | bytes 122896 | tf_op jit(solution)/shard_map/convert_element_type | solution.py:474
  8.6 17.3 %all-to-all-start = ((f16[16,24,128]{2,1,0:T(8,128)(2,1)}), f16[16,24,128]{2,1,0:T(8,128)(2,1)S(1)}, u32[]{:S(2)}, u32[]{:S(2)}) async-start(f16[16,24,128]{2,1,0:T(8,128)(2,1)} %select_convert_fusion), calls=%async_computation | async-start | bytes 196608 | tf_op jit(solution)/shard_map/all_to_all | solution.py:447
  25.9 0.0 copy-start
  25.9 3.9 %within.1.near_ref = f32[1240,128]{1,0:T(8,128)S(1)} custom-call(f32[2,8,16]{2,1,0:T(8,128)S(1)} %get-tuple-element.25.table_ref, f32[2,128,512]{2,1,0:T(8,128)S(1)} %get-tuple-element.26.pair_ref, f32[2,16,512]{2,1,0:T(8,128)S(1)} %get-tuple-element.27.states_ref, f32[4,8,128]{2,1,0:T(8,128)S(1)} %get-tuple-element.28.patch_ref, ...), custom_call_target="tpu_custom_call" | custom-call | flops 8000000000 | bytes 24000000 | tf_op jit(solution)/shard_map/within/pallas_call | solution.py:476
  29.8 0.0 copy-start.1
  29.8 0.0 all-to-all-done
  29.9 0.0 copy-done
  29.9 0.9 %copy-done.1 = bf16[512,128]{1,0:T(8,128)(2,1)S(1)} copy-done((bf16[512,128]{1,0:T(8,128)(2,1)S(1)}, bf16[512,128]{1,0:T(8,128)(2,1)}, u32[]{:S(2)}) %copy-start.1) | copy-done | bytes 131096
  30.7 1.2 %across.1 = (f32[3,512,128]{2,1,0:T(8,128)S(1)}, f32[24,128]{1,0:T(8,128)S(1)}) custom-call(s32[1]{0:T(128)} %bitcast.me_ref, f32[16,24,128]{2,1,0:T(8,128)S(1)} %convert_element_type.13.arrived_ref, f32[2,8,16]{2,1,0:T(8,128)S(1)} %get-tuple-element.25.table_ref, f32[1240,128]{1,0:T(8,128)S(1)} %within.1.near_ref, ...), custom_call_target="tpu_custom_call" | custom-call | flops 4000000000 | bytes 12000000 | tf_op jit(solution)/shard_map/across/pallas_call | solution.py:482
  31.9 0.7 broadcast_in_dim.22
  32.6 11.5 %all-to-all-start.1 = ((f16[16,24,128]{2,1,0:T(8,128)(2,1)}), f16[16,24,128]{2,1,0:T(8,128)(2,1)S(1)}, u32[]{:S(2)}, u32[]{:S(2)}) async-start(f16[16,24,128]{2,1,0:T(8,128)(2,1)} %broadcast_in_dim.22), calls=%async_computation.1 | async-start | bytes 196608 | tf_op jit(solution)/shard_map/all_to_all | solution.py:447
  44.1 1.3 %collective-permute-start.1 = (f32[3,8,128]{2,1,0:T(8,128)S(1)}, f32[3,8,128]{2,1,0:T(8,128)S(1)}, u32[]{:S(2)}, u32[]{:S(2)}) collective-permute-start(f32[3,8,128]{2,1,0:T(8,128)S(1)} %slice.15), channel_id=1, source_target_pairs={{32,0},{64,32},{96,64},{128,96},{160,128},{192,160},{224,192},{256... | collective-permute-start | bytes 36872 | tf_op jit(solution)/shard_map/ppermute | solution.py:488
  45.4 2.5 %all-to-all-done.1 = f16[16,24,128]{2,1,0:T(8,128)(2,1)S(1)} async-done(((f16[16,24,128]{2,1,0:T(8,128)(2,1)}), f16[16,24,128]{2,1,0:T(8,128)(2,1)S(1)}, u32[]{:S(2)}, u32[]{:S(2)}) %all-to-all-start.1) | async-done | bytes 98336 | tf_op jit(solution)/shard_map/all_to_all | solution.py:447
  47.9 0.6 total.1
  48.6 10.6 %all-to-all-start.2 = ((f32[32,1,128]{2,1,0:T(1,128)}), f32[32,1,128]{2,1,0:T(1,128)S(1)}, u32[]{:S(2)}, u32[]{:S(2)}) async-start(f32[32,1,128]{2,1,0:T(1,128)} %get-tuple-element.33), calls=%async_computation.2 | async-start | bytes 32768 | tf_op jit(solution)/shard_map/all_to_all | solution.py:500
  59.2 0.0 collective-permute-done.1.after_ref
  59.2 1.2 %inputs.1 = bf16[3,512,128]{2,1,0:T(8,128)(2,1)} custom-call(f32[3,512,128]{2,1,0:T(8,128)S(1)} %get-tuple-element.31.feature_ref, f32[3,8,128]{2,1,0:T(8,128)S(1)} %collective-permute-done.1.after_ref, f32[3,7,128]{2,1,0:T(8,128)S(1)} %copy-done.2), custom_call_target="tpu_custom_call" | custom-call | flops 2000000000 | bytes 6000000 | tf_op jit(solution)/shard_map/inputs/pallas_call | solution.py:493
  60.4 5.7 %all-to-all-done.2.square_ref = f32[32,1,128]{2,1,0:T(1,128)S(1)} async-done(((f32[32,1,128]{2,1,0:T(1,128)}), f32[32,1,128]{2,1,0:T(1,128)S(1)}, u32[]{:S(2)}, u32[]{:S(2)}) %all-to-all-start.2) | async-done | bytes 16416 | tf_op jit(solution)/shard_map/all_to_all | solution.py:500
  66.1 0.8 %scale.1 = (f32[3,7,128]{2,1,0:T(8,128)}, f32[8,16]{1,0:T(8,128)}, f32[8,16]{1,0:T(8,128)}) custom-call(f32[32,1,128]{2,1,0:T(1,128)S(1)} %all-to-all-done.2.square_ref, f32[24,128]{1,0:T(8,128)S(1)} %get-tuple-element.34.total_ref), custom_call_target="tpu_custom_call" | custom-call | flops 1000000000 | bytes 3000000 | tf_op jit(solution)/shard_map/scale/pallas_call | solution.py:501
  (6 shorter events, 0.1 us)
Async XLA Ops:
  0.6 5.3 %copy-start.2 = (f32[3,7,128]{2,1,0:T(8,128)S(1)}, f32[3,7,128]{2,1,0:T(8,128)}, u32[]{:S(2)}) copy-start(f32[3,7,128]{2,1,0:T(8,128)} %weight_ref.5) | copy-start | bytes 32260
  0.6 5.3 %copy-start.4 = (f32[8,16]{1,0:T(8,128)S(1)}, f32[8,16]{1,0:T(8,128)}, u32[]{:S(2)}) copy-start(f32[8,16]{1,0:T(8,128)} %residue_ref.1) | copy-start | bytes 1540
  1.4 4.5 %copy-start.3 = (f32[8,16]{1,0:T(8,128)S(1)}, f32[8,16]{1,0:T(8,128)}, u32[]{:S(2)}) copy-start(f32[8,16]{1,0:T(8,128)} %rate_ref.1) | copy-start | bytes 1540
  1.4 6.3 %collective-permute-start = (bf16[3,16,128]{2,1,0:T(8,128)(2,1)S(1)}, bf16[3,16,128]{2,1,0:T(8,128)(2,1)S(1)}, u32[]{:S(2)}, u32[]{:S(2)}) collective-permute-start(bf16[3,16,128]{2,1,0:T(8,128)(2,1)S(1)} %slice.12), channel_id=1, source_target_pairs={{0,32},{32,64},{64,96},{96,128},{128,160},{160,192},{192,224},{224... | collective-permute-start | bytes 36872 | tf_op jit(solution)/shard_map/ppermute | solution.py:454
  8.6 21.3 %all-to-all-start = ((f16[16,24,128]{2,1,0:T(8,128)(2,1)}), f16[16,24,128]{2,1,0:T(8,128)(2,1)S(1)}, u32[]{:S(2)}, u32[]{:S(2)}) async-start(f16[16,24,128]{2,1,0:T(8,128)(2,1)} %select_convert_fusion), calls=%async_computation | async-start | bytes 196608 | tf_op jit(solution)/shard_map/all_to_all | solution.py:447
  25.9 4.0 %copy-start = (bf16[3,512,128]{2,1,0:T(8,128)(2,1)S(1)}, bf16[3,512,128]{2,1,0:T(8,128)(2,1)}, u32[]{:S(2)}) copy-start(bf16[3,512,128]{2,1,0:T(8,128)(2,1)} %proj_ref.3) | copy-start | bytes 1179652
  29.8 0.9 %copy-start.1 = (bf16[512,128]{1,0:T(8,128)(2,1)S(1)}, bf16[512,128]{1,0:T(8,128)(2,1)}, u32[]{:S(2)}) copy-start(bf16[512,128]{1,0:T(8,128)(2,1)} %out_grad_ref.3) | copy-start | bytes 393220
  32.6 15.3 %all-to-all-start.1 = ((f16[16,24,128]{2,1,0:T(8,128)(2,1)}), f16[16,24,128]{2,1,0:T(8,128)(2,1)S(1)}, u32[]{:S(2)}, u32[]{:S(2)}) async-start(f16[16,24,128]{2,1,0:T(8,128)(2,1)} %broadcast_in_dim.22), calls=%async_computation.1 | async-start | bytes 196608 | tf_op jit(solution)/shard_map/all_to_all | solution.py:447
  44.1 15.1 %collective-permute-start.1 = (f32[3,8,128]{2,1,0:T(8,128)S(1)}, f32[3,8,128]{2,1,0:T(8,128)S(1)}, u32[]{:S(2)}, u32[]{:S(2)}) collective-permute-start(f32[3,8,128]{2,1,0:T(8,128)S(1)} %slice.15), channel_id=1, source_target_pairs={{32,0},{64,32},{96,64},{128,96},{160,128},{192,160},{224,192},{256... | collective-permute-start | bytes 36872 | tf_op jit(solution)/shard_map/ppermute | solution.py:488
  48.6 17.6 %all-to-all-start.2 = ((f32[32,1,128]{2,1,0:T(1,128)}), f32[32,1,128]{2,1,0:T(1,128)S(1)}, u32[]{:S(2)}, u32[]{:S(2)}) async-start(f32[32,1,128]{2,1,0:T(1,128)} %get-tuple-element.33), calls=%async_computation.2 | async-start | bytes 32768 | tf_op jit(solution)/shard_map/all_to_all | solution.py:500

commit v6 on v5

--- a/solution.py
+++ b/solution.py
@@ -442,9 +442,9 @@
     )
 
 
-def exchange(blocks):
+def exchange(blocks, axis, first):
     count = blocks.shape[0]
-    return lax.all_to_all(blocks, "ctx", 0, 0, axis_index_groups=[[member(p, count) for p in range(count)]])
+    return lax.all_to_all(blocks, axis, 0, 0, axis_index_groups=[[(first + p) % count for p in range(count)]])
 
 
 def shards(projected, conv_weight, residues, decay_rates, grad_out):
@@ -472,7 +472,7 @@
     )(before, conv_weight, head, powers, ends)
     later = member(lax.broadcasted_iota(jnp.int32, (ctx, 1, 1), 0), ctx) > me.reshape(1, 1, 1)
     send = jnp.where(later, send[1], send[0]).astype(F16)
-    arrived = exchange(send).astype(F32)
+    arrived = exchange(send, "ctx", ctx // 2).astype(F32)
     near = call(
         middle_kernel, "within",
         shape(2 * ROWS + LOCAL + 8, CHANNELS),
@@ -489,7 +489,7 @@
         grad_feature[:, :8, :], "ctx", [(source + 1, source) for source in range(ctx - 1)]
     )
     stats = jnp.broadcast_to(stats.astype(F16), (ctx, STATS, CHANNELS))
-    gathered = exchange(stats).astype(F32)
+    gathered = exchange(stats, "ctx", ctx // 2).astype(F32)
     grad_projected = call(
         inputs_kernel, "inputs", shape(3, ROWS, CHANNELS, dtype=BF16), [VMEM] * 3, 2,
         scratch=[pltpu.VMEM((ROWS + 8, CHANNELS), F32)],
@@ -497,7 +497,7 @@
     total, square = call(
         total_kernel, "total", (shape(STATS, CHANNELS), shape(planes, 1, CHANNELS)), [VMEM], 1,
     )(gathered)
-    squares = lax.all_to_all(square, "ch", 0, 0)
+    squares = exchange(square, "ch", planes // 2 + planes // 8)
     grad_conv, grad_residues, grad_log_rates = call(
         scale_kernel, "scale",
         (shape(3, KW, CHANNELS), shape(GROUPS, MODES), shape(GROUPS, MODES)), [VMEM] * 2, 1,

time: 67.4 us -> 64.2 us (0.953)
  waiting for transfers between devices: 8.27 us -> 3.31 us
  starting transfers between devices: 45.2 us -> 47 us
    all_to_all x3, waiting for transfers between devices: 8.27 us -> 3.31 us  [exchange(): lax.all_to_all(blocks, axis, 0, 0, axis_index_groups=[[(first + p) % coun...]
    all_to_all x3, starting transfers between devices: 39.4 us -> 41.2 us  [exchange(): lax.all_to_all(blocks, axis, 0, 0, axis_index_groups=[[(first + p) % coun...]
  transfers between devices with their start and end apart: 5 -> 5, of which waited for: 2 -> 2; matrix products, arithmetic and copies ran while one was open for 0% -> 0% of each run, Pallas kernels for 11% -> 12%
where the time goes in v6:
time: 64.2 us; the launch traced here: 63.8 us
  starting transfers between devices  47 us (73%)
  Pallas kernels  9.67 us (15%)
  waiting for transfers between devices  3.31 us (5%)
  local copies, waits for them, and re-layouts  2.28 us (4%)
  between operations  0.8 us (1%)
  other arithmetic  0.79 us (1%)
    all_to_all x3, starting transfers between devices, exchange(): lax.all_to_all(blocks, axis, 0, 0, axis_index_groups=[[(first + p) % coun...  41.2 us
    ppermute x1, starting transfers between devices, shards(): lax.ppermute(projected[:, ROWS - LEAD:, :], 'ctx', [(source, source + 1)...  4.49 us
    pallas_call x1, Pallas kernels, shards(): call(middle_kernel, 'within', shape(2 * ROWS + LOCAL + 8, CHANNELS), [VME...  3.93 us
    all_to_all x3, waiting for transfers between devices, exchange(): lax.all_to_all(blocks, axis, 0, 0, axis_index_groups=[[(first + p) % coun...  3.31 us
    pallas_call x1, Pallas kernels, shards(): call(prepare_kernel, 'prepare', (shape(2, ROWS, CHANNELS), shape(2, CHUNK...  1.79 us
    ppermute x1, starting transfers between devices, shards(): lax.ppermute(grad_feature[:, :8, :], 'ctx', [(source + 1, source) for sou...  1.29 us
  transfers between devices with their start and end apart: 5, of which 2 were waited for; matrix products, arithmetic and copies ran while one was open for 0% of the time, Pallas kernels for 12%

profile of v6, /device:TPU:1, one launch (start us, length us, event | category | flops | bytes accessed | tf_op | source)
XLA Modules:
  0.0 63.8 jit_solution(1427403920316798212)
XLA Ops:
  0.6 0.0 copy-start.2
  0.6 0.0 copy-start.4
  0.7 0.7 %slice.12 = bf16[3,16,128]{2,1,0:T(8,128)(2,1)S(1)} slice(bf16[3,512,128]{2,1,0:T(8,128)(2,1)} %proj_ref.3), slice={[0:3], [496:512], [0:128]} | slice | bytes 24576 | tf_op jit(solution)/shard_map/slice | solution.py:455
  1.4 0.0 copy-start.3
  1.4 4.5 %collective-permute-start = (bf16[3,16,128]{2,1,0:T(8,128)(2,1)S(1)}, bf16[3,16,128]{2,1,0:T(8,128)(2,1)S(1)}, u32[]{:S(2)}, u32[]{:S(2)}) collective-permute-start(bf16[3,16,128]{2,1,0:T(8,128)(2,1)S(1)} %slice.12), channel_id=1, source_target_pairs={{0,32},{32,64},{64,96},{96,128},{128,160},{160,192},{192,224},{224... | collective-permute-start | bytes 36872 | tf_op jit(solution)/shard_map/ppermute | solution.py:454
  5.9 0.0 copy-done.2
  5.9 0.0 copy-done.4
  5.9 0.0 copy-done.3
  5.9 1.8 %prepare.1 = (f32[2,512,128]{2,1,0:T(8,128)S(1)}, f32[2,128,512]{2,1,0:T(8,128)S(1)}, f32[2,16,512]{2,1,0:T(8,128)S(1)}, f32[2,16,128]{2,1,0:T(8,128)S(1)}, f32[...) custom-call(f32[3,7,128]{2,1,0:T(8,128)S(1)} %copy-done.2, f32[8,16]{1,0:T(8,128)S(1)} %copy-done.3, ...), custom_call_target="tpu_custom_call" | custom-call | flops 3000000000 | bytes 9000000 | tf_op jit(solution)/shard_map/prepare/pallas_call | solution.py:457
  7.7 0.0 collective-permute-done.before_ref
  7.7 0.1 patch.1
  7.8 0.7 %select_convert_fusion = f16[16,24,128]{2,1,0:T(8,128)(2,1)} fusion(f32[24,128]{1,0:T(8,128)S(1)} %get-tuple-element.39, f32[24,128]{1,0:T(8,128)S(1)} %get-tuple-element.38, pred[16]{0:T(512)(128)(4,1)S(1)} %fusion), kind=kLoop, calls=%fused_computation | loop fusion | flops 98304 | bytes 122896 | tf_op jit(solution)/shard_map/convert_element_type | solution.py:474
  8.6 17.3 %all-to-all-start = ((f16[16,24,128]{2,1,0:T(8,128)(2,1)}), f16[16,24,128]{2,1,0:T(8,128)(2,1)S(1)}, u32[]{:S(2)}, u32[]{:S(2)}) async-start(f16[16,24,128]{2,1,0:T(8,128)(2,1)} %select_convert_fusion), calls=%async_computation | async-start | bytes 196608 | tf_op jit(solution)/shard_map/all_to_all | solution.py:447
  25.9 0.0 copy-start
  25.9 3.9 %within.1.near_ref = f32[1240,128]{1,0:T(8,128)S(1)} custom-call(f32[2,8,16]{2,1,0:T(8,128)S(1)} %get-tuple-element.25.table_ref, f32[2,128,512]{2,1,0:T(8,128)S(1)} %get-tuple-element.26.pair_ref, f32[2,16,512]{2,1,0:T(8,128)S(1)} %get-tuple-element.27.states_ref, f32[4,8,128]{2,1,0:T(8,128)S(1)} %get-tuple-element.28.patch_ref, ...), custom_call_target="tpu_custom_call" | custom-call | flops 8000000000 | bytes 24000000 | tf_op jit(solution)/shard_map/within/pallas_call | solution.py:476
  29.8 0.0 copy-start.1
  29.8 0.0 all-to-all-done
  29.9 0.0 copy-done
  29.9 0.9 %copy-done.1 = bf16[512,128]{1,0:T(8,128)(2,1)S(1)} copy-done((bf16[512,128]{1,0:T(8,128)(2,1)S(1)}, bf16[512,128]{1,0:T(8,128)(2,1)}, u32[]{:S(2)}) %copy-start.1) | copy-done | bytes 131096
  30.7 1.2 %across.1 = (f32[3,512,128]{2,1,0:T(8,128)S(1)}, f32[24,128]{1,0:T(8,128)S(1)}) custom-call(s32[1]{0:T(128)} %bitcast.me_ref, f32[16,24,128]{2,1,0:T(8,128)S(1)} %convert_element_type.13.arrived_ref, f32[2,8,16]{2,1,0:T(8,128)S(1)} %get-tuple-element.25.table_ref, f32[1240,128]{1,0:T(8,128)S(1)} %within.1.near_ref, ...), custom_call_target="tpu_custom_call" | custom-call | flops 4000000000 | bytes 12000000 | tf_op jit(solution)/shard_map/across/pallas_call | solution.py:482
  31.9 0.7 %broadcast_in_dim.22 = f16[16,24,128]{2,1,0:T(8,128)(2,1)} broadcast(f16[24,128]{1,0:T(8,128)(2,1)S(1)} %convert_element_type.14), dimensions={1,2} | broadcast | bytes 104448 | tf_op jit(solution)/shard_map/broadcast_in_dim | solution.py:491
  32.6 11.5 %all-to-all-start.1 = ((f16[16,24,128]{2,1,0:T(8,128)(2,1)}), f16[16,24,128]{2,1,0:T(8,128)(2,1)S(1)}, u32[]{:S(2)}, u32[]{:S(2)}) async-start(f16[16,24,128]{2,1,0:T(8,128)(2,1)} %broadcast_in_dim.22), calls=%async_computation.1 | async-start | bytes 196608 | tf_op jit(solution)/shard_map/all_to_all | solution.py:447
  44.1 1.3 %collective-permute-start.1 = (f32[3,8,128]{2,1,0:T(8,128)S(1)}, f32[3,8,128]{2,1,0:T(8,128)S(1)}, u32[]{:S(2)}, u32[]{:S(2)}) collective-permute-start(f32[3,8,128]{2,1,0:T(8,128)S(1)} %slice.15), channel_id=1, source_target_pairs={{32,0},{64,32},{96,64},{128,96},{160,128},{192,160},{224,192},{256... | collective-permute-start | bytes 36872 | tf_op jit(solution)/shard_map/ppermute | solution.py:488
  45.4 2.5 %all-to-all-done.1 = f16[16,24,128]{2,1,0:T(8,128)(2,1)S(1)} async-done(((f16[16,24,128]{2,1,0:T(8,128)(2,1)}), f16[16,24,128]{2,1,0:T(8,128)(2,1)S(1)}, u32[]{:S(2)}, u32[]{:S(2)}) %all-to-all-start.1) | async-done | bytes 98336 | tf_op jit(solution)/shard_map/all_to_all | solution.py:447
  47.9 0.6 %total.1 = (f32[24,128]{1,0:T(8,128)S(1)}, f32[32,1,128]{2,1,0:T(1,128)}) custom-call(f32[16,24,128]{2,1,0:T(8,128)S(1)} %convert_element_type.15.stats_ref), custom_call_target="tpu_custom_call" | custom-call | flops 1000000000 | bytes 3000000 | tf_op jit(solution)/shard_map/total/pallas_call | solution.py:497
  48.6 12.4 %all-to-all-start.2 = ((f32[32,1,128]{2,1,0:T(1,128)}), f32[32,1,128]{2,1,0:T(1,128)S(1)}, u32[]{:S(2)}, u32[]{:S(2)}) async-start(f32[32,1,128]{2,1,0:T(1,128)} %get-tuple-element.33), calls=%async_computation.2 | async-start | bytes 32768 | tf_op jit(solution)/shard_map/all_to_all | solution.py:447
  61.0 0.0 collective-permute-done.1.after_ref
  61.0 1.2 %inputs.1 = bf16[3,512,128]{2,1,0:T(8,128)(2,1)} custom-call(f32[3,512,128]{2,1,0:T(8,128)S(1)} %get-tuple-element.31.feature_ref, f32[3,8,128]{2,1,0:T(8,128)S(1)} %collective-permute-done.1.after_ref, f32[3,7,128]{2,1,0:T(8,128)S(1)} %copy-done.2), custom_call_target="tpu_custom_call" | custom-call | flops 2000000000 | bytes 6000000 | tf_op jit(solution)/shard_map/inputs/pallas_call | solution.py:493
  62.2 0.8 %all-to-all-done.2.square_ref = f32[32,1,128]{2,1,0:T(1,128)S(1)} async-done(((f32[32,1,128]{2,1,0:T(1,128)}), f32[32,1,128]{2,1,0:T(1,128)S(1)}, u32[]{:S(2)}, u32[]{:S(2)}) %all-to-all-start.2) | async-done | bytes 16416 | tf_op jit(solution)/shard_map/all_to_all | solution.py:447
  63.0 0.8 %scale.1 = (f32[3,7,128]{2,1,0:T(8,128)}, f32[8,16]{1,0:T(8,128)}, f32[8,16]{1,0:T(8,128)}) custom-call(f32[32,1,128]{2,1,0:T(1,128)S(1)} %all-to-all-done.2.square_ref, f32[24,128]{1,0:T(8,128)S(1)} %get-tuple-element.34.total_ref), custom_call_target="tpu_custom_call" | custom-call | flops 1000000000 | bytes 3000000 | tf_op jit(solution)/shard_map/scale/pallas_call | solution.py:501
  (6 shorter events, 0.1 us)
Async XLA Ops:
  0.6 5.3 %copy-start.2 = (f32[3,7,128]{2,1,0:T(8,128)S(1)}, f32[3,7,128]{2,1,0:T(8,128)}, u32[]{:S(2)}) copy-start(f32[3,7,128]{2,1,0:T(8,128)} %weight_ref.5) | copy-start | bytes 32260
  0.6 5.3 %copy-start.4 = (f32[8,16]{1,0:T(8,128)S(1)}, f32[8,16]{1,0:T(8,128)}, u32[]{:S(2)}) copy-start(f32[8,16]{1,0:T(8,128)} %residue_ref.1) | copy-start | bytes 1540
  1.4 4.5 %copy-start.3 = (f32[8,16]{1,0:T(8,128)S(1)}, f32[8,16]{1,0:T(8,128)}, u32[]{:S(2)}) copy-start(f32[8,16]{1,0:T(8,128)} %rate_ref.1) | copy-start | bytes 1540
  1.4 6.3 %collective-permute-start = (bf16[3,16,128]{2,1,0:T(8,128)(2,1)S(1)}, bf16[3,16,128]{2,1,0:T(8,128)(2,1)S(1)}, u32[]{:S(2)}, u32[]{:S(2)}) collective-permute-start(bf16[3,16,128]{2,1,0:T(8,128)(2,1)S(1)} %slice.12), channel_id=1, source_target_pairs={{0,32},{32,64},{64,96},{96,128},{128,160},{160,192},{192,224},{224... | collective-permute-start | bytes 36872 | tf_op jit(solution)/shard_map/ppermute | solution.py:454
  8.6 21.3 %all-to-all-start = ((f16[16,24,128]{2,1,0:T(8,128)(2,1)}), f16[16,24,128]{2,1,0:T(8,128)(2,1)S(1)}, u32[]{:S(2)}, u32[]{:S(2)}) async-start(f16[16,24,128]{2,1,0:T(8,128)(2,1)} %select_convert_fusion), calls=%async_computation | async-start | bytes 196608 | tf_op jit(solution)/shard_map/all_to_all | solution.py:447
  25.9 4.0 %copy-start = (bf16[3,512,128]{2,1,0:T(8,128)(2,1)S(1)}, bf16[3,512,128]{2,1,0:T(8,128)(2,1)}, u32[]{:S(2)}) copy-start(bf16[3,512,128]{2,1,0:T(8,128)(2,1)} %proj_ref.3) | copy-start | bytes 1179652
  29.8 0.9 %copy-start.1 = (bf16[512,128]{1,0:T(8,128)(2,1)S(1)}, bf16[512,128]{1,0:T(8,128)(2,1)}, u32[]{:S(2)}) copy-start(bf16[512,128]{1,0:T(8,128)(2,1)} %out_grad_ref.3) | copy-start | bytes 393220
  32.6 15.3 %all-to-all-start.1 = ((f16[16,24,128]{2,1,0:T(8,128)(2,1)}), f16[16,24,128]{2,1,0:T(8,128)(2,1)S(1)}, u32[]{:S(2)}, u32[]{:S(2)}) async-start(f16[16,24,128]{2,1,0:T(8,128)(2,1)} %broadcast_in_dim.22), calls=%async_computation.1 | async-start | bytes 196608 | tf_op jit(solution)/shard_map/all_to_all | solution.py:447
  44.1 16.9 %collective-permute-start.1 = (f32[3,8,128]{2,1,0:T(8,128)S(1)}, f32[3,8,128]{2,1,0:T(8,128)S(1)}, u32[]{:S(2)}, u32[]{:S(2)}) collective-permute-start(f32[3,8,128]{2,1,0:T(8,128)S(1)} %slice.15), channel_id=1, source_target_pairs={{32,0},{64,32},{96,64},{128,96},{160,128},{192,160},{224,192},{256... | collective-permute-start | bytes 36872 | tf_op jit(solution)/shard_map/ppermute | solution.py:488
  48.6 14.4 %all-to-all-start.2 = ((f32[32,1,128]{2,1,0:T(1,128)}), f32[32,1,128]{2,1,0:T(1,128)S(1)}, u32[]{:S(2)}, u32[]{:S(2)}) async-start(f32[32,1,128]{2,1,0:T(1,128)} %get-tuple-element.33), calls=%async_computation.2 | async-start | bytes 32768 | tf_op jit(solution)/shard_map/all_to_all | solution.py:447

commit v7 on v6

--- a/solution.py
+++ b/solution.py
@@ -19,7 +19,9 @@
 LEAD = 16
 HEAD = 8
 STATS = 24
-LOCAL = (2 * CHUNKS + 5) * MODES
+FACTOR = 2 * CHUNKS + 5
+LOCAL = (FACTOR + CHUNKS) * MODES
+POWER = FACTOR + CHUNKS + 1
 
 F32 = jnp.float32
 BF16 = jnp.bfloat16
@@ -212,8 +214,8 @@
     return jnp.concatenate([top, wide_ref[HEAD:, :]], axis=0)
 
 
-def middle_kernel(table_ref, pair_ref, states_ref, patch_ref, delta_ref,
-                  near_ref, lag_ref):
+def middle_kernel(me_ref, table_ref, pair_ref, states_ref, patch_ref, delta_ref,
+                  near_ref, halves_ref, lag_ref):
     long_ref, gated_ref, small_ref = near_parts(near_ref)
     gi_ref, gl_ref = pair_ref.at[0], pair_ref.at[1]
     rates = table_ref[0]
@@ -265,9 +267,11 @@
     residue_sums = lax.dot_general(lag_grad, powers, MM, precision=EXACT, preferred_element_type=F32)
     moment_sums = lax.dot_general(lag_grad, powers * down_lag, MM, precision=EXACT, preferred_element_type=F32)
     own_group = lane_group(GROUPS)
+    small_ref[LOCAL + 2 : LOCAL + 3, :] = -row * mode_row(table_ref[1])
     small_ref[LOCAL : LOCAL + 1, :] = jnp.sum(residue_sums * own_group, axis=0, keepdims=True)
     small_ref[LOCAL + 1 : LOCAL + 2, :] = jnp.sum(moment_sums * own_group, axis=0, keepdims=True)
     small_rates = mode_compact(rates)
+    small_residues = mode_compact(table_ref[1])
     chunk_decay = jnp.exp(-small_rates * CHUNK)
     lag_value = lag.astype(F32)
     end_moments = compact(dot3(split(descending * (CHUNK - 1 - lag_value)), gi))
@@ -284,7 +288,7 @@
             end, lead = end + delta_ref[0], lead + delta_ref[1]
         leads.append(lead)
         lead_here = chunk_lanes(lead_moments, q)
-        small_ref[piece(q), :] = state
+        small_ref[piece(q), :] = small_residues * state
         residue_part = residue_part + lead * state
         moment_part = moment_part + lead_here * state + lead * moment
         lead_moment = lead_moment + offset_decay * (lead_here + float(q * CHUNK) * lead)
@@ -293,46 +297,46 @@
         state = chunk_decay * state + end
     back = zero
     for q in reversed(range(CHUNKS)):
-        small_ref[piece(CHUNKS + q), :] = back
+        small_ref[piece(CHUNKS + q), :] = small_residues * back
         back = chunk_decay * back + leads[q]
     for at, value in enumerate((residue_part, moment_part, lead_moment, moment, back)):
         small_ref[piece(2 * CHUNKS + at), :] = value
-
-
-def finish_kernel(me_ref, arrived_ref, table_ref, near_ref,
+    factor = small_residues
+    for q in range(CHUNKS):
+        small_ref[piece(FACTOR + q), :] = factor
+        factor = factor * chunk_decay
+    count = small_ref.shape[0] // MODES - POWER
+    for at in range(count):
+        away = jnp.maximum(jnp.abs(me_ref[0] - member(at, count)) - 1, 0).astype(F32) * float(ROWS)
+        small_ref[piece(POWER + at), :] = jnp.exp(-small_rates * away)
+    steps = down.astype(F32)
+    halves_ref[0], halves_ref[1] = split(jnp.exp(-row * (steps + 1.0)))
+    halves_ref[2], halves_ref[3] = split(jnp.exp(-row * (CHUNK - 1 - steps)))
+
+
+def finish_kernel(me_ref, arrived_ref, near_ref, halves_ref,
                   kv_ref, patch_ref, out_grad_ref, proj_ref, before_ref, feature_ref, stats_ref, ext_ref):
     for i in range(3):
         ext_ref[i, 0:LEAD, :] = before_ref[i].astype(F32)
         ext_ref[i, LEAD:, :] = proj_ref[i].astype(F32)
     long_ref, gated_ref, small_ref = near_parts(near_ref)
     me = me_ref[0]
-    rates, residues = table_ref[0], table_ref[1]
-    row = mode_row(rates)
-    small_rates = mode_compact(rates)
-    small_residues = mode_compact(residues)
-    chunk_decay = jnp.exp(-small_rates * CHUNK)
     zero = jnp.zeros((MODES, CHANNELS), F32)
     state_in, late_in, back_in = zero, zero, zero
     for at in range(arrived_ref.shape[0]):
         d = member(at, arrived_ref.shape[0])
         away = (jnp.abs(me - d) - 1).astype(F32) * float(ROWS)
         scale = jnp.exp2(arrived_ref[at, MODES : MODES + 1, :])
-        term = jnp.exp(-small_rates * away) * (arrived_ref[at, 0:MODES, :] * scale)
+        term = small_ref[piece(POWER + at), :] * (arrived_ref[at, 0:MODES, :] * scale)
         state_in = state_in + jnp.where(d < me, term, 0.0)
         late_in = late_in + jnp.where(d < me, term * away, 0.0)
         back_in = back_in + jnp.where(d > me, term, 0.0)
     states, backs = [], []
-    carried = state_in
     for q in range(CHUNKS):
-        states.append(small_residues * (small_ref[piece(q), :] + carried))
-        carried = carried * chunk_decay
-    carried = back_in
-    for q in reversed(range(CHUNKS)):
-        backs.insert(0, small_residues * (small_ref[piece(CHUNKS + q), :] + carried))
-        carried = carried * chunk_decay
-    down = iota((CHUNK, CHANNELS), 0).astype(F32)
-    long_far = dot3(split(jnp.exp(-row * (down + 1.0))), expand(jnp.concatenate(states, axis=1)))
-    gated_far = dot3(split(jnp.exp(-row * (CHUNK - 1 - down))), expand(jnp.concatenate(backs, axis=1)))
+        states.append(small_ref[piece(q), :] + small_ref[piece(FACTOR + q), :] * state_in)
+        backs.append(small_ref[piece(CHUNKS + q), :] + small_ref[piece(FACTOR + CHUNKS - 1 - q), :] * back_in)
+    long_far = dot3((halves_ref[0], halves_ref[1]), expand(jnp.concatenate(states, axis=1)))
+    gated_far = dot3((halves_ref[2], halves_ref[3]), expand(jnp.concatenate(backs, axis=1)))
     sums = [jnp.zeros((8, CHANNELS), F32) for _ in range(3 * KW)]
     for q in range(CHUNKS):
         rows = pl.ds(q * CHUNK, CHUNK)
@@ -368,7 +372,7 @@
 
     residue_row = small_ref[LOCAL : LOCAL + 1, :] + by_mode(residue_part)
     moment_row = small_ref[LOCAL + 1 : LOCAL + 2, :] + by_mode(moment_part)
-    rate_row = -row * mode_row(residues) * moment_row
+    rate_row = small_ref[LOCAL + 2 : LOCAL + 3, :] * moment_row
     lines = [jnp.sum(part, axis=0, keepdims=True) for part in sums]
     stats = jnp.concatenate(lines + [residue_row, rate_row, jnp.zeros((1, CHANNELS), F32)], axis=0)
     scaled, exponent = scaled_columns(stats)
@@ -473,18 +477,18 @@
     later = member(lax.broadcasted_iota(jnp.int32, (ctx, 1, 1), 0), ctx) > me.reshape(1, 1, 1)
     send = jnp.where(later, send[1], send[0]).astype(F16)
     arrived = exchange(send, "ctx", ctx // 2).astype(F32)
-    near = call(
+    near, halves = call(
         middle_kernel, "within",
-        shape(2 * ROWS + LOCAL + 8, CHANNELS),
-        [VMEM] * 5, 8,
+        (shape(2 * ROWS + (POWER + ctx) * MODES, CHANNELS), shape(4, CHUNK, CHANNELS, dtype=BF16)),
+        [SMEM] + [VMEM] * 5, 8,
         scratch=[pltpu.VMEM((GROUPS, CHANNELS), F32)],
-    )(table, pair, states, patch, delta)
+    )(me, table, pair, states, patch, delta)
     grad_feature, stats = call(
         finish_kernel, "across",
         (shape(3, ROWS, CHANNELS), shape(STATS, CHANNELS)),
         [SMEM] + [VMEM] * 8, 4,
         scratch=[pltpu.VMEM((3, LEAD + ROWS, CHANNELS), F32)],
-    )(me, arrived, table, near, kv, patch, grad_out, projected, before)
+    )(me, arrived, near, halves, kv, patch, grad_out, projected, before)
     after = lax.ppermute(
         grad_feature[:, :8, :], "ctx", [(source + 1, source) for source in range(ctx - 1)]
     )

time: 64.2 us -> 64.1 us (level)
  no operation moved by 1% of the time
where the time goes in v7:
time: 64.1 us; the launch traced here: 63.7 us
  starting transfers between devices  47 us (73%)
  Pallas kernels  9.57 us (15%)
  waiting for transfers between devices  3.29 us (5%)
  local copies, waits for them, and re-layouts  2.28 us (4%)
  between operations  0.8 us (1%)
  other arithmetic  0.78 us (1%)
    all_to_all x3, starting transfers between devices, exchange(): lax.all_to_all(blocks, axis, 0, 0, axis_index_groups=[[(first + p) % coun...  41.2 us
    ppermute x1, starting transfers between devices, shards(): lax.ppermute(projected[:, ROWS - LEAD:, :], 'ctx', [(source, source + 1)...  4.49 us
    pallas_call x1, Pallas kernels, shards(): call(middle_kernel, 'within', (shape(2 * ROWS + (POWER + ctx) * MODES, CH...  3.99 us
    all_to_all x3, waiting for transfers between devices, exchange(): lax.all_to_all(blocks, axis, 0, 0, axis_index_groups=[[(first + p) % coun...  3.28 us
    pallas_call x1, Pallas kernels, shards(): call(prepare_kernel, 'prepare', (shape(2, ROWS, CHANNELS), shape(2, CHUNK...  1.79 us
    ppermute x1, starting transfers between devices, shards(): lax.ppermute(grad_feature[:, :8, :], 'ctx', [(source + 1, source) for sou...  1.29 us
  transfers between devices with their start and end apart: 5, of which 2 were waited for; matrix products, arithmetic and copies ran while one was open for 0% of the time, Pallas kernels for 12%

profile of v7, /device:TPU:1, one launch (start us, length us, event | category | flops | bytes accessed | tf_op | source)
XLA Modules:
  0.0 63.7 jit_solution(10341807382781380796)
XLA Ops:
  0.6 0.0 copy-start.2
  0.6 0.0 copy-start.4
  0.7 0.7 %slice.12 = bf16[3,16,128]{2,1,0:T(8,128)(2,1)S(1)} slice(bf16[3,512,128]{2,1,0:T(8,128)(2,1)} %proj_ref.3), slice={[0:3], [496:512], [0:128]} | slice | bytes 24576 | tf_op jit(solution)/shard_map/slice | solution.py:459
  1.4 0.0 copy-start.3
  1.4 4.5 %collective-permute-start = (bf16[3,16,128]{2,1,0:T(8,128)(2,1)S(1)}, bf16[3,16,128]{2,1,0:T(8,128)(2,1)S(1)}, u32[]{:S(2)}, u32[]{:S(2)}) collective-permute-start(bf16[3,16,128]{2,1,0:T(8,128)(2,1)S(1)} %slice.12), channel_id=1, source_target_pairs={{0,32},{32,64},{64,96},{96,128},{128,160},{160,192},{192,224},{224... | collective-permute-start | bytes 36872 | tf_op jit(solution)/shard_map/ppermute | solution.py:458
  5.9 0.0 copy-done.2
  5.9 0.0 copy-done.4
  5.9 0.0 copy-done.3
  5.9 1.8 %prepare.1 = (f32[2,512,128]{2,1,0:T(8,128)S(1)}, f32[2,128,512]{2,1,0:T(8,128)S(1)}, f32[2,16,512]{2,1,0:T(8,128)S(1)}, f32[2,16,128]{2,1,0:T(8,128)S(1)}, f32[...) custom-call(f32[3,7,128]{2,1,0:T(8,128)S(1)} %copy-done.2, f32[8,16]{1,0:T(8,128)S(1)} %copy-done.3, ...), custom_call_target="tpu_custom_call" | custom-call | flops 3000000000 | bytes 9000000 | tf_op jit(solution)/shard_map/prepare/pallas_call | solution.py:461
  7.7 0.0 collective-permute-done.before_ref
  7.7 0.1 patch.1
  7.8 0.7 %select_convert_fusion = f16[16,24,128]{2,1,0:T(8,128)(2,1)} fusion(f32[24,128]{1,0:T(8,128)S(1)} %get-tuple-element.43, f32[24,128]{1,0:T(8,128)S(1)} %get-tuple-element.42, pred[16]{0:T(512)(128)(4,1)S(1)} %fusion), kind=kLoop, calls=%fused_computation | loop fusion | flops 98304 | bytes 122896 | tf_op jit(solution)/shard_map/convert_element_type | solution.py:478
  8.6 17.3 %all-to-all-start = ((f16[16,24,128]{2,1,0:T(8,128)(2,1)}), f16[16,24,128]{2,1,0:T(8,128)(2,1)S(1)}, u32[]{:S(2)}, u32[]{:S(2)}) async-start(f16[16,24,128]{2,1,0:T(8,128)(2,1)} %select_convert_fusion), calls=%async_computation | async-start | bytes 196608 | tf_op jit(solution)/shard_map/all_to_all | solution.py:451
  25.9 0.0 copy-start
  25.9 4.0 %within.1 = (f32[1568,128]{1,0:T(8,128)S(1)}, bf16[4,128,128]{2,1,0:T(8,128)(2,1)S(1)}) custom-call(s32[1]{0:T(128)} %bitcast.me_ref, f32[2,8,16]{2,1,0:T(8,128)S(1)} %get-tuple-element.27.table_ref, f32[2,128,512]{2,1,0:T(8,128)S(1)} %get-tuple-element.28.pair_ref, f32[2,16,512]{2,1,0:T(8,128)S(1)} %get-tuple-element.29.states_ref, ...), custom_call_target="tpu_custom_call" | custom-call | flops 8000000000 | bytes 24000000 | tf_op jit(solution)/shard_map/within/pallas_call | solution.py:480
  29.9 0.0 copy-start.1
  29.9 0.0 all-to-all-done
  29.9 0.0 copy-done
  29.9 0.9 %copy-done.1 = bf16[512,128]{1,0:T(8,128)(2,1)S(1)} copy-done((bf16[512,128]{1,0:T(8,128)(2,1)S(1)}, bf16[512,128]{1,0:T(8,128)(2,1)}, u32[]{:S(2)}) %copy-start.1) | copy-done | bytes 131096
  30.8 1.0 %across.1 = (f32[3,512,128]{2,1,0:T(8,128)S(1)}, f32[24,128]{1,0:T(8,128)S(1)}) custom-call(s32[1]{0:T(128)} %bitcast.me_ref, f32[16,24,128]{2,1,0:T(8,128)S(1)} %convert_element_type.13.arrived_ref, f32[1568,128]{1,0:T(8,128)S(1)} %get-tuple-element.32.near_ref, bf16[4,128,128]{2,1,0:T(8,128)(2,1)S(1)} %get-tuple-element.33.halves_ref, ...), custom_call_target="tpu_custom_call" | custom-call | flops 4000000000 | bytes 12000000 | tf_op jit(solution)/shard_map/across/pallas_call | solution.py:486
  31.8 0.7 %broadcast_in_dim.22 = f16[16,24,128]{2,1,0:T(8,128)(2,1)} broadcast(f16[24,128]{1,0:T(8,128)(2,1)S(1)} %convert_element_type.14), dimensions={1,2} | broadcast | bytes 104448 | tf_op jit(solution)/shard_map/broadcast_in_dim | solution.py:495
  32.5 11.5 %all-to-all-start.1 = ((f16[16,24,128]{2,1,0:T(8,128)(2,1)}), f16[16,24,128]{2,1,0:T(8,128)(2,1)S(1)}, u32[]{:S(2)}, u32[]{:S(2)}) async-start(f16[16,24,128]{2,1,0:T(8,128)(2,1)} %broadcast_in_dim.22), calls=%async_computation.1 | async-start | bytes 196608 | tf_op jit(solution)/shard_map/all_to_all | solution.py:451
  44.0 1.3 %collective-permute-start.1 = (f32[3,8,128]{2,1,0:T(8,128)S(1)}, f32[3,8,128]{2,1,0:T(8,128)S(1)}, u32[]{:S(2)}, u32[]{:S(2)}) collective-permute-start(f32[3,8,128]{2,1,0:T(8,128)S(1)} %slice.15), channel_id=1, source_target_pairs={{32,0},{64,32},{96,64},{128,96},{160,128},{192,160},{224,192},{256... | collective-permute-start | bytes 36872 | tf_op jit(solution)/shard_map/ppermute | solution.py:492
  45.3 2.5 %all-to-all-done.1 = f16[16,24,128]{2,1,0:T(8,128)(2,1)S(1)} async-done(((f16[16,24,128]{2,1,0:T(8,128)(2,1)}), f16[16,24,128]{2,1,0:T(8,128)(2,1)S(1)}, u32[]{:S(2)}, u32[]{:S(2)}) %all-to-all-start.1) | async-done | bytes 98336 | tf_op jit(solution)/shard_map/all_to_all | solution.py:451
  47.8 0.6 %total.1 = (f32[24,128]{1,0:T(8,128)S(1)}, f32[32,1,128]{2,1,0:T(1,128)}) custom-call(f32[16,24,128]{2,1,0:T(8,128)S(1)} %convert_element_type.15.stats_ref), custom_call_target="tpu_custom_call" | custom-call | flops 1000000000 | bytes 3000000 | tf_op jit(solution)/shard_map/total/pallas_call | solution.py:501
  48.5 12.4 %all-to-all-start.2 = ((f32[32,1,128]{2,1,0:T(1,128)}), f32[32,1,128]{2,1,0:T(1,128)S(1)}, u32[]{:S(2)}, u32[]{:S(2)}) async-start(f32[32,1,128]{2,1,0:T(1,128)} %get-tuple-element.37), calls=%async_computation.2 | async-start | bytes 32768 | tf_op jit(solution)/shard_map/all_to_all | solution.py:451
  60.9 0.0 collective-permute-done.1.after_ref
  60.9 1.2 %inputs.1 = bf16[3,512,128]{2,1,0:T(8,128)(2,1)} custom-call(f32[3,512,128]{2,1,0:T(8,128)S(1)} %get-tuple-element.35.feature_ref, f32[3,8,128]{2,1,0:T(8,128)S(1)} %collective-permute-done.1.after_ref, f32[3,7,128]{2,1,0:T(8,128)S(1)} %copy-done.2), custom_call_target="tpu_custom_call" | custom-call | flops 2000000000 | bytes 6000000 | tf_op jit(solution)/shard_map/inputs/pallas_call | solution.py:497
  62.1 0.8 %all-to-all-done.2.square_ref = f32[32,1,128]{2,1,0:T(1,128)S(1)} async-done(((f32[32,1,128]{2,1,0:T(1,128)}), f32[32,1,128]{2,1,0:T(1,128)S(1)}, u32[]{:S(2)}, u32[]{:S(2)}) %all-to-all-start.2) | async-done | bytes 16416 | tf_op jit(solution)/shard_map/all_to_all | solution.py:451
  62.8 0.8 %scale.1 = (f32[3,7,128]{2,1,0:T(8,128)}, f32[8,16]{1,0:T(8,128)}, f32[8,16]{1,0:T(8,128)}) custom-call(f32[32,1,128]{2,1,0:T(1,128)S(1)} %all-to-all-done.2.square_ref, f32[24,128]{1,0:T(8,128)S(1)} %get-tuple-element.38.total_ref), custom_call_target="tpu_custom_call" | custom-call | flops 1000000000 | bytes 3000000 | tf_op jit(solution)/shard_map/scale/pallas_call | solution.py:505
  (6 shorter events, 0.1 us)
Async XLA Ops:
  0.6 5.3 %copy-start.2 = (f32[3,7,128]{2,1,0:T(8,128)S(1)}, f32[3,7,128]{2,1,0:T(8,128)}, u32[]{:S(2)}) copy-start(f32[3,7,128]{2,1,0:T(8,128)} %weight_ref.5) | copy-start | bytes 32260
  0.6 5.3 %copy-start.4 = (f32[8,16]{1,0:T(8,128)S(1)}, f32[8,16]{1,0:T(8,128)}, u32[]{:S(2)}) copy-start(f32[8,16]{1,0:T(8,128)} %residue_ref.1) | copy-start | bytes 1540
  1.4 4.5 %copy-start.3 = (f32[8,16]{1,0:T(8,128)S(1)}, f32[8,16]{1,0:T(8,128)}, u32[]{:S(2)}) copy-start(f32[8,16]{1,0:T(8,128)} %rate_ref.1) | copy-start | bytes 1540
  1.4 6.3 %collective-permute-start = (bf16[3,16,128]{2,1,0:T(8,128)(2,1)S(1)}, bf16[3,16,128]{2,1,0:T(8,128)(2,1)S(1)}, u32[]{:S(2)}, u32[]{:S(2)}) collective-permute-start(bf16[3,16,128]{2,1,0:T(8,128)(2,1)S(1)} %slice.12), channel_id=1, source_target_pairs={{0,32},{32,64},{64,96},{96,128},{128,160},{160,192},{192,224},{224... | collective-permute-start | bytes 36872 | tf_op jit(solution)/shard_map/ppermute | solution.py:458
  8.6 21.3 %all-to-all-start = ((f16[16,24,128]{2,1,0:T(8,128)(2,1)}), f16[16,24,128]{2,1,0:T(8,128)(2,1)S(1)}, u32[]{:S(2)}, u32[]{:S(2)}) async-start(f16[16,24,128]{2,1,0:T(8,128)(2,1)} %select_convert_fusion), calls=%async_computation | async-start | bytes 196608 | tf_op jit(solution)/shard_map/all_to_all | solution.py:451
  25.9 4.1 %copy-start = (bf16[3,512,128]{2,1,0:T(8,128)(2,1)S(1)}, bf16[3,512,128]{2,1,0:T(8,128)(2,1)}, u32[]{:S(2)}) copy-start(bf16[3,512,128]{2,1,0:T(8,128)(2,1)} %proj_ref.3) | copy-start | bytes 1179652
  29.9 0.9 %copy-start.1 = (bf16[512,128]{1,0:T(8,128)(2,1)S(1)}, bf16[512,128]{1,0:T(8,128)(2,1)}, u32[]{:S(2)}) copy-start(bf16[512,128]{1,0:T(8,128)(2,1)} %out_grad_ref.3) | copy-start | bytes 393220
  32.5 15.3 %all-to-all-start.1 = ((f16[16,24,128]{2,1,0:T(8,128)(2,1)}), f16[16,24,128]{2,1,0:T(8,128)(2,1)S(1)}, u32[]{:S(2)}, u32[]{:S(2)}) async-start(f16[16,24,128]{2,1,0:T(8,128)(2,1)} %broadcast_in_dim.22), calls=%async_computation.1 | async-start | bytes 196608 | tf_op jit(solution)/shard_map/all_to_all | solution.py:451
  44.0 16.9 %collective-permute-start.1 = (f32[3,8,128]{2,1,0:T(8,128)S(1)}, f32[3,8,128]{2,1,0:T(8,128)S(1)}, u32[]{:S(2)}, u32[]{:S(2)}) collective-permute-start(f32[3,8,128]{2,1,0:T(8,128)S(1)} %slice.15), channel_id=1, source_target_pairs={{32,0},{64,32},{96,64},{128,96},{160,128},{192,160},{224,192},{256... | collective-permute-start | bytes 36872 | tf_op jit(solution)/shard_map/ppermute | solution.py:492
  48.5 14.4 %all-to-all-start.2 = ((f32[32,1,128]{2,1,0:T(1,128)}), f32[32,1,128]{2,1,0:T(1,128)S(1)}, u32[]{:S(2)}, u32[]{:S(2)}) async-start(f32[32,1,128]{2,1,0:T(1,128)} %get-tuple-element.37), calls=%async_computation.2 | async-start | bytes 32768 | tf_op jit(solution)/shard_map/all_to_all | solution.py:451

commit v8 on v7

--- a/solution.py
+++ b/solution.py
@@ -380,7 +380,11 @@
     stats_ref[...] = jnp.where(last, exponent, scaled)
 
 
-def inputs_kernel(feature_ref, after_ref, weight_ref, out_ref, ext_ref):
+def inputs_kernel(feature_ref, after_ref, weight_ref, total_ref, out_ref, table_ref, ext_ref):
+    pick = (iota((MODES, CHANNELS), 1) % MODES == iota((MODES, CHANNELS), 0)).astype(F32)
+    for at in range(2):
+        line = total_ref[3 * KW + at : 3 * KW + at + 1, :] * lane_group(GROUPS)
+        table_ref[at] = lax.dot_general(line, pick, NT, precision=EXACT, preferred_element_type=F32)
     for i in range(3):
         ext_ref[0:ROWS, :] = feature_ref[i]
         ext_ref[ROWS:, :] = after_ref[i]
@@ -403,21 +407,13 @@
         square_ref[d] = jnp.broadcast_to(square, square_ref.shape[1:])
 
 
-def scale_kernel(square_ref, total_ref, conv_ref, residue_ref, rate_ref):
+def scale_kernel(square_ref, total_ref, table_ref, conv_ref, residue_ref, rate_ref):
     squares = jnp.sum(jnp.sum(square_ref[:, 0, :], axis=0, keepdims=True), axis=1, keepdims=True)
     factor = jnp.minimum(1.0, lax.rsqrt(squares / (3 * KW * D + 2 * G * MODES) + 1e-6))
-    total = total_ref[...] * factor
     for i in range(3):
-        conv_ref[i] = total[i * KW : (i + 1) * KW, :]
-    pick = (iota((MODES, CHANNELS), 1) % MODES == iota((MODES, CHANNELS), 0)).astype(F32)
-    own = lane_group(GROUPS)
-    at = 3 * KW
-    residue_ref[...] = lax.dot_general(
-        total[at : at + 1, :] * own, pick, NT, precision=EXACT, preferred_element_type=F32
-    )
-    rate_ref[...] = lax.dot_general(
-        total[at + 1 : at + 2, :] * own, pick, NT, precision=EXACT, preferred_element_type=F32
-    )
+        conv_ref[i] = total_ref[i * KW : (i + 1) * KW, :] * factor
+    residue_ref[...] = table_ref[0] * factor
+    rate_ref[...] = table_ref[1] * factor
 
 
 def shape(*dims, dtype=F32):
@@ -493,19 +489,20 @@
         grad_feature[:, :8, :], "ctx", [(source + 1, source) for source in range(ctx - 1)]
     )
     stats = jnp.broadcast_to(stats.astype(F16), (ctx, STATS, CHANNELS))
-    gathered = exchange(stats, "ctx", ctx // 2).astype(F32)
-    grad_projected = call(
-        inputs_kernel, "inputs", shape(3, ROWS, CHANNELS, dtype=BF16), [VMEM] * 3, 2,
-        scratch=[pltpu.VMEM((ROWS + 8, CHANNELS), F32)],
-    )(grad_feature, after, conv_weight)
+    gathered = exchange(stats, "ctx", ctx // 2 - 1).astype(F32)
     total, square = call(
         total_kernel, "total", (shape(STATS, CHANNELS), shape(planes, 1, CHANNELS)), [VMEM], 1,
     )(gathered)
     squares = exchange(square, "ch", planes // 2 + planes // 8)
+    grad_projected, table = call(
+        inputs_kernel, "inputs",
+        (shape(3, ROWS, CHANNELS, dtype=BF16), shape(2, GROUPS, MODES)), [VMEM] * 4, 2,
+        scratch=[pltpu.VMEM((ROWS + 8, CHANNELS), F32)],
+    )(grad_feature, after, conv_weight, total)
     grad_conv, grad_residues, grad_log_rates = call(
         scale_kernel, "scale",
-        (shape(3, KW, CHANNELS), shape(GROUPS, MODES), shape(GROUPS, MODES)), [VMEM] * 2, 1,
-    )(squares, total)
+        (shape(3, KW, CHANNELS), shape(GROUPS, MODES), shape(GROUPS, MODES)), [VMEM] * 3, 1,
+    )(squares, total, table)
     return grad_projected, grad_conv, grad_residues, grad_log_rates
 
 

time: 64.1 us -> 65.6 us (1.023)
  waiting for transfers between devices: 3.29 us -> 5.31 us
    all_to_all x3, waiting for transfers between devices: 3.28 us -> 5.31 us  [exchange(): lax.all_to_all(blocks, axis, 0, 0, axis_index_groups=[[(first + p) % coun...]
where the time goes in v8:
time: 65.6 us; the launch traced here: 65.1 us
  starting transfers between devices  46.5 us (71%)
  Pallas kernels  9.46 us (14%)
  waiting for transfers between devices  5.31 us (8%)
  local copies, waits for them, and re-layouts  2.28 us (3%)
  between operations  0.8 us (1%)
  other arithmetic  0.78 us (1%)
    all_to_all x3, starting transfers between devices, exchange(): lax.all_to_all(blocks, axis, 0, 0, axis_index_groups=[[(first + p) % coun...  40.7 us
    all_to_all x3, waiting for transfers between devices, exchange(): lax.all_to_all(blocks, axis, 0, 0, axis_index_groups=[[(first + p) % coun...  5.31 us
    ppermute x1, starting transfers between devices, shards(): lax.ppermute(projected[:, ROWS - LEAD:, :], 'ctx', [(source, source + 1)...  4.49 us
    pallas_call x1, Pallas kernels, shards(): call(middle_kernel, 'within', (shape(2 * ROWS + (POWER + ctx) * MODES, CH...  3.99 us
    pallas_call x1, Pallas kernels, shards(): call(prepare_kernel, 'prepare', (shape(2, ROWS, CHANNELS), shape(2, CHUNK...  1.79 us
  transfers between devices with their start and end apart: 5, of which 2 were waited for; matrix products, arithmetic and copies ran while one was open for 0% of the time, Pallas kernels for 12%

profile of v8, /device:TPU:1, one launch (start us, length us, event | category | flops | bytes accessed | tf_op | source)
XLA Modules:
  0.0 65.1 jit_solution(2584967177455734171)
XLA Ops:
  0.6 0.0 copy-start.2
  0.6 0.0 copy-start.4
  0.7 0.7 %slice.12 = bf16[3,16,128]{2,1,0:T(8,128)(2,1)S(1)} slice(bf16[3,512,128]{2,1,0:T(8,128)(2,1)} %proj_ref.3), slice={[0:3], [496:512], [0:128]} | slice | bytes 24576 | tf_op jit(solution)/shard_map/slice | solution.py:455
  1.4 0.0 copy-start.3
  1.4 4.5 %collective-permute-start = (bf16[3,16,128]{2,1,0:T(8,128)(2,1)S(1)}, bf16[3,16,128]{2,1,0:T(8,128)(2,1)S(1)}, u32[]{:S(2)}, u32[]{:S(2)}) collective-permute-start(bf16[3,16,128]{2,1,0:T(8,128)(2,1)S(1)} %slice.12), channel_id=1, source_target_pairs={{0,32},{32,64},{64,96},{96,128},{128,160},{160,192},{192,224},{224... | collective-permute-start | bytes 36872 | tf_op jit(solution)/shard_map/ppermute | solution.py:454
  5.9 0.0 copy-done.2
  5.9 0.0 copy-done.4
  5.9 0.0 copy-done.3
  5.9 1.8 %prepare.1 = (f32[2,512,128]{2,1,0:T(8,128)S(1)}, f32[2,128,512]{2,1,0:T(8,128)S(1)}, f32[2,16,512]{2,1,0:T(8,128)S(1)}, f32[2,16,128]{2,1,0:T(8,128)S(1)}, f32[...) custom-call(f32[3,7,128]{2,1,0:T(8,128)S(1)} %copy-done.2, f32[8,16]{1,0:T(8,128)S(1)} %copy-done.3, ...), custom_call_target="tpu_custom_call" | custom-call | flops 3000000000 | bytes 9000000 | tf_op jit(solution)/shard_map/prepare/pallas_call | solution.py:457
  7.7 0.0 collective-permute-done.before_ref
  7.7 0.1 patch.1
  7.8 0.7 %select_convert_fusion = f16[16,24,128]{2,1,0:T(8,128)(2,1)} fusion(f32[24,128]{1,0:T(8,128)S(1)} %get-tuple-element.47, f32[24,128]{1,0:T(8,128)S(1)} %get-tuple-element.46, pred[16]{0:T(512)(128)(4,1)S(1)} %fusion), kind=kLoop, calls=%fused_computation | loop fusion | flops 98304 | bytes 122896 | tf_op jit(solution)/shard_map/convert_element_type | solution.py:474
  8.6 17.3 %all-to-all-start = ((f16[16,24,128]{2,1,0:T(8,128)(2,1)}), f16[16,24,128]{2,1,0:T(8,128)(2,1)S(1)}, u32[]{:S(2)}, u32[]{:S(2)}) async-start(f16[16,24,128]{2,1,0:T(8,128)(2,1)} %select_convert_fusion), calls=%async_computation | async-start | bytes 196608 | tf_op jit(solution)/shard_map/all_to_all | solution.py:447
  25.9 0.0 copy-start
  25.9 4.0 %within.1 = (f32[1568,128]{1,0:T(8,128)S(1)}, bf16[4,128,128]{2,1,0:T(8,128)(2,1)S(1)}) custom-call(s32[1]{0:T(128)} %bitcast.me_ref, f32[2,8,16]{2,1,0:T(8,128)S(1)} %get-tuple-element.29.table_ref, f32[2,128,512]{2,1,0:T(8,128)S(1)} %get-tuple-element.30.pair_ref, f32[2,16,512]{2,1,0:T(8,128)S(1)} %get-tuple-element.31.states_ref, ...), custom_call_target="tpu_custom_call" | custom-call | flops 8000000000 | bytes 24000000 | tf_op jit(solution)/shard_map/within/pallas_call | solution.py:476
  29.9 0.0 copy-start.1
  29.9 0.0 all-to-all-done
  29.9 0.0 copy-done
  29.9 0.9 %copy-done.1 = bf16[512,128]{1,0:T(8,128)(2,1)S(1)} copy-done((bf16[512,128]{1,0:T(8,128)(2,1)S(1)}, bf16[512,128]{1,0:T(8,128)(2,1)}, u32[]{:S(2)}) %copy-start.1) | copy-done | bytes 131096
  30.8 1.0 %across.1 = (f32[3,512,128]{2,1,0:T(8,128)S(1)}, f32[24,128]{1,0:T(8,128)S(1)}) custom-call(s32[1]{0:T(128)} %bitcast.me_ref, f32[16,24,128]{2,1,0:T(8,128)S(1)} %convert_element_type.13.arrived_ref, f32[1568,128]{1,0:T(8,128)S(1)} %get-tuple-element.34.near_ref, bf16[4,128,128]{2,1,0:T(8,128)(2,1)S(1)} %get-tuple-element.35.halves_ref, ...), custom_call_target="tpu_custom_call" | custom-call | flops 4000000000 | bytes 12000000 | tf_op jit(solution)/shard_map/across/pallas_call | solution.py:482
  31.8 0.7 %broadcast_in_dim.22 = f16[16,24,128]{2,1,0:T(8,128)(2,1)} broadcast(f16[24,128]{1,0:T(8,128)(2,1)S(1)} %convert_element_type.14), dimensions={1,2} | broadcast | bytes 104448 | tf_op jit(solution)/shard_map/broadcast_in_dim | solution.py:491
  32.5 10.4 %all-to-all-start.1 = ((f16[16,24,128]{2,1,0:T(8,128)(2,1)}), f16[16,24,128]{2,1,0:T(8,128)(2,1)S(1)}, u32[]{:S(2)}, u32[]{:S(2)}) async-start(f16[16,24,128]{2,1,0:T(8,128)(2,1)} %broadcast_in_dim.22), calls=%async_computation.1 | async-start | bytes 196608 | tf_op jit(solution)/shard_map/all_to_all | solution.py:447
  43.0 1.3 %collective-permute-start.1 = (f32[3,8,128]{2,1,0:T(8,128)S(1)}, f32[3,8,128]{2,1,0:T(8,128)S(1)}, u32[]{:S(2)}, u32[]{:S(2)}) collective-permute-start(f32[3,8,128]{2,1,0:T(8,128)S(1)} %slice.15), channel_id=1, source_target_pairs={{32,0},{64,32},{96,64},{128,96},{160,128},{192,160},{224,192},{256... | collective-permute-start | bytes 36872 | tf_op jit(solution)/shard_map/ppermute | solution.py:488
  44.3 4.6 %all-to-all-done.1 = f16[16,24,128]{2,1,0:T(8,128)(2,1)S(1)} async-done(((f16[16,24,128]{2,1,0:T(8,128)(2,1)}), f16[16,24,128]{2,1,0:T(8,128)(2,1)S(1)}, u32[]{:S(2)}, u32[]{:S(2)}) %all-to-all-start.1) | async-done | bytes 98336 | tf_op jit(solution)/shard_map/all_to_all | solution.py:447
  48.8 0.6 total.1
  49.5 12.9 %all-to-all-start.2 = ((f32[32,1,128]{2,1,0:T(1,128)}), f32[32,1,128]{2,1,0:T(1,128)S(1)}, u32[]{:S(2)}, u32[]{:S(2)}) async-start(f32[32,1,128]{2,1,0:T(1,128)} %get-tuple-element.41), calls=%async_computation.2 | async-start | bytes 32768 | tf_op jit(solution)/shard_map/all_to_all | solution.py:447
  62.4 0.0 collective-permute-done.1.after_ref
  62.5 1.2 %inputs.1 = (bf16[3,512,128]{2,1,0:T(8,128)(2,1)}, f32[2,8,16]{2,1,0:T(8,128)S(1)}) custom-call(f32[3,512,128]{2,1,0:T(8,128)S(1)} %get-tuple-element.37.feature_ref, f32[3,8,128]{2,1,0:T(8,128)S(1)} %collective-permute-done.1.after_ref, f32[3,7,128]{2,1,0:T(8,128)S(1)} %copy-done.2, f32[24,128]{1,0:T(8,128)S(1)} %get-tuple-element.39.total_ref), custom_call_target="tpu_custom_call" | custom-call | flops 2000000000 | bytes 6000000 | tf_op jit(solution)/shard_map/inputs/pallas_call | solution.py:497
  63.7 0.7 %all-to-all-done.2.square_ref = f32[32,1,128]{2,1,0:T(1,128)S(1)} async-done(((f32[32,1,128]{2,1,0:T(1,128)}), f32[32,1,128]{2,1,0:T(1,128)S(1)}, u32[]{:S(2)}, u32[]{:S(2)}) %all-to-all-start.2) | async-done | bytes 16416 | tf_op jit(solution)/shard_map/all_to_all | solution.py:447
  64.4 0.7 %scale.1 = (f32[3,7,128]{2,1,0:T(8,128)}, f32[8,16]{1,0:T(8,128)}, f32[8,16]{1,0:T(8,128)}) custom-call(f32[32,1,128]{2,1,0:T(1,128)S(1)} %all-to-all-done.2.square_ref, f32[24,128]{1,0:T(8,128)S(1)} %get-tuple-element.39.total_ref, f32[2,8,16]{2,1,0:T(8,128)S(1)} %get-tuple-element.42.table_ref), custom_call_target="tpu_custom_call" | custom-call | flops 1000000000 | bytes 3000000 | tf_op jit(solution)/shard_map/scale/pallas_call | solution.py:502
  (6 shorter events, 0.1 us)
Async XLA Ops:
  0.6 5.3 %copy-start.2 = (f32[3,7,128]{2,1,0:T(8,128)S(1)}, f32[3,7,128]{2,1,0:T(8,128)}, u32[]{:S(2)}) copy-start(f32[3,7,128]{2,1,0:T(8,128)} %weight_ref.5) | copy-start | bytes 32260
  0.6 5.3 %copy-start.4 = (f32[8,16]{1,0:T(8,128)S(1)}, f32[8,16]{1,0:T(8,128)}, u32[]{:S(2)}) copy-start(f32[8,16]{1,0:T(8,128)} %residue_ref.1) | copy-start | bytes 1540
  1.4 4.5 %copy-start.3 = (f32[8,16]{1,0:T(8,128)S(1)}, f32[8,16]{1,0:T(8,128)}, u32[]{:S(2)}) copy-start(f32[8,16]{1,0:T(8,128)} %rate_ref.1) | copy-start | bytes 1540
  1.4 6.3 %collective-permute-start = (bf16[3,16,128]{2,1,0:T(8,128)(2,1)S(1)}, bf16[3,16,128]{2,1,0:T(8,128)(2,1)S(1)}, u32[]{:S(2)}, u32[]{:S(2)}) collective-permute-start(bf16[3,16,128]{2,1,0:T(8,128)(2,1)S(1)} %slice.12), channel_id=1, source_target_pairs={{0,32},{32,64},{64,96},{96,128},{128,160},{160,192},{192,224},{224... | collective-permute-start | bytes 36872 | tf_op jit(solution)/shard_map/ppermute | solution.py:454
  8.6 21.3 %all-to-all-start = ((f16[16,24,128]{2,1,0:T(8,128)(2,1)}), f16[16,24,128]{2,1,0:T(8,128)(2,1)S(1)}, u32[]{:S(2)}, u32[]{:S(2)}) async-start(f16[16,24,128]{2,1,0:T(8,128)(2,1)} %select_convert_fusion), calls=%async_computation | async-start | bytes 196608 | tf_op jit(solution)/shard_map/all_to_all | solution.py:447
  25.9 4.1 %copy-start = (bf16[3,512,128]{2,1,0:T(8,128)(2,1)S(1)}, bf16[3,512,128]{2,1,0:T(8,128)(2,1)}, u32[]{:S(2)}) copy-start(bf16[3,512,128]{2,1,0:T(8,128)(2,1)} %proj_ref.3) | copy-start | bytes 1179652
  29.9 0.9 %copy-start.1 = (bf16[512,128]{1,0:T(8,128)(2,1)S(1)}, bf16[512,128]{1,0:T(8,128)(2,1)}, u32[]{:S(2)}) copy-start(bf16[512,128]{1,0:T(8,128)(2,1)} %out_grad_ref.3) | copy-start | bytes 393220
  32.5 16.3 %all-to-all-start.1 = ((f16[16,24,128]{2,1,0:T(8,128)(2,1)}), f16[16,24,128]{2,1,0:T(8,128)(2,1)S(1)}, u32[]{:S(2)}, u32[]{:S(2)}) async-start(f16[16,24,128]{2,1,0:T(8,128)(2,1)} %broadcast_in_dim.22), calls=%async_computation.1 | async-start | bytes 196608 | tf_op jit(solution)/shard_map/all_to_all | solution.py:447
  43.0 19.5 %collective-permute-start.1 = (f32[3,8,128]{2,1,0:T(8,128)S(1)}, f32[3,8,128]{2,1,0:T(8,128)S(1)}, u32[]{:S(2)}, u32[]{:S(2)}) collective-permute-start(f32[3,8,128]{2,1,0:T(8,128)S(1)} %slice.15), channel_id=1, source_target_pairs={{32,0},{64,32},{96,64},{128,96},{160,128},{192,160},{224,192},{256... | collective-permute-start | bytes 36872 | tf_op jit(solution)/shard_map/ppermute | solution.py:488
  49.5 14.9 %all-to-all-start.2 = ((f32[32,1,128]{2,1,0:T(1,128)}), f32[32,1,128]{2,1,0:T(1,128)S(1)}, u32[]{:S(2)}, u32[]{:S(2)}) async-start(f32[32,1,128]{2,1,0:T(1,128)} %get-tuple-element.41), calls=%async_computation.2 | async-start | bytes 32768 | tf_op jit(solution)/shard_map/all_to_all | solution.py:447

commit v9 on v8

--- a/solution.py
+++ b/solution.py
@@ -489,7 +489,7 @@
         grad_feature[:, :8, :], "ctx", [(source + 1, source) for source in range(ctx - 1)]
     )
     stats = jnp.broadcast_to(stats.astype(F16), (ctx, STATS, CHANNELS))
-    gathered = exchange(stats, "ctx", ctx // 2 - 1).astype(F32)
+    gathered = exchange(stats, "ctx", ctx // 2).astype(F32)
     total, square = call(
         total_kernel, "total", (shape(STATS, CHANNELS), shape(planes, 1, CHANNELS)), [VMEM], 1,
     )(gathered)

time: 65.6 us -> 63.9 us (0.974)
  waiting for transfers between devices: 5.31 us -> 3.27 us
    all_to_all x3, waiting for transfers between devices: 5.31 us -> 3.27 us  [exchange(): lax.all_to_all(blocks, axis, 0, 0, axis_index_groups=[[(first + p) % coun...]
where the time goes in v9:
time: 63.9 us; the launch traced here: 63.5 us
  starting transfers between devices  46.9 us (73%)
  Pallas kernels  9.46 us (15%)
  waiting for transfers between devices  3.27 us (5%)
  local copies, waits for them, and re-layouts  2.28 us (4%)
  between operations  0.8 us (1%)
  other arithmetic  0.78 us (1%)
    all_to_all x3, starting transfers between devices, exchange(): lax.all_to_all(blocks, axis, 0, 0, axis_index_groups=[[(first + p) % coun...  41.1 us
    ppermute x1, starting transfers between devices, shards(): lax.ppermute(projected[:, ROWS - LEAD:, :], 'ctx', [(source, source + 1)...  4.49 us
    pallas_call x1, Pallas kernels, shards(): call(middle_kernel, 'within', (shape(2 * ROWS + (POWER + ctx) * MODES, CH...  3.99 us
    all_to_all x3, waiting for transfers between devices, exchange(): lax.all_to_all(blocks, axis, 0, 0, axis_index_groups=[[(first + p) % coun...  3.27 us
    pallas_call x1, Pallas kernels, shards(): call(prepare_kernel, 'prepare', (shape(2, ROWS, CHANNELS), shape(2, CHUNK...  1.79 us
    ppermute x1, starting transfers between devices, shards(): lax.ppermute(grad_feature[:, :8, :], 'ctx', [(source + 1, source) for sou...  1.29 us
  transfers between devices with their start and end apart: 5, of which 2 were waited for; matrix products, arithmetic and copies ran while one was open for 0% of the time, Pallas kernels for 12%

profile of v9, /device:TPU:1, one launch (start us, length us, event | category | flops | bytes accessed | tf_op | source)
XLA Modules:
  0.0 63.5 jit_solution(17239508641602643752)
XLA Ops:
  0.6 0.0 copy-start.2
  0.6 0.0 copy-start.4
  0.7 0.7 %slice.12 = bf16[3,16,128]{2,1,0:T(8,128)(2,1)S(1)} slice(bf16[3,512,128]{2,1,0:T(8,128)(2,1)} %proj_ref.3), slice={[0:3], [496:512], [0:128]} | slice | bytes 24576 | tf_op jit(solution)/shard_map/slice | solution.py:455
  1.4 0.0 copy-start.3
  1.4 4.5 %collective-permute-start = (bf16[3,16,128]{2,1,0:T(8,128)(2,1)S(1)}, bf16[3,16,128]{2,1,0:T(8,128)(2,1)S(1)}, u32[]{:S(2)}, u32[]{:S(2)}) collective-permute-start(bf16[3,16,128]{2,1,0:T(8,128)(2,1)S(1)} %slice.12), channel_id=1, source_target_pairs={{0,32},{32,64},{64,96},{96,128},{128,160},{160,192},{192,224},{224... | collective-permute-start | bytes 36872 | tf_op jit(solution)/shard_map/ppermute | solution.py:454
  5.9 0.0 copy-done.2
  5.9 0.0 copy-done.4
  5.9 0.0 copy-done.3
  5.9 1.8 %prepare.1 = (f32[2,512,128]{2,1,0:T(8,128)S(1)}, f32[2,128,512]{2,1,0:T(8,128)S(1)}, f32[2,16,512]{2,1,0:T(8,128)S(1)}, f32[2,16,128]{2,1,0:T(8,128)S(1)}, f32[...) custom-call(f32[3,7,128]{2,1,0:T(8,128)S(1)} %copy-done.2, f32[8,16]{1,0:T(8,128)S(1)} %copy-done.3, ...), custom_call_target="tpu_custom_call" | custom-call | flops 3000000000 | bytes 9000000 | tf_op jit(solution)/shard_map/prepare/pallas_call | solution.py:457
  7.7 0.0 collective-permute-done.before_ref
  7.7 0.1 patch.1
  7.8 0.7 %select_convert_fusion = f16[16,24,128]{2,1,0:T(8,128)(2,1)} fusion(f32[24,128]{1,0:T(8,128)S(1)} %get-tuple-element.47, f32[24,128]{1,0:T(8,128)S(1)} %get-tuple-element.46, pred[16]{0:T(512)(128)(4,1)S(1)} %fusion), kind=kLoop, calls=%fused_computation | loop fusion | flops 98304 | bytes 122896 | tf_op jit(solution)/shard_map/convert_element_type | solution.py:474
  8.6 17.3 %all-to-all-start = ((f16[16,24,128]{2,1,0:T(8,128)(2,1)}), f16[16,24,128]{2,1,0:T(8,128)(2,1)S(1)}, u32[]{:S(2)}, u32[]{:S(2)}) async-start(f16[16,24,128]{2,1,0:T(8,128)(2,1)} %select_convert_fusion), calls=%async_computation | async-start | bytes 196608 | tf_op jit(solution)/shard_map/all_to_all | solution.py:447
  25.9 0.0 copy-start
  25.9 4.0 %within.1 = (f32[1568,128]{1,0:T(8,128)S(1)}, bf16[4,128,128]{2,1,0:T(8,128)(2,1)S(1)}) custom-call(s32[1]{0:T(128)} %bitcast.me_ref, f32[2,8,16]{2,1,0:T(8,128)S(1)} %get-tuple-element.29.table_ref, f32[2,128,512]{2,1,0:T(8,128)S(1)} %get-tuple-element.30.pair_ref, f32[2,16,512]{2,1,0:T(8,128)S(1)} %get-tuple-element.31.states_ref, ...), custom_call_target="tpu_custom_call" | custom-call | flops 8000000000 | bytes 24000000 | tf_op jit(solution)/shard_map/within/pallas_call | solution.py:476
  29.9 0.0 copy-start.1
  29.9 0.0 all-to-all-done
  29.9 0.0 copy-done
  29.9 0.9 %copy-done.1 = bf16[512,128]{1,0:T(8,128)(2,1)S(1)} copy-done((bf16[512,128]{1,0:T(8,128)(2,1)S(1)}, bf16[512,128]{1,0:T(8,128)(2,1)}, u32[]{:S(2)}) %copy-start.1) | copy-done | bytes 131096
  30.8 1.0 %across.1 = (f32[3,512,128]{2,1,0:T(8,128)S(1)}, f32[24,128]{1,0:T(8,128)S(1)}) custom-call(s32[1]{0:T(128)} %bitcast.me_ref, f32[16,24,128]{2,1,0:T(8,128)S(1)} %convert_element_type.13.arrived_ref, f32[1568,128]{1,0:T(8,128)S(1)} %get-tuple-element.34.near_ref, bf16[4,128,128]{2,1,0:T(8,128)(2,1)S(1)} %get-tuple-element.35.halves_ref, ...), custom_call_target="tpu_custom_call" | custom-call | flops 4000000000 | bytes 12000000 | tf_op jit(solution)/shard_map/across/pallas_call | solution.py:482
  31.8 0.7 %broadcast_in_dim.22 = f16[16,24,128]{2,1,0:T(8,128)(2,1)} broadcast(f16[24,128]{1,0:T(8,128)(2,1)S(1)} %convert_element_type.14), dimensions={1,2} | broadcast | bytes 104448 | tf_op jit(solution)/shard_map/broadcast_in_dim | solution.py:491
  32.5 11.5 %all-to-all-start.1 = ((f16[16,24,128]{2,1,0:T(8,128)(2,1)}), f16[16,24,128]{2,1,0:T(8,128)(2,1)S(1)}, u32[]{:S(2)}, u32[]{:S(2)}) async-start(f16[16,24,128]{2,1,0:T(8,128)(2,1)} %broadcast_in_dim.22), calls=%async_computation.1 | async-start | bytes 196608 | tf_op jit(solution)/shard_map/all_to_all | solution.py:447
  44.0 1.3 %collective-permute-start.1 = (f32[3,8,128]{2,1,0:T(8,128)S(1)}, f32[3,8,128]{2,1,0:T(8,128)S(1)}, u32[]{:S(2)}, u32[]{:S(2)}) collective-permute-start(f32[3,8,128]{2,1,0:T(8,128)S(1)} %slice.15), channel_id=1, source_target_pairs={{32,0},{64,32},{96,64},{128,96},{160,128},{192,160},{224,192},{256... | collective-permute-start | bytes 36872 | tf_op jit(solution)/shard_map/ppermute | solution.py:488
  45.3 2.5 %all-to-all-done.1 = f16[16,24,128]{2,1,0:T(8,128)(2,1)S(1)} async-done(((f16[16,24,128]{2,1,0:T(8,128)(2,1)}), f16[16,24,128]{2,1,0:T(8,128)(2,1)S(1)}, u32[]{:S(2)}, u32[]{:S(2)}) %all-to-all-start.1) | async-done | bytes 98336 | tf_op jit(solution)/shard_map/all_to_all | solution.py:447
  47.8 0.6 %total.1 = (f32[24,128]{1,0:T(8,128)S(1)}, f32[32,1,128]{2,1,0:T(1,128)}) custom-call(f32[16,24,128]{2,1,0:T(8,128)S(1)} %convert_element_type.15.stats_ref), custom_call_target="tpu_custom_call" | custom-call | flops 1000000000 | bytes 3000000 | tf_op jit(solution)/shard_map/total/pallas_call | solution.py:493
  48.5 12.3 %all-to-all-start.2 = ((f32[32,1,128]{2,1,0:T(1,128)}), f32[32,1,128]{2,1,0:T(1,128)S(1)}, u32[]{:S(2)}, u32[]{:S(2)}) async-start(f32[32,1,128]{2,1,0:T(1,128)} %get-tuple-element.41), calls=%async_computation.2 | async-start | bytes 32768 | tf_op jit(solution)/shard_map/all_to_all | solution.py:447
  60.8 0.0 collective-permute-done.1.after_ref
  60.8 1.2 %inputs.1 = (bf16[3,512,128]{2,1,0:T(8,128)(2,1)}, f32[2,8,16]{2,1,0:T(8,128)S(1)}) custom-call(f32[3,512,128]{2,1,0:T(8,128)S(1)} %get-tuple-element.37.feature_ref, f32[3,8,128]{2,1,0:T(8,128)S(1)} %collective-permute-done.1.after_ref, f32[3,7,128]{2,1,0:T(8,128)S(1)} %copy-done.2, f32[24,128]{1,0:T(8,128)S(1)} %get-tuple-element.39.total_ref), custom_call_target="tpu_custom_call" | custom-call | flops 2000000000 | bytes 6000000 | tf_op jit(solution)/shard_map/inputs/pallas_call | solution.py:497
  62.0 0.7 %all-to-all-done.2.square_ref = f32[32,1,128]{2,1,0:T(1,128)S(1)} async-done(((f32[32,1,128]{2,1,0:T(1,128)}), f32[32,1,128]{2,1,0:T(1,128)S(1)}, u32[]{:S(2)}, u32[]{:S(2)}) %all-to-all-start.2) | async-done | bytes 16416 | tf_op jit(solution)/shard_map/all_to_all | solution.py:447
  62.8 0.7 %scale.1 = (f32[3,7,128]{2,1,0:T(8,128)}, f32[8,16]{1,0:T(8,128)}, f32[8,16]{1,0:T(8,128)}) custom-call(f32[32,1,128]{2,1,0:T(1,128)S(1)} %all-to-all-done.2.square_ref, f32[24,128]{1,0:T(8,128)S(1)} %get-tuple-element.39.total_ref, f32[2,8,16]{2,1,0:T(8,128)S(1)} %get-tuple-element.42.table_ref), custom_call_target="tpu_custom_call" | custom-call | flops 1000000000 | bytes 3000000 | tf_op jit(solution)/shard_map/scale/pallas_call | solution.py:502
  (6 shorter events, 0.1 us)
Async XLA Ops:
  0.6 5.3 %copy-start.2 = (f32[3,7,128]{2,1,0:T(8,128)S(1)}, f32[3,7,128]{2,1,0:T(8,128)}, u32[]{:S(2)}) copy-start(f32[3,7,128]{2,1,0:T(8,128)} %weight_ref.5) | copy-start | bytes 32260
  0.6 5.3 %copy-start.4 = (f32[8,16]{1,0:T(8,128)S(1)}, f32[8,16]{1,0:T(8,128)}, u32[]{:S(2)}) copy-start(f32[8,16]{1,0:T(8,128)} %residue_ref.1) | copy-start | bytes 1540
  1.4 4.5 %copy-start.3 = (f32[8,16]{1,0:T(8,128)S(1)}, f32[8,16]{1,0:T(8,128)}, u32[]{:S(2)}) copy-start(f32[8,16]{1,0:T(8,128)} %rate_ref.1) | copy-start | bytes 1540
  1.4 6.3 %collective-permute-start = (bf16[3,16,128]{2,1,0:T(8,128)(2,1)S(1)}, bf16[3,16,128]{2,1,0:T(8,128)(2,1)S(1)}, u32[]{:S(2)}, u32[]{:S(2)}) collective-permute-start(bf16[3,16,128]{2,1,0:T(8,128)(2,1)S(1)} %slice.12), channel_id=1, source_target_pairs={{0,32},{32,64},{64,96},{96,128},{128,160},{160,192},{192,224},{224... | collective-permute-start | bytes 36872 | tf_op jit(solution)/shard_map/ppermute | solution.py:454
  8.6 21.3 %all-to-all-start = ((f16[16,24,128]{2,1,0:T(8,128)(2,1)}), f16[16,24,128]{2,1,0:T(8,128)(2,1)S(1)}, u32[]{:S(2)}, u32[]{:S(2)}) async-start(f16[16,24,128]{2,1,0:T(8,128)(2,1)} %select_convert_fusion), calls=%async_computation | async-start | bytes 196608 | tf_op jit(solution)/shard_map/all_to_all | solution.py:447
  25.9 4.1 %copy-start = (bf16[3,512,128]{2,1,0:T(8,128)(2,1)S(1)}, bf16[3,512,128]{2,1,0:T(8,128)(2,1)}, u32[]{:S(2)}) copy-start(bf16[3,512,128]{2,1,0:T(8,128)(2,1)} %proj_ref.3) | copy-start | bytes 1179652
  29.9 0.9 %copy-start.1 = (bf16[512,128]{1,0:T(8,128)(2,1)S(1)}, bf16[512,128]{1,0:T(8,128)(2,1)}, u32[]{:S(2)}) copy-start(bf16[512,128]{1,0:T(8,128)(2,1)} %out_grad_ref.3) | copy-start | bytes 393220
  32.5 15.3 %all-to-all-start.1 = ((f16[16,24,128]{2,1,0:T(8,128)(2,1)}), f16[16,24,128]{2,1,0:T(8,128)(2,1)S(1)}, u32[]{:S(2)}, u32[]{:S(2)}) async-start(f16[16,24,128]{2,1,0:T(8,128)(2,1)} %broadcast_in_dim.22), calls=%async_computation.1 | async-start | bytes 196608 | tf_op jit(solution)/shard_map/all_to_all | solution.py:447
  44.0 16.8 %collective-permute-start.1 = (f32[3,8,128]{2,1,0:T(8,128)S(1)}, f32[3,8,128]{2,1,0:T(8,128)S(1)}, u32[]{:S(2)}, u32[]{:S(2)}) collective-permute-start(f32[3,8,128]{2,1,0:T(8,128)S(1)} %slice.15), channel_id=1, source_target_pairs={{32,0},{64,32},{96,64},{128,96},{160,128},{192,160},{224,192},{256... | collective-permute-start | bytes 36872 | tf_op jit(solution)/shard_map/ppermute | solution.py:488
  48.5 14.3 %all-to-all-start.2 = ((f32[32,1,128]{2,1,0:T(1,128)}), f32[32,1,128]{2,1,0:T(1,128)S(1)}, u32[]{:S(2)}, u32[]{:S(2)}) async-start(f32[32,1,128]{2,1,0:T(1,128)} %get-tuple-element.41), calls=%async_computation.2 | async-start | bytes 32768 | tf_op jit(solution)/shard_map/all_to_all | solution.py:447

commit v10 on v9

--- a/solution.py
+++ b/solution.py
@@ -471,8 +471,9 @@
         scratch=[pltpu.VMEM((LEAD + HEAD, CHANNELS), F32)],
     )(before, conv_weight, head, powers, ends)
     later = member(lax.broadcasted_iota(jnp.int32, (ctx, 1, 1), 0), ctx) > me.reshape(1, 1, 1)
-    send = jnp.where(later, send[1], send[0]).astype(F16)
-    arrived = exchange(send, "ctx", ctx // 2).astype(F32)
+    send = send[:, : MODES + 2, :].reshape(2, MODES // 2 + 1, 2, CHANNELS)
+    send = jnp.where(later[..., None], send[1], send[0]).astype(F16)
+    arrived = exchange(send, "ctx", ctx // 2).astype(F32).reshape(ctx, MODES + 2, CHANNELS)
     near, halves = call(
         middle_kernel, "within",
         (shape(2 * ROWS + (POWER + ctx) * MODES, CHANNELS), shape(4, CHUNK, CHANNELS, dtype=BF16)),

time: 63.9 us -> 64.3 us (level)
  no operation moved by 1% of the time
where the time goes in v10:
time: 64.3 us; the launch traced here: 63.9 us
  starting transfers between devices  47.1 us (73%)
  Pallas kernels  9.49 us (15%)
  waiting for transfers between devices  3.27 us (5%)
  local copies, waits for them, and re-layouts  2.41 us (4%)
  between operations  0.82 us (1%)
  other arithmetic  0.81 us (1%)
    all_to_all x3, starting transfers between devices, exchange(): lax.all_to_all(blocks, axis, 0, 0, axis_index_groups=[[(first + p) % coun...  41.3 us
    ppermute x1, starting transfers between devices, shards(): lax.ppermute(projected[:, ROWS - LEAD:, :], 'ctx', [(source, source + 1)...  4.49 us
    pallas_call x1, Pallas kernels, shards(): call(middle_kernel, 'within', (shape(2 * ROWS + (POWER + ctx) * MODES, CH...  4 us
    all_to_all x3, waiting for transfers between devices, exchange(): lax.all_to_all(blocks, axis, 0, 0, axis_index_groups=[[(first + p) % coun...  3.27 us
    pallas_call x1, Pallas kernels, shards(): call(prepare_kernel, 'prepare', (shape(2, ROWS, CHANNELS), shape(2, CHUNK...  1.8 us
    ppermute x1, starting transfers between devices, shards(): lax.ppermute(grad_feature[:, :8, :], 'ctx', [(source + 1, source) for sou...  1.29 us
  transfers between devices with their start and end apart: 5, of which 2 were waited for; matrix products, arithmetic and copies ran while one was open for 0% of the time, Pallas kernels for 12%

profile of v10, /device:TPU:1, one launch (start us, length us, event | category | flops | bytes accessed | tf_op | source)
XLA Modules:
  0.0 63.9 jit_solution(9312859572459333225)
XLA Ops:
  0.6 0.0 copy-start.2
  0.6 0.0 copy-start.4
  0.7 0.7 %slice.17 = bf16[3,16,128]{2,1,0:T(8,128)(2,1)S(1)} slice(bf16[3,512,128]{2,1,0:T(8,128)(2,1)} %proj_ref.3), slice={[0:3], [496:512], [0:128]} | slice | bytes 24576 | tf_op jit(solution)/shard_map/slice | solution.py:455
  1.4 0.0 copy-start.3
  1.4 4.5 %collective-permute-start = (bf16[3,16,128]{2,1,0:T(8,128)(2,1)S(1)}, bf16[3,16,128]{2,1,0:T(8,128)(2,1)S(1)}, u32[]{:S(2)}, u32[]{:S(2)}) collective-permute-start(bf16[3,16,128]{2,1,0:T(8,128)(2,1)S(1)} %slice.17), channel_id=1, source_target_pairs={{0,32},{32,64},{64,96},{96,128},{128,160},{160,192},{192,224},{224... | collective-permute-start | bytes 36872 | tf_op jit(solution)/shard_map/ppermute | solution.py:454
  5.9 0.0 copy-done.2
  5.9 0.0 copy-done.4
  5.9 0.0 copy-done.3
  5.9 1.8 %prepare.1 = (f32[2,512,128]{2,1,0:T(8,128)S(1)}, f32[2,128,512]{2,1,0:T(8,128)S(1)}, f32[2,16,512]{2,1,0:T(8,128)S(1)}, f32[2,16,128]{2,1,0:T(8,128)S(1)}, f32[...) custom-call(f32[3,7,128]{2,1,0:T(8,128)S(1)} %copy-done.2, f32[8,16]{1,0:T(8,128)S(1)} %copy-done.3, ...), custom_call_target="tpu_custom_call" | custom-call | flops 3000000000 | bytes 9000000 | tf_op jit(solution)/shard_map/prepare/pallas_call | solution.py:457
  7.7 0.0 collective-permute-done.before_ref
  7.8 0.1 patch.1
  7.9 0.8 %select_convert_fusion = f16[16,9,2,128]{3,2,1,0:T(2,128)(2,1)} fusion(pred[16]{0:T(512)(128)(4,1)S(1)} %fusion, f32[9,2,128]{2,1,0:T(2,128)S(1)} %squeeze.7, f32[9,2,128]{2,1,0:T(2,128)S(1)} %squeeze.6), kind=kLoop, calls=%fused_computation | loop fusion | flops 73728 | bytes 92176 | tf_op jit(solution)/shard_map/convert_element_type | solution.py:475
  8.6 17.3 %all-to-all-start = ((f16[16,9,2,128]{3,2,1,0:T(2,128)(2,1)}), f16[16,9,2,128]{3,2,1,0:T(2,128)(2,1)S(1)}, u32[]{:S(2)}, u32[]{:S(2)}) async-start(f16[16,9,2,128]{3,2,1,0:T(2,128)(2,1)} %select_convert_fusion), calls=%async_computation | async-start | bytes 147456 | tf_op jit(solution)/shard_map/all_to_all | solution.py:447
  25.9 4.0 %within.1 = (f32[1568,128]{1,0:T(8,128)S(1)}, bf16[4,128,128]{2,1,0:T(8,128)(2,1)S(1)}) custom-call(s32[1]{0:T(128)} %bitcast.me_ref, f32[2,8,16]{2,1,0:T(8,128)S(1)} %get-tuple-element.29.table_ref, f32[2,128,512]{2,1,0:T(8,128)S(1)} %get-tuple-element.30.pair_ref, f32[2,16,512]{2,1,0:T(8,128)S(1)} %get-tuple-element.31.states_ref, ...), custom_call_target="tpu_custom_call" | custom-call | flops 8000000000 | bytes 24000000 | tf_op jit(solution)/shard_map/within/pallas_call | solution.py:477
  29.9 0.0 copy-start
  30.0 0.0 all-to-all-done
  30.0 0.0 copy-start.1
  30.0 0.1 copy.11.arrived_ref
  30.1 0.8 %copy-done = bf16[3,512,128]{2,1,0:T(8,128)(2,1)S(1)} copy-done((bf16[3,512,128]{2,1,0:T(8,128)(2,1)S(1)}, bf16[3,512,128]{2,1,0:T(8,128)(2,1)}, u32[]{:S(2)}) %copy-start) | copy-done | bytes 393240
  30.9 0.0 copy-done.1
  31.0 1.0 %across.1 = (f32[3,512,128]{2,1,0:T(8,128)S(1)}, f32[24,128]{1,0:T(8,128)S(1)}) custom-call(s32[1]{0:T(128)} %bitcast.me_ref, f32[16,18,128]{2,1,0:T(8,128)S(1)} %copy.11.arrived_ref, f32[1568,128]{1,0:T(8,128)S(1)} %get-tuple-element.34.near_ref, bf16[4,128,128]{2,1,0:T(8,128)(2,1)S(1)} %get-tuple-element.35.halves_ref, ...), custom_call_target="tpu_custom_call" | custom-call | flops 4000000000 | bytes 12000000 | tf_op jit(solution)/shard_map/across/pallas_call | solution.py:483
  32.0 0.7 %broadcast_in_dim.23 = f16[16,24,128]{2,1,0:T(8,128)(2,1)} broadcast(f16[24,128]{1,0:T(8,128)(2,1)S(1)} %convert_element_type.11), dimensions={1,2} | broadcast | bytes 104448 | tf_op jit(solution)/shard_map/broadcast_in_dim | solution.py:492
  32.7 11.5 %all-to-all-start.1 = ((f16[16,24,128]{2,1,0:T(8,128)(2,1)}), f16[16,24,128]{2,1,0:T(8,128)(2,1)S(1)}, u32[]{:S(2)}, u32[]{:S(2)}) async-start(f16[16,24,128]{2,1,0:T(8,128)(2,1)} %broadcast_in_dim.23), calls=%async_computation.1 | async-start | bytes 196608 | tf_op jit(solution)/shard_map/all_to_all | solution.py:447
  44.2 1.3 %collective-permute-start.1 = (f32[3,8,128]{2,1,0:T(8,128)S(1)}, f32[3,8,128]{2,1,0:T(8,128)S(1)}, u32[]{:S(2)}, u32[]{:S(2)}) collective-permute-start(f32[3,8,128]{2,1,0:T(8,128)S(1)} %slice.20), channel_id=1, source_target_pairs={{32,0},{64,32},{96,64},{128,96},{160,128},{192,160},{224,192},{256... | collective-permute-start | bytes 36872 | tf_op jit(solution)/shard_map/ppermute | solution.py:489
  45.5 2.5 %all-to-all-done.1 = f16[16,24,128]{2,1,0:T(8,128)(2,1)S(1)} async-done(((f16[16,24,128]{2,1,0:T(8,128)(2,1)}), f16[16,24,128]{2,1,0:T(8,128)(2,1)S(1)}, u32[]{:S(2)}, u32[]{:S(2)}) %all-to-all-start.1) | async-done | bytes 98336 | tf_op jit(solution)/shard_map/all_to_all | solution.py:447
  48.0 0.6 %total.1 = (f32[24,128]{1,0:T(8,128)S(1)}, f32[32,1,128]{2,1,0:T(1,128)}) custom-call(f32[16,24,128]{2,1,0:T(8,128)S(1)} %convert_element_type.12.stats_ref), custom_call_target="tpu_custom_call" | custom-call | flops 1000000000 | bytes 3000000 | tf_op jit(solution)/shard_map/total/pallas_call | solution.py:494
  48.7 12.5 %all-to-all-start.2 = ((f32[32,1,128]{2,1,0:T(1,128)}), f32[32,1,128]{2,1,0:T(1,128)S(1)}, u32[]{:S(2)}, u32[]{:S(2)}) async-start(f32[32,1,128]{2,1,0:T(1,128)} %get-tuple-element.41), calls=%async_computation.2 | async-start | bytes 32768 | tf_op jit(solution)/shard_map/all_to_all | solution.py:447
  61.2 0.0 collective-permute-done.1.after_ref
  61.2 1.2 %inputs.1 = (bf16[3,512,128]{2,1,0:T(8,128)(2,1)}, f32[2,8,16]{2,1,0:T(8,128)S(1)}) custom-call(f32[3,512,128]{2,1,0:T(8,128)S(1)} %get-tuple-element.37.feature_ref, f32[3,8,128]{2,1,0:T(8,128)S(1)} %collective-permute-done.1.after_ref, f32[3,7,128]{2,1,0:T(8,128)S(1)} %copy-done.2, f32[24,128]{1,0:T(8,128)S(1)} %get-tuple-element.39.total_ref), custom_call_target="tpu_custom_call" | custom-call | flops 2000000000 | bytes 6000000 | tf_op jit(solution)/shard_map/inputs/pallas_call | solution.py:498
  62.4 0.7 %all-to-all-done.2.square_ref = f32[32,1,128]{2,1,0:T(1,128)S(1)} async-done(((f32[32,1,128]{2,1,0:T(1,128)}), f32[32,1,128]{2,1,0:T(1,128)S(1)}, u32[]{:S(2)}, u32[]{:S(2)}) %all-to-all-start.2) | async-done | bytes 16416 | tf_op jit(solution)/shard_map/all_to_all | solution.py:447
  63.2 0.7 %scale.1 = (f32[3,7,128]{2,1,0:T(8,128)}, f32[8,16]{1,0:T(8,128)}, f32[8,16]{1,0:T(8,128)}) custom-call(f32[32,1,128]{2,1,0:T(1,128)S(1)} %all-to-all-done.2.square_ref, f32[24,128]{1,0:T(8,128)S(1)} %get-tuple-element.39.total_ref, f32[2,8,16]{2,1,0:T(8,128)S(1)} %get-tuple-element.42.table_ref), custom_call_target="tpu_custom_call" | custom-call | flops 1000000000 | bytes 3000000 | tf_op jit(solution)/shard_map/scale/pallas_call | solution.py:503
  (9 shorter events, 0.1 us)
Async XLA Ops:
  0.6 5.3 %copy-start.2 = (f32[3,7,128]{2,1,0:T(8,128)S(1)}, f32[3,7,128]{2,1,0:T(8,128)}, u32[]{:S(2)}) copy-start(f32[3,7,128]{2,1,0:T(8,128)} %weight_ref.5) | copy-start | bytes 32260
  0.6 5.3 %copy-start.4 = (f32[8,16]{1,0:T(8,128)S(1)}, f32[8,16]{1,0:T(8,128)}, u32[]{:S(2)}) copy-start(f32[8,16]{1,0:T(8,128)} %residue_ref.1) | copy-start | bytes 1540
  1.4 4.5 %copy-start.3 = (f32[8,16]{1,0:T(8,128)S(1)}, f32[8,16]{1,0:T(8,128)}, u32[]{:S(2)}) copy-start(f32[8,16]{1,0:T(8,128)} %rate_ref.1) | copy-start | bytes 1540
  1.4 6.4 %collective-permute-start = (bf16[3,16,128]{2,1,0:T(8,128)(2,1)S(1)}, bf16[3,16,128]{2,1,0:T(8,128)(2,1)S(1)}, u32[]{:S(2)}, u32[]{:S(2)}) collective-permute-start(bf16[3,16,128]{2,1,0:T(8,128)(2,1)S(1)} %slice.17), channel_id=1, source_target_pairs={{0,32},{32,64},{64,96},{96,128},{128,160},{160,192},{192,224},{224... | collective-permute-start | bytes 36872 | tf_op jit(solution)/shard_map/ppermute | solution.py:454
  8.6 21.3 %all-to-all-start = ((f16[16,9,2,128]{3,2,1,0:T(2,128)(2,1)}), f16[16,9,2,128]{3,2,1,0:T(2,128)(2,1)S(1)}, u32[]{:S(2)}, u32[]{:S(2)}) async-start(f16[16,9,2,128]{3,2,1,0:T(2,128)(2,1)} %select_convert_fusion), calls=%async_computation | async-start | bytes 147456 | tf_op jit(solution)/shard_map/all_to_all | solution.py:447
  29.9 1.0 %copy-start = (bf16[3,512,128]{2,1,0:T(8,128)(2,1)S(1)}, bf16[3,512,128]{2,1,0:T(8,128)(2,1)}, u32[]{:S(2)}) copy-start(bf16[3,512,128]{2,1,0:T(8,128)(2,1)} %proj_ref.3) | copy-start | bytes 1179652
  30.0 1.0 %copy-start.1 = (bf16[512,128]{1,0:T(8,128)(2,1)S(1)}, bf16[512,128]{1,0:T(8,128)(2,1)}, u32[]{:S(2)}) copy-start(bf16[512,128]{1,0:T(8,128)(2,1)} %out_grad_ref.3) | copy-start | bytes 393220
  32.7 15.3 %all-to-all-start.1 = ((f16[16,24,128]{2,1,0:T(8,128)(2,1)}), f16[16,24,128]{2,1,0:T(8,128)(2,1)S(1)}, u32[]{:S(2)}, u32[]{:S(2)}) async-start(f16[16,24,128]{2,1,0:T(8,128)(2,1)} %broadcast_in_dim.23), calls=%async_computation.1 | async-start | bytes 196608 | tf_op jit(solution)/shard_map/all_to_all | solution.py:447
  44.2 17.0 %collective-permute-start.1 = (f32[3,8,128]{2,1,0:T(8,128)S(1)}, f32[3,8,128]{2,1,0:T(8,128)S(1)}, u32[]{:S(2)}, u32[]{:S(2)}) collective-permute-start(f32[3,8,128]{2,1,0:T(8,128)S(1)} %slice.20), channel_id=1, source_target_pairs={{32,0},{64,32},{96,64},{128,96},{160,128},{192,160},{224,192},{256... | collective-permute-start | bytes 36872 | tf_op jit(solution)/shard_map/ppermute | solution.py:489
  48.7 14.5 %all-to-all-start.2 = ((f32[32,1,128]{2,1,0:T(1,128)}), f32[32,1,128]{2,1,0:T(1,128)S(1)}, u32[]{:S(2)}, u32[]{:S(2)}) async-start(f32[32,1,128]{2,1,0:T(1,128)} %get-tuple-element.41), calls=%async_computation.2 | async-start | bytes 32768 | tf_op jit(solution)/shard_map/all_to_all | solution.py:447

commit v11 on v9

--- a/solution.py
+++ b/solution.py
@@ -493,7 +493,7 @@
     total, square = call(
         total_kernel, "total", (shape(STATS, CHANNELS), shape(planes, 1, CHANNELS)), [VMEM], 1,
     )(gathered)
-    squares = exchange(square, "ch", planes // 2 + planes // 8)
+    squares = exchange(square, "ch", planes - 2)
     grad_projected, table = call(
         inputs_kernel, "inputs",
         (shape(3, ROWS, CHANNELS, dtype=BF16), shape(2, GROUPS, MODES)), [VMEM] * 4, 2,

time: 63.9 us -> 65.3 us (1.022)
  waiting for transfers between devices: 3.27 us -> 5.06 us
    all_to_all x3, waiting for transfers between devices: 3.27 us -> 5.06 us  [exchange(): lax.all_to_all(blocks, axis, 0, 0, axis_index_groups=[[(first + p) % coun...]
where the time goes in v11:
time: 65.3 us; the launch traced here: 64.8 us
  starting transfers between devices  46.5 us (71%)
  Pallas kernels  9.46 us (14%)
  waiting for transfers between devices  5.06 us (8%)
  local copies, waits for them, and re-layouts  2.28 us (3%)
  between operations  0.8 us (1%)
  other arithmetic  0.78 us (1%)
    all_to_all x3, starting transfers between devices, exchange(): lax.all_to_all(blocks, axis, 0, 0, axis_index_groups=[[(first + p) % coun...  40.7 us
    all_to_all x3, waiting for transfers between devices, exchange(): lax.all_to_all(blocks, axis, 0, 0, axis_index_groups=[[(first + p) % coun...  5.06 us
    ppermute x1, starting transfers between devices, shards(): lax.ppermute(projected[:, ROWS - LEAD:, :], 'ctx', [(source, source + 1)...  4.49 us
    pallas_call x1, Pallas kernels, shards(): call(middle_kernel, 'within', (shape(2 * ROWS + (POWER + ctx) * MODES, CH...  3.99 us
    pallas_call x1, Pallas kernels, shards(): call(prepare_kernel, 'prepare', (shape(2, ROWS, CHANNELS), shape(2, CHUNK...  1.79 us
  transfers between devices with their start and end apart: 5, of which 2 were waited for; matrix products, arithmetic and copies ran while one was open for 0% of the time, Pallas kernels for 12%

profile of v11, /device:TPU:1, one launch (start us, length us, event | category | flops | bytes accessed | tf_op | source)
XLA Modules:
  0.0 64.8 jit_solution(5531573138426665607)
XLA Ops:
  0.6 0.0 copy-start.2
  0.6 0.0 copy-start.4
  0.7 0.7 %slice.12 = bf16[3,16,128]{2,1,0:T(8,128)(2,1)S(1)} slice(bf16[3,512,128]{2,1,0:T(8,128)(2,1)} %proj_ref.3), slice={[0:3], [496:512], [0:128]} | slice | bytes 24576 | tf_op jit(solution)/shard_map/slice | solution.py:455
  1.4 0.0 copy-start.3
  1.4 4.5 %collective-permute-start = (bf16[3,16,128]{2,1,0:T(8,128)(2,1)S(1)}, bf16[3,16,128]{2,1,0:T(8,128)(2,1)S(1)}, u32[]{:S(2)}, u32[]{:S(2)}) collective-permute-start(bf16[3,16,128]{2,1,0:T(8,128)(2,1)S(1)} %slice.12), channel_id=1, source_target_pairs={{0,32},{32,64},{64,96},{96,128},{128,160},{160,192},{192,224},{224... | collective-permute-start | bytes 36872 | tf_op jit(solution)/shard_map/ppermute | solution.py:454
  5.9 0.0 copy-done.2
  5.9 0.0 copy-done.4
  5.9 0.0 copy-done.3
  5.9 1.8 %prepare.1 = (f32[2,512,128]{2,1,0:T(8,128)S(1)}, f32[2,128,512]{2,1,0:T(8,128)S(1)}, f32[2,16,512]{2,1,0:T(8,128)S(1)}, f32[2,16,128]{2,1,0:T(8,128)S(1)}, f32[...) custom-call(f32[3,7,128]{2,1,0:T(8,128)S(1)} %copy-done.2, f32[8,16]{1,0:T(8,128)S(1)} %copy-done.3, ...), custom_call_target="tpu_custom_call" | custom-call | flops 3000000000 | bytes 9000000 | tf_op jit(solution)/shard_map/prepare/pallas_call | solution.py:457
  7.7 0.0 collective-permute-done.before_ref
  7.7 0.1 patch.1
  7.8 0.7 %select_convert_fusion = f16[16,24,128]{2,1,0:T(8,128)(2,1)} fusion(f32[24,128]{1,0:T(8,128)S(1)} %get-tuple-element.47, f32[24,128]{1,0:T(8,128)S(1)} %get-tuple-element.46, pred[16]{0:T(512)(128)(4,1)S(1)} %fusion), kind=kLoop, calls=%fused_computation | loop fusion | flops 98304 | bytes 122896 | tf_op jit(solution)/shard_map/convert_element_type | solution.py:474
  8.6 17.3 %all-to-all-start = ((f16[16,24,128]{2,1,0:T(8,128)(2,1)}), f16[16,24,128]{2,1,0:T(8,128)(2,1)S(1)}, u32[]{:S(2)}, u32[]{:S(2)}) async-start(f16[16,24,128]{2,1,0:T(8,128)(2,1)} %select_convert_fusion), calls=%async_computation | async-start | bytes 196608 | tf_op jit(solution)/shard_map/all_to_all | solution.py:447
  25.9 0.0 copy-start
  25.9 4.0 %within.1 = (f32[1568,128]{1,0:T(8,128)S(1)}, bf16[4,128,128]{2,1,0:T(8,128)(2,1)S(1)}) custom-call(s32[1]{0:T(128)} %bitcast.me_ref, f32[2,8,16]{2,1,0:T(8,128)S(1)} %get-tuple-element.29.table_ref, f32[2,128,512]{2,1,0:T(8,128)S(1)} %get-tuple-element.30.pair_ref, f32[2,16,512]{2,1,0:T(8,128)S(1)} %get-tuple-element.31.states_ref, ...), custom_call_target="tpu_custom_call" | custom-call | flops 8000000000 | bytes 24000000 | tf_op jit(solution)/shard_map/within/pallas_call | solution.py:476
  29.9 0.0 copy-start.1
  29.9 0.0 all-to-all-done
  29.9 0.0 copy-done
  29.9 0.9 %copy-done.1 = bf16[512,128]{1,0:T(8,128)(2,1)S(1)} copy-done((bf16[512,128]{1,0:T(8,128)(2,1)S(1)}, bf16[512,128]{1,0:T(8,128)(2,1)}, u32[]{:S(2)}) %copy-start.1) | copy-done | bytes 131096
  30.8 1.0 %across.1 = (f32[3,512,128]{2,1,0:T(8,128)S(1)}, f32[24,128]{1,0:T(8,128)S(1)}) custom-call(s32[1]{0:T(128)} %bitcast.me_ref, f32[16,24,128]{2,1,0:T(8,128)S(1)} %convert_element_type.13.arrived_ref, f32[1568,128]{1,0:T(8,128)S(1)} %get-tuple-element.34.near_ref, bf16[4,128,128]{2,1,0:T(8,128)(2,1)S(1)} %get-tuple-element.35.halves_ref, ...), custom_call_target="tpu_custom_call" | custom-call | flops 4000000000 | bytes 12000000 | tf_op jit(solution)/shard_map/across/pallas_call | solution.py:482
  31.8 0.7 %broadcast_in_dim.22 = f16[16,24,128]{2,1,0:T(8,128)(2,1)} broadcast(f16[24,128]{1,0:T(8,128)(2,1)S(1)} %convert_element_type.14), dimensions={1,2} | broadcast | bytes 104448 | tf_op jit(solution)/shard_map/broadcast_in_dim | solution.py:491
  32.5 11.5 %all-to-all-start.1 = ((f16[16,24,128]{2,1,0:T(8,128)(2,1)}), f16[16,24,128]{2,1,0:T(8,128)(2,1)S(1)}, u32[]{:S(2)}, u32[]{:S(2)}) async-start(f16[16,24,128]{2,1,0:T(8,128)(2,1)} %broadcast_in_dim.22), calls=%async_computation.1 | async-start | bytes 196608 | tf_op jit(solution)/shard_map/all_to_all | solution.py:447
  44.0 1.3 %collective-permute-start.1 = (f32[3,8,128]{2,1,0:T(8,128)S(1)}, f32[3,8,128]{2,1,0:T(8,128)S(1)}, u32[]{:S(2)}, u32[]{:S(2)}) collective-permute-start(f32[3,8,128]{2,1,0:T(8,128)S(1)} %slice.15), channel_id=1, source_target_pairs={{32,0},{64,32},{96,64},{128,96},{160,128},{192,160},{224,192},{256... | collective-permute-start | bytes 36872 | tf_op jit(solution)/shard_map/ppermute | solution.py:488
  45.3 2.5 %all-to-all-done.1 = f16[16,24,128]{2,1,0:T(8,128)(2,1)S(1)} async-done(((f16[16,24,128]{2,1,0:T(8,128)(2,1)}), f16[16,24,128]{2,1,0:T(8,128)(2,1)S(1)}, u32[]{:S(2)}, u32[]{:S(2)}) %all-to-all-start.1) | async-done | bytes 98336 | tf_op jit(solution)/shard_map/all_to_all | solution.py:447
  47.8 0.6 total.1
  48.5 11.9 %all-to-all-start.2 = ((f32[32,1,128]{2,1,0:T(1,128)}), f32[32,1,128]{2,1,0:T(1,128)S(1)}, u32[]{:S(2)}, u32[]{:S(2)}) async-start(f32[32,1,128]{2,1,0:T(1,128)} %get-tuple-element.41), calls=%async_computation.2 | async-start | bytes 32768 | tf_op jit(solution)/shard_map/all_to_all | solution.py:447
  60.4 0.0 collective-permute-done.1.after_ref
  60.4 1.2 %inputs.1 = (bf16[3,512,128]{2,1,0:T(8,128)(2,1)}, f32[2,8,16]{2,1,0:T(8,128)S(1)}) custom-call(f32[3,512,128]{2,1,0:T(8,128)S(1)} %get-tuple-element.37.feature_ref, f32[3,8,128]{2,1,0:T(8,128)S(1)} %collective-permute-done.1.after_ref, f32[3,7,128]{2,1,0:T(8,128)S(1)} %copy-done.2, f32[24,128]{1,0:T(8,128)S(1)} %get-tuple-element.39.total_ref), custom_call_target="tpu_custom_call" | custom-call | flops 2000000000 | bytes 6000000 | tf_op jit(solution)/shard_map/inputs/pallas_call | solution.py:497
  61.6 2.5 %all-to-all-done.2.square_ref = f32[32,1,128]{2,1,0:T(1,128)S(1)} async-done(((f32[32,1,128]{2,1,0:T(1,128)}), f32[32,1,128]{2,1,0:T(1,128)S(1)}, u32[]{:S(2)}, u32[]{:S(2)}) %all-to-all-start.2) | async-done | bytes 16416 | tf_op jit(solution)/shard_map/all_to_all | solution.py:447
  64.1 0.7 %scale.1 = (f32[3,7,128]{2,1,0:T(8,128)}, f32[8,16]{1,0:T(8,128)}, f32[8,16]{1,0:T(8,128)}) custom-call(f32[32,1,128]{2,1,0:T(1,128)S(1)} %all-to-all-done.2.square_ref, f32[24,128]{1,0:T(8,128)S(1)} %get-tuple-element.39.total_ref, f32[2,8,16]{2,1,0:T(8,128)S(1)} %get-tuple-element.42.table_ref), custom_call_target="tpu_custom_call" | custom-call | flops 1000000000 | bytes 3000000 | tf_op jit(solution)/shard_map/scale/pallas_call | solution.py:502
  (6 shorter events, 0.1 us)
Async XLA Ops:
  0.6 5.3 %copy-start.2 = (f32[3,7,128]{2,1,0:T(8,128)S(1)}, f32[3,7,128]{2,1,0:T(8,128)}, u32[]{:S(2)}) copy-start(f32[3,7,128]{2,1,0:T(8,128)} %weight_ref.5) | copy-start | bytes 32260
  0.6 5.3 %copy-start.4 = (f32[8,16]{1,0:T(8,128)S(1)}, f32[8,16]{1,0:T(8,128)}, u32[]{:S(2)}) copy-start(f32[8,16]{1,0:T(8,128)} %residue_ref.1) | copy-start | bytes 1540
  1.4 4.5 %copy-start.3 = (f32[8,16]{1,0:T(8,128)S(1)}, f32[8,16]{1,0:T(8,128)}, u32[]{:S(2)}) copy-start(f32[8,16]{1,0:T(8,128)} %rate_ref.1) | copy-start | bytes 1540
  1.4 6.3 %collective-permute-start = (bf16[3,16,128]{2,1,0:T(8,128)(2,1)S(1)}, bf16[3,16,128]{2,1,0:T(8,128)(2,1)S(1)}, u32[]{:S(2)}, u32[]{:S(2)}) collective-permute-start(bf16[3,16,128]{2,1,0:T(8,128)(2,1)S(1)} %slice.12), channel_id=1, source_target_pairs={{0,32},{32,64},{64,96},{96,128},{128,160},{160,192},{192,224},{224... | collective-permute-start | bytes 36872 | tf_op jit(solution)/shard_map/ppermute | solution.py:454
  8.6 21.3 %all-to-all-start = ((f16[16,24,128]{2,1,0:T(8,128)(2,1)}), f16[16,24,128]{2,1,0:T(8,128)(2,1)S(1)}, u32[]{:S(2)}, u32[]{:S(2)}) async-start(f16[16,24,128]{2,1,0:T(8,128)(2,1)} %select_convert_fusion), calls=%async_computation | async-start | bytes 196608 | tf_op jit(solution)/shard_map/all_to_all | solution.py:447
  25.9 4.1 %copy-start = (bf16[3,512,128]{2,1,0:T(8,128)(2,1)S(1)}, bf16[3,512,128]{2,1,0:T(8,128)(2,1)}, u32[]{:S(2)}) copy-start(bf16[3,512,128]{2,1,0:T(8,128)(2,1)} %proj_ref.3) | copy-start | bytes 1179652
  29.9 0.9 %copy-start.1 = (bf16[512,128]{1,0:T(8,128)(2,1)S(1)}, bf16[512,128]{1,0:T(8,128)(2,1)}, u32[]{:S(2)}) copy-start(bf16[512,128]{1,0:T(8,128)(2,1)} %out_grad_ref.3) | copy-start | bytes 393220
  32.5 15.3 %all-to-all-start.1 = ((f16[16,24,128]{2,1,0:T(8,128)(2,1)}), f16[16,24,128]{2,1,0:T(8,128)(2,1)S(1)}, u32[]{:S(2)}, u32[]{:S(2)}) async-start(f16[16,24,128]{2,1,0:T(8,128)(2,1)} %broadcast_in_dim.22), calls=%async_computation.1 | async-start | bytes 196608 | tf_op jit(solution)/shard_map/all_to_all | solution.py:447
  44.0 16.4 %collective-permute-start.1 = (f32[3,8,128]{2,1,0:T(8,128)S(1)}, f32[3,8,128]{2,1,0:T(8,128)S(1)}, u32[]{:S(2)}, u32[]{:S(2)}) collective-permute-start(f32[3,8,128]{2,1,0:T(8,128)S(1)} %slice.15), channel_id=1, source_target_pairs={{32,0},{64,32},{96,64},{128,96},{160,128},{192,160},{224,192},{256... | collective-permute-start | bytes 36872 | tf_op jit(solution)/shard_map/ppermute | solution.py:488
  48.5 15.7 %all-to-all-start.2 = ((f32[32,1,128]{2,1,0:T(1,128)}), f32[32,1,128]{2,1,0:T(1,128)S(1)}, u32[]{:S(2)}, u32[]{:S(2)}) async-start(f32[32,1,128]{2,1,0:T(1,128)} %get-tuple-element.41), calls=%async_computation.2 | async-start | bytes 32768 | tf_op jit(solution)/shard_map/all_to_all | solution.py:447

commit v12 on v9

--- a/solution.py
+++ b/solution.py
@@ -93,7 +93,7 @@
 
 
 def member(position, count):
-    return (position + count // 2) % count
+    return (position + count // 2 + 1) % count
 
 
 def piece(at):
@@ -472,7 +472,7 @@
     )(before, conv_weight, head, powers, ends)
     later = member(lax.broadcasted_iota(jnp.int32, (ctx, 1, 1), 0), ctx) > me.reshape(1, 1, 1)
     send = jnp.where(later, send[1], send[0]).astype(F16)
-    arrived = exchange(send, "ctx", ctx // 2).astype(F32)
+    arrived = exchange(send, "ctx", ctx // 2 + 1).astype(F32)
     near, halves = call(
         middle_kernel, "within",
         (shape(2 * ROWS + (POWER + ctx) * MODES, CHANNELS), shape(4, CHUNK, CHANNELS, dtype=BF16)),

time: 63.9 us -> 63.6 us (level)
  waiting for transfers between devices: 3.27 us -> 3.99 us
  local copies, waits for them, and re-layouts: 2.28 us -> 1.57 us
    all_to_all x3, waiting for transfers between devices: 3.27 us -> 3.99 us  [exchange(): lax.all_to_all(blocks, axis, 0, 0, axis_index_groups=[[(first + p) % coun...]
    unnamed x10, local copies, waits for them, and re-layouts: 0.87 us -> 0.16 us
  transfers between devices with their start and end apart: 5 -> 5, of which waited for: 2 -> 3; matrix products, arithmetic and copies ran while one was open for 0% -> 0% of each run, Pallas kernels for 12% -> 12%
where the time goes in v12:
time: 63.6 us; the launch traced here: 63.2 us
  starting transfers between devices  46.6 us (73%)
  Pallas kernels  9.46 us (15%)
  waiting for transfers between devices  3.99 us (6%)
  local copies, waits for them, and re-layouts  1.57 us (2%)
  between operations  0.79 us (1%)
  other arithmetic  0.78 us (1%)
    all_to_all x3, starting transfers between devices, exchange(): lax.all_to_all(blocks, axis, 0, 0, axis_index_groups=[[(first + p) % coun...  40.8 us
    ppermute x1, starting transfers between devices, shards(): lax.ppermute(projected[:, ROWS - LEAD:, :], 'ctx', [(source, source + 1)...  4.49 us
    pallas_call x1, Pallas kernels, shards(): call(middle_kernel, 'within', (shape(2 * ROWS + (POWER + ctx) * MODES, CH...  3.99 us
    all_to_all x3, waiting for transfers between devices, exchange(): lax.all_to_all(blocks, axis, 0, 0, axis_index_groups=[[(first + p) % coun...  3.99 us
    pallas_call x1, Pallas kernels, shards(): call(prepare_kernel, 'prepare', (shape(2, ROWS, CHANNELS), shape(2, CHUNK...  1.79 us
    ppermute x1, starting transfers between devices, shards(): lax.ppermute(grad_feature[:, :8, :], 'ctx', [(source + 1, source) for sou...  1.29 us
  transfers between devices with their start and end apart: 5, of which 3 were waited for; matrix products, arithmetic and copies ran while one was open for 0% of the time, Pallas kernels for 12%

profile of v12, /device:TPU:1, one launch (start us, length us, event | category | flops | bytes accessed | tf_op | source)
XLA Modules:
  0.0 63.2 jit_solution(14166620979560115316)
XLA Ops:
  0.6 0.0 copy-start.2
  0.6 0.0 copy-start.4
  0.7 0.7 %slice.12 = bf16[3,16,128]{2,1,0:T(8,128)(2,1)S(1)} slice(bf16[3,512,128]{2,1,0:T(8,128)(2,1)} %proj_ref.3), slice={[0:3], [496:512], [0:128]} | slice | bytes 24576 | tf_op jit(solution)/shard_map/slice | solution.py:455
  1.4 0.0 copy-start.3
  1.4 4.5 %collective-permute-start = (bf16[3,16,128]{2,1,0:T(8,128)(2,1)S(1)}, bf16[3,16,128]{2,1,0:T(8,128)(2,1)S(1)}, u32[]{:S(2)}, u32[]{:S(2)}) collective-permute-start(bf16[3,16,128]{2,1,0:T(8,128)(2,1)S(1)} %slice.12), channel_id=1, source_target_pairs={{0,32},{32,64},{64,96},{96,128},{128,160},{160,192},{192,224},{224... | collective-permute-start | bytes 36872 | tf_op jit(solution)/shard_map/ppermute | solution.py:454
  5.9 0.0 copy-done.2
  5.9 0.0 copy-done.4
  5.9 0.0 copy-done.3
  5.9 1.8 %prepare.1 = (f32[2,512,128]{2,1,0:T(8,128)S(1)}, f32[2,128,512]{2,1,0:T(8,128)S(1)}, f32[2,16,512]{2,1,0:T(8,128)S(1)}, f32[2,16,128]{2,1,0:T(8,128)S(1)}, f32[...) custom-call(f32[3,7,128]{2,1,0:T(8,128)S(1)} %copy-done.2, f32[8,16]{1,0:T(8,128)S(1)} %copy-done.3, ...), custom_call_target="tpu_custom_call" | custom-call | flops 3000000000 | bytes 9000000 | tf_op jit(solution)/shard_map/prepare/pallas_call | solution.py:457
  7.7 0.0 collective-permute-done.before_ref
  7.7 0.1 patch.1
  7.8 0.7 %select_convert_fusion = f16[16,24,128]{2,1,0:T(8,128)(2,1)} fusion(f32[24,128]{1,0:T(8,128)S(1)} %get-tuple-element.47, f32[24,128]{1,0:T(8,128)S(1)} %get-tuple-element.46, pred[16]{0:T(512)(128)(4,1)S(1)} %fusion), kind=kLoop, calls=%fused_computation | loop fusion | flops 98304 | bytes 122896 | tf_op jit(solution)/shard_map/convert_element_type | solution.py:474
  8.6 16.4 %all-to-all-start = ((f16[16,24,128]{2,1,0:T(8,128)(2,1)}), f16[16,24,128]{2,1,0:T(8,128)(2,1)S(1)}, u32[]{:S(2)}, u32[]{:S(2)}) async-start(f16[16,24,128]{2,1,0:T(8,128)(2,1)} %select_convert_fusion), calls=%async_computation | async-start | bytes 196608 | tf_op jit(solution)/shard_map/all_to_all | solution.py:447
  25.0 0.0 copy-start
  25.0 4.0 %within.1 = (f32[1568,128]{1,0:T(8,128)S(1)}, bf16[4,128,128]{2,1,0:T(8,128)(2,1)S(1)}) custom-call(s32[1]{0:T(128)} %bitcast.me_ref, f32[2,8,16]{2,1,0:T(8,128)S(1)} %get-tuple-element.29.table_ref, f32[2,128,512]{2,1,0:T(8,128)S(1)} %get-tuple-element.30.pair_ref, f32[2,16,512]{2,1,0:T(8,128)S(1)} %get-tuple-element.31.states_ref, ...), custom_call_target="tpu_custom_call" | custom-call | flops 8000000000 | bytes 24000000 | tf_op jit(solution)/shard_map/within/pallas_call | solution.py:476
  29.0 0.0 copy-start.1
  29.0 0.7 %all-to-all-done = f16[16,24,128]{2,1,0:T(8,128)(2,1)S(1)} async-done(((f16[16,24,128]{2,1,0:T(8,128)(2,1)}), f16[16,24,128]{2,1,0:T(8,128)(2,1)S(1)}, u32[]{:S(2)}, u32[]{:S(2)}) %all-to-all-start) | async-done | bytes 98336 | tf_op jit(solution)/shard_map/all_to_all | solution.py:447
  29.7 0.0 copy-done
  29.7 0.1 copy-done.1
  29.9 1.0 %across.1 = (f32[3,512,128]{2,1,0:T(8,128)S(1)}, f32[24,128]{1,0:T(8,128)S(1)}) custom-call(s32[1]{0:T(128)} %bitcast.me_ref, f32[16,24,128]{2,1,0:T(8,128)S(1)} %convert_element_type.13.arrived_ref, f32[1568,128]{1,0:T(8,128)S(1)} %get-tuple-element.34.near_ref, bf16[4,128,128]{2,1,0:T(8,128)(2,1)S(1)} %get-tuple-element.35.halves_ref, ...), custom_call_target="tpu_custom_call" | custom-call | flops 4000000000 | bytes 12000000 | tf_op jit(solution)/shard_map/across/pallas_call | solution.py:482
  30.9 0.7 %broadcast_in_dim.22 = f16[16,24,128]{2,1,0:T(8,128)(2,1)} broadcast(f16[24,128]{1,0:T(8,128)(2,1)S(1)} %convert_element_type.14), dimensions={1,2} | broadcast | bytes 104448 | tf_op jit(solution)/shard_map/broadcast_in_dim | solution.py:491
  31.6 11.5 %all-to-all-start.1 = ((f16[16,24,128]{2,1,0:T(8,128)(2,1)}), f16[16,24,128]{2,1,0:T(8,128)(2,1)S(1)}, u32[]{:S(2)}, u32[]{:S(2)}) async-start(f16[16,24,128]{2,1,0:T(8,128)(2,1)} %broadcast_in_dim.22), calls=%async_computation.1 | async-start | bytes 196608 | tf_op jit(solution)/shard_map/all_to_all | solution.py:447
  43.1 1.3 %collective-permute-start.1 = (f32[3,8,128]{2,1,0:T(8,128)S(1)}, f32[3,8,128]{2,1,0:T(8,128)S(1)}, u32[]{:S(2)}, u32[]{:S(2)}) collective-permute-start(f32[3,8,128]{2,1,0:T(8,128)S(1)} %slice.15), channel_id=1, source_target_pairs={{32,0},{64,32},{96,64},{128,96},{160,128},{192,160},{224,192},{256... | collective-permute-start | bytes 36872 | tf_op jit(solution)/shard_map/ppermute | solution.py:488
  44.4 2.5 %all-to-all-done.1 = f16[16,24,128]{2,1,0:T(8,128)(2,1)S(1)} async-done(((f16[16,24,128]{2,1,0:T(8,128)(2,1)}), f16[16,24,128]{2,1,0:T(8,128)(2,1)S(1)}, u32[]{:S(2)}, u32[]{:S(2)}) %all-to-all-start.1) | async-done | bytes 98336 | tf_op jit(solution)/shard_map/all_to_all | solution.py:447
  46.9 0.6 %total.1 = (f32[24,128]{1,0:T(8,128)S(1)}, f32[32,1,128]{2,1,0:T(1,128)}) custom-call(f32[16,24,128]{2,1,0:T(8,128)S(1)} %convert_element_type.15.stats_ref), custom_call_target="tpu_custom_call" | custom-call | flops 1000000000 | bytes 3000000 | tf_op jit(solution)/shard_map/total/pallas_call | solution.py:493
  47.6 12.9 %all-to-all-start.2 = ((f32[32,1,128]{2,1,0:T(1,128)}), f32[32,1,128]{2,1,0:T(1,128)S(1)}, u32[]{:S(2)}, u32[]{:S(2)}) async-start(f32[32,1,128]{2,1,0:T(1,128)} %get-tuple-element.41), calls=%async_computation.2 | async-start | bytes 32768 | tf_op jit(solution)/shard_map/all_to_all | solution.py:447
  60.5 0.0 collective-permute-done.1.after_ref
  60.5 1.2 %inputs.1 = (bf16[3,512,128]{2,1,0:T(8,128)(2,1)}, f32[2,8,16]{2,1,0:T(8,128)S(1)}) custom-call(f32[3,512,128]{2,1,0:T(8,128)S(1)} %get-tuple-element.37.feature_ref, f32[3,8,128]{2,1,0:T(8,128)S(1)} %collective-permute-done.1.after_ref, f32[3,7,128]{2,1,0:T(8,128)S(1)} %copy-done.2, f32[24,128]{1,0:T(8,128)S(1)} %get-tuple-element.39.total_ref), custom_call_target="tpu_custom_call" | custom-call | flops 2000000000 | bytes 6000000 | tf_op jit(solution)/shard_map/inputs/pallas_call | solution.py:497
  61.7 0.7 %all-to-all-done.2.square_ref = f32[32,1,128]{2,1,0:T(1,128)S(1)} async-done(((f32[32,1,128]{2,1,0:T(1,128)}), f32[32,1,128]{2,1,0:T(1,128)S(1)}, u32[]{:S(2)}, u32[]{:S(2)}) %all-to-all-start.2) | async-done | bytes 16416 | tf_op jit(solution)/shard_map/all_to_all | solution.py:447
  62.5 0.7 %scale.1 = (f32[3,7,128]{2,1,0:T(8,128)}, f32[8,16]{1,0:T(8,128)}, f32[8,16]{1,0:T(8,128)}) custom-call(f32[32,1,128]{2,1,0:T(1,128)S(1)} %all-to-all-done.2.square_ref, f32[24,128]{1,0:T(8,128)S(1)} %get-tuple-element.39.total_ref, f32[2,8,16]{2,1,0:T(8,128)S(1)} %get-tuple-element.42.table_ref), custom_call_target="tpu_custom_call" | custom-call | flops 1000000000 | bytes 3000000 | tf_op jit(solution)/shard_map/scale/pallas_call | solution.py:502
  (6 shorter events, 0.1 us)
Async XLA Ops:
  0.6 5.3 %copy-start.2 = (f32[3,7,128]{2,1,0:T(8,128)S(1)}, f32[3,7,128]{2,1,0:T(8,128)}, u32[]{:S(2)}) copy-start(f32[3,7,128]{2,1,0:T(8,128)} %weight_ref.5) | copy-start | bytes 32260
  0.6 5.3 %copy-start.4 = (f32[8,16]{1,0:T(8,128)S(1)}, f32[8,16]{1,0:T(8,128)}, u32[]{:S(2)}) copy-start(f32[8,16]{1,0:T(8,128)} %residue_ref.1) | copy-start | bytes 1540
  1.4 4.5 %copy-start.3 = (f32[8,16]{1,0:T(8,128)S(1)}, f32[8,16]{1,0:T(8,128)}, u32[]{:S(2)}) copy-start(f32[8,16]{1,0:T(8,128)} %rate_ref.1) | copy-start | bytes 1540
  1.4 6.3 %collective-permute-start = (bf16[3,16,128]{2,1,0:T(8,128)(2,1)S(1)}, bf16[3,16,128]{2,1,0:T(8,128)(2,1)S(1)}, u32[]{:S(2)}, u32[]{:S(2)}) collective-permute-start(bf16[3,16,128]{2,1,0:T(8,128)(2,1)S(1)} %slice.12), channel_id=1, source_target_pairs={{0,32},{32,64},{64,96},{96,128},{128,160},{160,192},{192,224},{224... | collective-permute-start | bytes 36872 | tf_op jit(solution)/shard_map/ppermute | solution.py:454
  8.6 21.2 %all-to-all-start = ((f16[16,24,128]{2,1,0:T(8,128)(2,1)}), f16[16,24,128]{2,1,0:T(8,128)(2,1)S(1)}, u32[]{:S(2)}, u32[]{:S(2)}) async-start(f16[16,24,128]{2,1,0:T(8,128)(2,1)} %select_convert_fusion), calls=%async_computation | async-start | bytes 196608 | tf_op jit(solution)/shard_map/all_to_all | solution.py:447
  25.0 4.8 %copy-start = (bf16[3,512,128]{2,1,0:T(8,128)(2,1)S(1)}, bf16[3,512,128]{2,1,0:T(8,128)(2,1)}, u32[]{:S(2)}) copy-start(bf16[3,512,128]{2,1,0:T(8,128)(2,1)} %proj_ref.3) | copy-start | bytes 1179652
  29.0 0.9 %copy-start.1 = (bf16[512,128]{1,0:T(8,128)(2,1)S(1)}, bf16[512,128]{1,0:T(8,128)(2,1)}, u32[]{:S(2)}) copy-start(bf16[512,128]{1,0:T(8,128)(2,1)} %out_grad_ref.3) | copy-start | bytes 393220
  31.6 15.3 %all-to-all-start.1 = ((f16[16,24,128]{2,1,0:T(8,128)(2,1)}), f16[16,24,128]{2,1,0:T(8,128)(2,1)S(1)}, u32[]{:S(2)}, u32[]{:S(2)}) async-start(f16[16,24,128]{2,1,0:T(8,128)(2,1)} %broadcast_in_dim.22), calls=%async_computation.1 | async-start | bytes 196608 | tf_op jit(solution)/shard_map/all_to_all | solution.py:447
  43.1 17.4 %collective-permute-start.1 = (f32[3,8,128]{2,1,0:T(8,128)S(1)}, f32[3,8,128]{2,1,0:T(8,128)S(1)}, u32[]{:S(2)}, u32[]{:S(2)}) collective-permute-start(f32[3,8,128]{2,1,0:T(8,128)S(1)} %slice.15), channel_id=1, source_target_pairs={{32,0},{64,32},{96,64},{128,96},{160,128},{192,160},{224,192},{256... | collective-permute-start | bytes 36872 | tf_op jit(solution)/shard_map/ppermute | solution.py:488
  47.6 14.9 %all-to-all-start.2 = ((f32[32,1,128]{2,1,0:T(1,128)}), f32[32,1,128]{2,1,0:T(1,128)S(1)}, u32[]{:S(2)}, u32[]{:S(2)}) async-start(f32[32,1,128]{2,1,0:T(1,128)} %get-tuple-element.41), calls=%async_computation.2 | async-start | bytes 32768 | tf_op jit(solution)/shard_map/all_to_all | solution.py:447
